TPU v7x, 32 devices: a whole 2x2x4 slice. The times are simulated.
32 devices in a mesh: rep: 2 (over y), seq: 4 (over z), sub: 4 (over x, core).
Axes of the slice: x: 2, y: 2, z: 4, core: 2. Of those that a mesh axis runs over, the one named last changes fastest.
Arguments:
- queries: bfloat16 [4096, 768], P(('rep', 'seq', 'sub')), parts along dimension 0, may hold values from -96 to 96
- keys: bfloat16 [4096, 768], P(('rep', 'seq', 'sub')), parts along dimension 0, may hold values from -7.2 to 7.2
- values: bfloat16 [4096, 768], P(('rep', 'seq', 'sub')), parts along dimension 0, may hold values from -24 to 24
- offsets: int32 [12], replicated, may hold values from 0 to 3
Outputs:
- attended: bfloat16 [4096, 768], P(('rep', 'seq', 'sub')), parts along dimension 0
There are 2 independent parts, one for each index of `rep`. A program takes and returns all parts, laid end to end along the dimension named above; an argument that names none is the same for every part. Nothing has to cross between parts.
All inputs are finite; a program needn't handle non-finite values.
Results may differ from a plain program's by a relative error of at most 0.0041.
Values may be sent and summed in bfloat16 or wider, within the bound.
No kernel may reach another device: no remote copies, remote signals or barrier semaphores. Data moves between devices by JAX's collectives and lax.ppermute only.
A program may use at most 64 MiB of HBM per device.

v0:
```python
import jax
import jax.numpy as jnp
from jax import lax
from jax.sharding import PartitionSpec as P

ATTENTION_HEADS = 12
HEAD_DIMENSION = 64


def make_accumulate(query_heads, heads, head_size):
    factor_scale = head_size ** (-0.5)

    def accumulate(carry, piece, start):
        run_max, run_sum, run_out = carry
        key_piece, value_piece = piece
        key_rows = key_piece.shape[0]
        key_heads = key_piece.reshape(key_rows, heads, head_size)
        value_heads = value_piece.reshape(key_rows, heads, head_size)
        maxima = []
        totals = []
        outputs = []
        for lead_head in range(0, heads, 2):
            chosen = slice(lead_head, lead_head + 2)
            scores = (
                jnp.einsum(
                    "thd,shd->hts",
                    query_heads[:, chosen],
                    key_heads[:, chosen],
                    preferred_element_type=jnp.float32,
                )
                * factor_scale
            )
            prior_max = run_max[chosen]
            newer_max = scores.max(-1)
            rescale = jnp.exp(prior_max - newer_max)
            weights = jnp.exp(scores - newer_max[..., None])
            totals.append(run_sum[chosen] * rescale + weights.sum(-1))
            update = jnp.einsum(
                "hts,shd->htd",
                weights.astype(jnp.bfloat16),
                value_heads[:, chosen],
                preferred_element_type=jnp.float32,
            )
            outputs.append(run_out[chosen] * rescale[..., None] + update)
            maxima.append(newer_max)
        return (jnp.concatenate(maxima, 0), jnp.concatenate(totals, 0), jnp.concatenate(outputs, 0))

    return accumulate


def start_carry(heads, query_rows, head_size):
    return (
        jnp.full((heads, query_rows), -jnp.inf, jnp.float32),
        jnp.zeros((heads, query_rows), jnp.float32),
        jnp.zeros((heads, query_rows, head_size), jnp.float32),
    )


def merge_level_outputs(
    level_zero_max,
    level_zero_sum,
    level_zero_output,
    level_one_max,
    level_one_sum,
    level_one_output,
    offsets,
    dilation,
):
    heads, tok_rows = level_zero_max.shape
    residue = jnp.arange(tok_rows, dtype=jnp.int32) % dilation
    member = residue[None, :] == offsets[:, None]
    wide_max = jnp.repeat(level_one_max, dilation, axis=1)
    wide_sum = jnp.repeat(level_one_sum, dilation, axis=1)
    wide_out = jnp.repeat(level_one_output, dilation, axis=1)
    top_both = jnp.where(member, jnp.maximum(level_zero_max, wide_max), level_zero_max)
    keep_zero = jnp.exp(level_zero_max - top_both)
    keep_one = jnp.where(member, jnp.exp(jnp.where(member, wide_max - top_both, 0.0)), 0.0)
    total = level_zero_sum * keep_zero + wide_sum * keep_one
    merged_output = (
        level_zero_output * keep_zero[..., None] + wide_out * keep_one[..., None]
    ) / total[..., None]
    return merged_output.transpose(1, 0, 2).reshape(tok_rows, heads * merged_output.shape[2])


def per_device(queries, keys, values, offsets):
    tok_rows = queries.shape[0]
    heads = ATTENTION_HEADS
    head_size = HEAD_DIMENSION
    dilation = lax.axis_size("seq")
    kept_rows = tok_rows // dilation
    selector_fn = (jnp.arange(dilation, dtype=jnp.int32)[:, None] == offsets[None, :]).astype(
        jnp.bfloat16
    )

    def dilated(source_tensor):
        reshaped_input = source_tensor.reshape(kept_rows, dilation, heads, head_size)
        picked = jnp.einsum(
            "rjhd,jh->rhd", reshaped_input, selector_fn, preferred_element_type=jnp.float32
        )
        return picked.astype(jnp.bfloat16)

    sparse_queries = dilated(queries)
    sparse_keys = dilated(keys).reshape(kept_rows, heads * head_size)
    sparse_values = dilated(values).reshape(kept_rows, heads * head_size)
    accumulate_sparse = make_accumulate(sparse_queries, heads, head_size)
    sparse_init = start_carry(heads, kept_rows, head_size)
    level_one_max, level_one_sum, level_one_output = accumulate_sparse(
        sparse_init,
        (
            lax.all_gather(sparse_keys, ("seq", "sub"), axis=0, tiled=True),
            lax.all_gather(sparse_values, ("seq", "sub"), axis=0, tiled=True),
        ),
        jnp.int32(0),
    )
    query_heads = queries.reshape(tok_rows, heads, head_size)
    accumulate_dense = make_accumulate(query_heads, heads, head_size)
    dense_init = start_carry(heads, tok_rows, head_size)
    level_zero_max, level_zero_sum, level_zero_output = accumulate_dense(
        dense_init,
        (
            lax.all_gather(keys, "sub", axis=0, tiled=True),
            lax.all_gather(values, "sub", axis=0, tiled=True),
        ),
        jnp.int32(0),
    )
    merged_output = merge_level_outputs(
        level_zero_max,
        level_zero_sum,
        level_zero_output,
        level_one_max,
        level_one_sum,
        level_one_output,
        offsets,
        dilation,
    )
    return merged_output.astype(jnp.bfloat16)


def solution(mesh):
    placed = (
        P(("rep", "seq", "sub"), None),
        P(("rep", "seq", "sub"), None),
        P(("rep", "seq", "sub"), None),
        P(),
    )
    return jax.shard_map(
        per_device,
        mesh=mesh,
        in_specs=placed,
        out_specs=P(("rep", "seq", "sub"), None),
        check_vma=False,
    )
```

profile of v0, /device:TPU:0, one launch (start us, length us, event | category | flops | bytes accessed | tf_op | source)
XLA Modules:
  0.0 82.1 jit_solution(842361426913333867)
XLA Ops:
  0.0 0.7 fusion.102
  0.8 1.3 %reshape.485 = bf16[32,4,12,64]{3,2,1,0:T(8,128)(2,1)S(1)} reshape(bf16[128,768]{1,0:T(8,128)(2,1)} %param.6) | data formatting | bytes 393216 | tf_op jit(solution)/shard_map/reshape | solution.py:96
  2.1 0.4 fusion.24
  2.7 25.4 %all_gather.15 = bf16[512,768]{1,0:T(8,128)(2,1)S(1)} all-gather(bf16[32,768]{1,0:T(8,128)(2,1)S(1)} %reshape.486), channel_id=1, replica_groups=mesh['rep'=2,'seq'=4,'sub'=4] {'seq','sub'}, dimensions={0}, use_global_device_ids=true | all-gather | bytes 835584 | tf_op jit(solution)/shard_map/all_gather | solution.py:111
  28.1 0.3 copy.70
  28.4 0.6 copy-done.1
  29.0 0.3 reshape.481
  29.4 0.4 fusion.26
  30.0 19.6 %all_gather.14 = bf16[512,768]{1,0:T(8,128)(2,1)S(1)} all-gather(bf16[32,768]{1,0:T(8,128)(2,1)S(1)} %reshape.482), channel_id=1, replica_groups=mesh['rep'=2,'seq'=4,'sub'=4] {'seq','sub'}, dimensions={0}, use_global_device_ids=true | all-gather | bytes 835584 | tf_op jit(solution)/shard_map/all_gather | solution.py:110
  49.6 0.3 copy.67
  49.9 0.6 copy-done
  50.5 0.3 reshape.480
  50.9 0.4 fusion.28
  55.7 8.9 %all_gather.12 = bf16[512,768]{1,0:T(8,128)(2,1)S(1)} all-gather(bf16[128,768]{1,0:T(8,128)(2,1)S(1)} %copy-done.1), channel_id=1, replica_groups=mesh['rep'=2,'seq'=4,'sub'=4] {'sub'}, dimensions={0}, use_global_device_ids=true | all-gather | bytes 983040 | tf_op jit(solution)/shard_map/all_gather | solution.py:121
  64.7 0.3 copy.65
  65.0 0.3 fusion.122
  65.3 0.6 copy-done.2
  65.9 8.7 %all_gather.13 = bf16[512,768]{1,0:T(8,128)(2,1)S(1)} all-gather(bf16[128,768]{1,0:T(8,128)(2,1)S(1)} %copy-done.2), channel_id=1, replica_groups=mesh['rep'=2,'seq'=4,'sub'=4] {'sub'}, dimensions={0}, use_global_device_ids=true | all-gather | bytes 983040 | tf_op jit(solution)/shard_map/all_gather | solution.py:122
  74.6 0.3 copy.66
  75.1 0.4 fusion.123
  75.7 0.3 fusion.5
  76.0 0.3 fusion.4
  76.3 0.3 fusion.124
  76.9 0.4 fusion.125
  77.5 0.3 fusion.3
  77.8 0.3 fusion.2
  78.1 0.3 fusion.126
  78.7 0.4 fusion.127
  79.3 0.3 fusion.1
  79.6 0.3 fusion
  80.4 0.7 copy-done.3
  81.2 0.8 %copy.75 = bf16[128,768]{1,0:T(8,128)(2,1)} copy(bf16[128,768]{0,1:T(8,128)(2,1)S(1)} %bitcast.96) | data formatting | bytes 393216 | tf_op jit(solution)/shard_map/convert_element_type | solution.py:136
  (56 shorter events, 7.2 us)
Async XLA Ops:
  28.1 0.9 %copy-start.1 = (bf16[128,768]{1,0:T(8,128)(2,1)S(1)}, bf16[128,768]{1,0:T(8,128)(2,1)}, u32[]{:S(2)}) copy-start(bf16[128,768]{1,0:T(8,128)(2,1)} %param.5) | copy-start | bytes 589828
  49.6 0.9 %copy-start = (bf16[128,768]{1,0:T(8,128)(2,1)S(1)}, bf16[128,768]{1,0:T(8,128)(2,1)}, u32[]{:S(2)}) copy-start(bf16[128,768]{1,0:T(8,128)(2,1)} %param.4) | copy-start | bytes 589828
  65.0 0.9 %copy-start.2 = (bf16[128,768]{1,0:T(8,128)(2,1)S(1)}, bf16[128,768]{1,0:T(8,128)(2,1)}, u32[]{:S(2)}) copy-start(bf16[128,768]{1,0:T(8,128)(2,1)} %param.6) | copy-start | bytes 589828
  80.4 0.7 copy-start.3
where the time goes:
time: 82.3 us; the launch traced here: 82.1 us
  blocking collectives  62.7 us (76%)
  local copies, waits for them, and re-layouts  8.07 us (10%)
  matrix products  7.68 us (9%)
  other arithmetic  3.36 us (4%)
    all_gather x1, blocking collectives, per_device(): lax.all_gather(sparse_values, ('seq', 'sub'), axis=0, tiled=True)  25.4 us
    all_gather x1, blocking collectives, per_device(): lax.all_gather(sparse_keys, ('seq', 'sub'), axis=0, tiled=True)  19.6 us
    all_gather x1, blocking collectives, per_device(): lax.all_gather(keys, 'sub', axis=0, tiled=True)  8.95 us
    all_gather x1, blocking collectives, per_device(): lax.all_gather(values, 'sub', axis=0, tiled=True)  8.71 us
    dot_general x12, matrix products, accumulate(): jnp.einsum('thd,shd->hts', query_heads[:, chosen], key_heads[:, chosen],...  3.54 us
    dot_general x12, matrix products, accumulate(): jnp.einsum('hts,shd->htd', weights.astype(jnp.bfloat16), value_heads[:, c...  3.07 us
    unnamed x9, local copies, waits for them, and re-layouts  2.69 us
    reduce_sum x12, other arithmetic, accumulate(): totals.append(run_sum[chosen] * rescale + weights.sum(-1))  2.45 us

commit v1 on v0

v1 whole, which is shorter than its diff:
```python
import functools

import jax
import jax.numpy as jnp
from jax import lax
from jax.experimental import pallas as pl
from jax.experimental.pallas import tpu as pltpu
from jax.sharding import PartitionSpec as P

ATTENTION_HEADS = 12
HEAD_DIMENSION = 64
PAIR = 2 * HEAD_DIMENSION
LOWEST = -1e30


def round_up(count, step):
    return -(-count // step) * step


class Sizes:
    def __init__(self, rows, dilation, sub):
        self.rows, self.dilation, self.sub = rows, dilation, sub
        self.kept = rows // dilation
        self.rest = rows - self.kept
        self.kept_pad = round_up(self.kept, 16)
        self.rest_pad = round_up(self.rest, 16)
        self.all_pad = self.kept_pad + self.rest_pad
        self.shift = dilation.bit_length() - 1
        self.kept_keys = sub * self.kept_pad
        self.keys = sub * self.all_pad
        self.padded = self.kept_pad != self.kept or self.rest_pad != self.rest


def target_rows(sizes, position, offset):
    residue = jnp.bitwise_and(position, sizes.dilation - 1)
    group = jnp.right_shift(position, sizes.shift)
    slab = jnp.bitwise_and(residue - offset + sizes.dilation, sizes.dilation - 1)
    return jnp.where(slab == 0, group, sizes.kept_pad + (slab - 1) * sizes.kept + group)


def order_rows(sizes, offset):
    shape = (sizes.all_pad, sizes.rows)
    place = lax.broadcasted_iota(jnp.int32, shape, 0)
    target = target_rows(sizes, lax.broadcasted_iota(jnp.int32, (1, sizes.rows), 1), offset)
    return jnp.where(place == target, 1.0, 0.0).astype(jnp.bfloat16)


def restore_rows(sizes, offset):
    shape = (sizes.rows, sizes.all_pad)
    place = lax.broadcasted_iota(jnp.int32, shape, 1)
    target = target_rows(sizes, lax.broadcasted_iota(jnp.int32, shape, 0), offset)
    return jnp.where(place == target, 1.0, 0.0).astype(jnp.bfloat16)


def first_head(shape):
    return lax.broadcasted_iota(jnp.int32, shape, 1) < HEAD_DIMENSION


def dot(a, b):
    return jnp.dot(a, b, preferred_element_type=jnp.float32)


def dot_rows(a, b):
    return lax.dot_general(a, b, (((1,), (1,)), ((), ())), preferred_element_type=jnp.float32)


def order_kernel(sizes, off_ref, q_ref, k_ref, v_ref, qs_ref, qd_ref, kvd_ref, kr_ref, vr_ref):
    width = q_ref.shape[1]
    kept = sizes.kept_pad
    scale = HEAD_DIMENSION ** (-0.5)
    for pair in range(width // PAIR):
        cols = slice(pair * PAIR, (pair + 1) * PAIR)
        chosen = jnp.concatenate(
            [order_rows(sizes, off_ref[2 * pair]), order_rows(sizes, off_ref[2 * pair + 1])], 0
        )
        joined = jnp.concatenate([q_ref[:, cols], k_ref[:, cols], v_ref[:, cols]], 1)
        both = dot(chosen, joined)
        lead, follow = both[: sizes.all_pad], both[sizes.all_pad :]
        mask = first_head((sizes.all_pad, PAIR))
        q = jnp.where(mask, lead[:, :PAIR], follow[:, :PAIR]) * scale
        k = jnp.where(mask, lead[:, PAIR : 2 * PAIR], follow[:, PAIR : 2 * PAIR])
        v = jnp.where(mask, lead[:, 2 * PAIR :], follow[:, 2 * PAIR :])
        q, k, v = (x.astype(jnp.bfloat16) for x in (q, k, v))
        qs_ref[:, cols] = q
        qd_ref[:, cols] = q[:kept]
        kvd_ref[:, cols] = k[:kept]
        kvd_ref[:, width + pair * PAIR : width + (pair + 1) * PAIR] = v[:kept]
        kr_ref[:, cols] = k[kept:]
        vr_ref[:, cols] = v[kept:]


def both_heads(q):
    mask = first_head(q.shape)
    zero = jnp.zeros_like(q)
    return jnp.concatenate([jnp.where(mask, q, zero), jnp.where(mask, zero, q)], 0)


def with_ones(v):
    return jnp.concatenate([v, jnp.ones_like(v)], 1)


def hide(col, step, used):
    return jnp.where(lax.rem(col + step, step) < used, 0.0, LOWEST)


def weigh(scores, top, v):
    weights = jnp.exp(scores - top).astype(jnp.bfloat16)
    return dot(weights, with_ones(v))


def partial_kernel(sizes, others, *refs):
    q_refs, kv_refs, out_refs = refs[:others], refs[others : others + sizes.sub], refs[others + sizes.sub :]
    width = q_refs[0].shape[1]
    kept = sizes.kept_pad
    rows = others * kept
    lane = lax.broadcasted_iota(jnp.int32, (rows, PAIR), 1)
    stats = jnp.zeros((rows, PAIR), jnp.float32)
    for pair in range(width // PAIR):
        cols = slice(pair * PAIR, (pair + 1) * PAIR)
        vcols = slice(width + pair * PAIR, width + (pair + 1) * PAIR)
        q = jnp.concatenate([r[:, cols] for r in q_refs], 0)
        k = jnp.concatenate([r[:, cols] for r in kv_refs], 0)
        v = jnp.concatenate([r[:, vcols] for r in kv_refs], 0)
        scores = dot_rows(both_heads(q), k)
        if sizes.padded:
            scores += hide(lax.broadcasted_iota(jnp.int32, (1, sizes.kept_keys), 1), kept, sizes.kept)
        top = jnp.max(scores, 1, keepdims=True).astype(jnp.bfloat16).astype(jnp.float32)
        both = weigh(scores, top, v)
        lead, follow = both[:rows], both[rows:]
        out = jnp.where(first_head((rows, PAIR)), lead[:, :PAIR], follow[:, :PAIR]).astype(jnp.bfloat16)
        for n, r in enumerate(out_refs):
            r[:, cols] = out[n * kept : (n + 1) * kept]
        for n, part in enumerate((lead, follow)):
            head = 3 * (2 * pair + n)
            total = part[:, PAIR:]
            coarse = total.astype(jnp.bfloat16).astype(jnp.float32)
            stats = jnp.where(lane == head, top[n * rows : (n + 1) * rows], stats)
            stats = jnp.where(lane == head + 1, coarse, stats)
            stats = jnp.where(lane == head + 2, total - coarse, stats)
    stats = stats.astype(jnp.bfloat16)
    for n, r in enumerate(out_refs):
        r[:, width:] = stats[n * kept : (n + 1) * kept]


def final_kernel(sizes, others, *refs):
    off_ref, q_ref = refs[:2]
    kv_refs, kr_refs, vr_refs = (refs[2 + n * sizes.sub : 2 + (n + 1) * sizes.sub] for n in range(3))
    part_refs = refs[2 + 3 * sizes.sub : 2 + 3 * sizes.sub + others]
    out_ref = refs[-1]
    width = q_ref.shape[1]
    kept, rows = sizes.kept_pad, sizes.all_pad
    stats = [r[:, width:].astype(jnp.float32) for r in part_refs]
    for pair in range(width // PAIR):
        cols = slice(pair * PAIR, (pair + 1) * PAIR)
        vcols = slice(width + pair * PAIR, width + (pair + 1) * PAIR)
        k = jnp.concatenate([r[:, cols] for r in kv_refs] + [r[:, cols] for r in kr_refs], 0)
        v = jnp.concatenate([r[:, vcols] for r in kv_refs] + [r[:, cols] for r in vr_refs], 0)
        scores = dot_rows(both_heads(q_ref[:, cols]), k)
        if sizes.padded:
            col = lax.broadcasted_iota(jnp.int32, (1, sizes.keys), 1)
            here = hide(col, kept, sizes.kept)
            there = hide(col - sizes.kept_keys, sizes.rest_pad, sizes.rest)
            scores += jnp.where(col < sizes.kept_keys, here, there)
        top = jnp.max(scores, 1, keepdims=True)
        weights = jnp.exp(scores - top)
        twice = [weights[n * rows : n * rows + kept, : sizes.kept_keys] for n in range(2)]
        rest = [weights[n * rows : n * rows + kept, sizes.kept_keys :] for n in range(2)]
        weights = jnp.concatenate(
            [
                jnp.concatenate([twice[0] * 2.0, rest[0]], 1),
                weights[kept:rows],
                jnp.concatenate([twice[1] * 2.0, rest[1]], 1),
                weights[rows + kept :],
            ],
            0,
        )
        both = dot(weights.astype(jnp.bfloat16), with_ones(v))
        done = []
        for n in range(2):
            part = both[n * rows : (n + 1) * rows]
            out, total = part[:, :PAIR], part[:, PAIR:]
            head = 3 * (2 * pair + n)
            own_top = top[n * rows : n * rows + kept]
            tops = [s[:, head : head + 1] for s in stats]
            best = functools.reduce(jnp.maximum, tops, own_top)
            factor = jnp.exp(own_top - best)
            kept_out, kept_total = out[:kept] * factor, total[:kept] * factor
            for s, t, r in zip(stats, tops, part_refs):
                factor = jnp.exp(t - best)
                kept_out += r[:, cols].astype(jnp.float32) * factor
                kept_total += (s[:, head + 1 : head + 2] + s[:, head + 2 : head + 3]) * factor
            done.append(
                jnp.concatenate([kept_out / kept_total, out[kept:] / total[kept:]], 0)
            )
        result = jnp.where(first_head((rows, PAIR)), done[0], done[1]).astype(jnp.bfloat16)
        back = jnp.concatenate(
            [restore_rows(sizes, off_ref[2 * pair]), restore_rows(sizes, off_ref[2 * pair + 1])], 0
        )
        back = dot(back, result)
        out_ref[:, cols] = jnp.where(
            first_head((sizes.rows, PAIR)), back[: sizes.rows], back[sizes.rows :]
        ).astype(jnp.bfloat16)


def call(kernel, out_shape, operands, flops):
    vmem = pl.BlockSpec(memory_space=pltpu.VMEM)
    smem = pl.BlockSpec(memory_space=pltpu.SMEM)
    in_specs = [smem if x.dtype == jnp.int32 else vmem for x in operands]
    out_specs = jax.tree.map(lambda _: vmem, out_shape)
    size = sum(x.size * 2 for x in operands)
    return pl.pallas_call(
        kernel,
        out_shape=out_shape,
        in_specs=in_specs,
        out_specs=out_specs,
        cost_estimate=pl.CostEstimate(flops=flops, bytes_accessed=size, transcendentals=0),
        compiler_params=pltpu.CompilerParams(vmem_limit_bytes=32 * 1024 * 1024),
    )(*operands)


def per_device(queries, keys, values, offsets):
    rows, width = queries.shape
    seq, sub = lax.axis_size("seq"), lax.axis_size("sub")
    sizes = Sizes(rows, seq, sub)

    def array(count, columns=width):
        return jax.ShapeDtypeStruct((count, columns), jnp.bfloat16)

    def swap(x, axis, mask):
        return lax.ppermute(x, axis, [(n, n ^ mask) for n in range(lax.axis_size(axis))])

    q, q_kept, kv_kept, k_rest, v_rest = call(
        functools.partial(order_kernel, sizes),
        (
            array(sizes.all_pad),
            array(sizes.kept_pad),
            array(sizes.kept_pad, 2 * width),
            array(sizes.rest_pad),
            array(sizes.rest_pad),
        ),
        (offsets, queries, keys, values),
        2 * 10**7,
    )

    def gather(x):
        mine = [x] + [swap(x, "sub", mask) for mask in range(2, sub, 2)]
        return mine + [swap(y, "sub", 1) for y in mine]

    kv_kept, k_rest, v_rest = gather(kv_kept), gather(k_rest), gather(v_rest)
    masks = range(1, seq)
    visitors = [swap(q_kept, "seq", mask) for mask in masks]
    parts = call(
        functools.partial(partial_kernel, sizes, len(masks)),
        [array(sizes.kept_pad, width + PAIR)] * len(masks),
        (*visitors, *kv_kept),
        5 * 10**7,
    )
    parts = [swap(part, "seq", mask) for mask, part in zip(masks, parts)]
    return call(
        functools.partial(final_kernel, sizes, len(masks)),
        array(rows),
        (offsets, q, *kv_kept, *k_rest, *v_rest, *parts),
        20 * 10**7,
    )


def solution(mesh):
    placed = P(("rep", "seq", "sub"), None)
    return jax.shard_map(
        per_device,
        mesh=mesh,
        in_specs=(placed, placed, placed, P()),
        out_specs=placed,
        check_vma=False,
    )
```

time: 82.3 us -> 37.3 us (0.45)
  blocking collectives: 62.7 us -> 0 us
  starting transfers between devices: 0 us -> 14.6 us
  waiting for transfers between devices: 0 us -> 12.5 us
  matrix products: 7.68 us -> 0 us
  Pallas kernels: 0 us -> 6.59 us
  local copies, waits for them, and re-layouts: 8.07 us -> 3.44 us
  other arithmetic: 3.36 us -> 0 us
    all_gather x4 -> x0, blocking collectives: 62.7 us -> none  [the longest x1 25.4 us: per_device(): lax.all_gather(sparse_values, ('seq', 'sub'), axis=0, tiled=True)]
    ppermute x0 -> x15, starting transfers between devices: none -> 14.6 us  [swap(): lax.ppermute(x, axis, [(n, n ^ mask) for n in range(lax.axis_size(axis))])]
    ppermute x0 -> x15, waiting for transfers between devices: none -> 12.5 us  [swap(): lax.ppermute(x, axis, [(n, n ^ mask) for n in range(lax.axis_size(axis))])]
    dot_general x27 -> x0, matrix products: 7.68 us -> none  [the longest x12 3.54 us: accumulate(): jnp.einsum('thd,shd->hts', query_heads[:, chosen], key_heads[:, chosen],...]
    pallas_call x0 -> x3, Pallas kernels: none -> 6.59 us  [call(): pl.pallas_call(kernel, out_shape=out_shape, in_specs=in_specs, out_specs=...]
    reshape x8 -> x0, local copies, waits for them, and re-layouts: 2.53 us -> none  [the longest x3 1.91 us: dilated(): source_tensor.reshape(kept_rows, dilation, heads, head_size)]
    reduce_sum x12 -> x0, other arithmetic: 2.45 us -> none  [accumulate(): totals.append(run_sum[chosen] * rescale + weights.sum(-1))]
    all_gather x4 -> x0, local copies, waits for them, and re-layouts: 1.11 us -> none  [the longest x1 0.28 us: per_device(): lax.all_gather(sparse_values, ('seq', 'sub'), axis=0, tiled=True)]
  transfers between devices with their start and end apart: 0 -> 15, of which waited for: 0 -> 8; matrix products, arithmetic and copies ran while one was open for 0% -> 0% of each run, Pallas kernels for 0% -> 2%
where the time goes in v1:
time: 37.3 us; the launch traced here: 37.1 us
  starting transfers between devices  14.6 us (39%)
  waiting for transfers between devices  12.5 us (34%)
  Pallas kernels  6.59 us (18%)
  local copies, waits for them, and re-layouts  3.44 us (9%)
    ppermute x15, starting transfers between devices, swap(): lax.ppermute(x, axis, [(n, n ^ mask) for n in range(lax.axis_size(axis))])  14.6 us
    ppermute x15, waiting for transfers between devices, swap(): lax.ppermute(x, axis, [(n, n ^ mask) for n in range(lax.axis_size(axis))])  12.5 us
    pallas_call x3, Pallas kernels, call(): pl.pallas_call(kernel, out_shape=out_shape, in_specs=in_specs, out_specs=...  6.59 us
    unnamed x10, local copies, waits for them, and re-layouts  3.44 us
  transfers between devices with their start and end apart: 15, of which 8 were waited for; matrix products, arithmetic and copies ran while one was open for 0% of the time, Pallas kernels for 2%

profile of v1, /device:TPU:0, one launch (start us, length us, event | category | flops | bytes accessed | tf_op | source)
XLA Modules:
  0.0 37.1 jit_solution(3786821837943171098)
XLA Ops:
  0.0 0.9 %copy-done = bf16[128,768]{1,0:T(8,128)(2,1)S(1)} copy-done((bf16[128,768]{1,0:T(8,128)(2,1)S(1)}, bf16[128,768]{1,0:T(8,128)(2,1)}, u32[]{:S(2)}) %copy-start) | copy-done | bytes 196632
  0.9 0.9 %copy-done.1 = bf16[128,768]{1,0:T(8,128)(2,1)S(1)} copy-done((bf16[128,768]{1,0:T(8,128)(2,1)S(1)}, bf16[128,768]{1,0:T(8,128)(2,1)}, u32[]{:S(2)}) %copy-start.1) | copy-done | bytes 196632
  1.9 0.9 %copy-done.2 = bf16[128,768]{1,0:T(8,128)(2,1)S(1)} copy-done((bf16[128,768]{1,0:T(8,128)(2,1)S(1)}, bf16[128,768]{1,0:T(8,128)(2,1)}, u32[]{:S(2)}) %copy-start.2) | copy-done | bytes 196632
  2.8 0.7 %copy-done.3 = s32[12]{0:T(128)S(1)} copy-done((s32[12]{0:T(128)S(1)}, s32[12]{0:T(128)}, u32[]{:S(2)}) %copy-start.3) | copy-done | bytes 72
  3.4 1.0 %shard_map.46 = (bf16[128,768]{1,0:T(8,128)(2,1)S(1)}, bf16[32,768]{1,0:T(8,128)(2,1)S(1)}, bf16[32,1536]{1,0:T(8,128)(2,1)S(1)}, bf16[96,768]{1,0:T(8,128)(2,1)S(1)}, bf16[96,768]{1,0:T(8,128)(2,1)S(1)}) custom-call(s32[12]{0:T(128)S(1)} %copy-done.3, bf16[128,768]{1,0:T(8,128)(2,1)S(1)} %copy-done, bf16[128,768]{1,0:T(8,128)(2,1)S(1)} %copy-done.1, ...), custom_call_target="tpu_custom_call" | custom-call | flops 20000000 | bytes 589848 | tf_op jit(solution)/shard_map/pallas_call | solution.py:211
  4.4 5.1 %collective-permute-start.11 = (bf16[32,768]{1,0:T(8,128)(2,1)S(1)}, bf16[32,768]{1,0:T(8,128)(2,1)S(1)}, u32[]{:S(2)}, u32[]{:S(2)}) collective-permute-start(bf16[32,768]{1,0:T(8,128)(2,1)S(1)} %get-tuple-element.17), channel_id=1, source_target_pairs={{0,12},{4,8},{8,4},{12,0},{1,13},{5,9},{9,5},{13,1},{2,14},{6,10},... | collective-permute-start | bytes 147464 | tf_op jit(solution)/shard_map/ppermute | solution.py:230
  9.6 0.0 collective-permute-start.10
  9.6 0.0 collective-permute-start.1
  9.6 1.5 %collective-permute-start.3 = (bf16[96,768]{1,0:T(8,128)(2,1)S(1)}, bf16[96,768]{1,0:T(8,128)(2,1)S(1)}, u32[]{:S(2)}, u32[]{:S(2)}) collective-permute-start(bf16[96,768]{1,0:T(8,128)(2,1)S(1)} %get-tuple-element.15.refs_6_), channel_id=1, source_target_pairs={{0,2},{1,3},{2,0},{3,1},{4,6},{5,7},{6,4},{7,5},{8,10},{9,11},{10,... | collective-permute-start | bytes 442376 | tf_op jit(solution)/shard_map/ppermute | solution.py:230
  11.1 0.5 %collective-permute-start.6 = (bf16[96,768]{1,0:T(8,128)(2,1)S(1)}, bf16[96,768]{1,0:T(8,128)(2,1)S(1)}, u32[]{:S(2)}, u32[]{:S(2)}) collective-permute-start(bf16[96,768]{1,0:T(8,128)(2,1)S(1)} %get-tuple-element.16.refs_10_), channel_id=1, source_target_pairs={{0,2},{1,3},{2,0},{3,1},{4,6},{5,7},{6,4},{7,5},{8,10},{9,11},{10,... | collective-permute-start | bytes 442376 | tf_op jit(solution)/shard_map/ppermute | solution.py:230
  11.6 0.2 collective-permute-done.11.refs_2_
  11.8 1.8 %collective-permute-start = (bf16[32,1536]{1,0:T(8,128)(2,1)S(1)}, bf16[32,1536]{1,0:T(8,128)(2,1)S(1)}, u32[]{:S(2)}, u32[]{:S(2)}) collective-permute-start(bf16[32,1536]{1,0:T(8,128)(2,1)S(1)} %get-tuple-element.14.refs_3_.refs_2_), channel_id=1, source_target_pairs={{0,2},{1,3},{2,0},{3,1},{4,6},{5,7},{6,4},{7,5},{8,10},{9,11},{10,... | collective-permute-start | bytes 294920 | tf_op jit(solution)/shard_map/ppermute | solution.py:230
  13.6 1.0 %collective-permute-done.10.refs_1_ = bf16[32,768]{1,0:T(8,128)(2,1)S(1)} collective-permute-done((bf16[32,768]{1,0:T(8,128)(2,1)S(1)}, bf16[32,768]{1,0:T(8,128)(2,1)S(1)}, u32[]{:S(2)}, u32[]{:S(2)}) %collective-permute-start.10) | collective-permute-done | bytes 49184 | tf_op jit(solution)/shard_map/ppermute | solution.py:230
  14.5 0.0 collective-permute-start.9
  14.5 4.1 %collective-permute-done.9.refs_0_ = bf16[32,768]{1,0:T(8,128)(2,1)S(1)} collective-permute-done((bf16[32,768]{1,0:T(8,128)(2,1)S(1)}, bf16[32,768]{1,0:T(8,128)(2,1)S(1)}, u32[]{:S(2)}, u32[]{:S(2)}) %collective-permute-start.9) | collective-permute-done | bytes 49184 | tf_op jit(solution)/shard_map/ppermute | solution.py:230
  18.6 0.0 collective-permute-start.4
  18.6 0.5 %collective-permute-start.7 = (bf16[96,768]{1,0:T(8,128)(2,1)S(1)}, bf16[96,768]{1,0:T(8,128)(2,1)S(1)}, u32[]{:S(2)}, u32[]{:S(2)}) collective-permute-start(bf16[96,768]{1,0:T(8,128)(2,1)S(1)} %get-tuple-element.16.refs_10_), channel_id=1, source_target_pairs={{0,1},{1,0},{2,3},{3,2},{4,5},{5,4},{6,7},{7,6},{8,9},{9,8},{10,11... | collective-permute-start | bytes 442376 | tf_op jit(solution)/shard_map/ppermute | solution.py:230
  19.2 1.9 %collective-permute-done.refs_4_.refs_3_ = bf16[32,1536]{1,0:T(8,128)(2,1)S(1)} collective-permute-done((bf16[32,1536]{1,0:T(8,128)(2,1)S(1)}, bf16[32,1536]{1,0:T(8,128)(2,1)S(1)}, u32[]{:S(2)}, u32[]{:S(2)}) %collective-permute-start) | collective-permute-done | bytes 98336 | tf_op jit(solution)/shard_map/ppermute | solution.py:230
  21.1 0.0 collective-permute-done.3.refs_7_
  21.1 0.5 %collective-permute-start.5 = (bf16[96,768]{1,0:T(8,128)(2,1)S(1)}, bf16[96,768]{1,0:T(8,128)(2,1)S(1)}, u32[]{:S(2)}, u32[]{:S(2)}) collective-permute-start(bf16[96,768]{1,0:T(8,128)(2,1)S(1)} %collective-permute-done.3.refs_7_), channel_id=1, source_target_pairs={{0,1},{1,0},{2,3},{3,2},{4,5},{5,4},{6,7},{7,6},{8,9},{9,8},{10,11... | collective-permute-start | bytes 442376 | tf_op jit(solution)/shard_map/ppermute | solution.py:230
  21.6 0.0 collective-permute-done.6.refs_11_
  21.6 0.1 collective-permute-start.8
  21.7 0.7 %collective-permute-done.2.refs_6_.refs_5_ = bf16[32,1536]{1,0:T(8,128)(2,1)S(1)} collective-permute-done((bf16[32,1536]{1,0:T(8,128)(2,1)S(1)}, bf16[32,1536]{1,0:T(8,128)(2,1)S(1)}, u32[]{:S(2)}, u32[]{:S(2)}) %collective-permute-start.2) | collective-permute-done | bytes 98336 | tf_op jit(solution)/shard_map/ppermute | solution.py:230
  22.4 0.8 %shard_map.47 = (bf16[32,896]{1,0:T(8,128)(2,1)S(1)}, bf16[32,896]{1,0:T(8,128)(2,1)S(1)}, bf16[32,896]{1,0:T(8,128)(2,1)S(1)}) custom-call(bf16[32,768]{1,0:T(8,128)(2,1)S(1)} %collective-permute-done.9.refs_0_, bf16[32,768]{1,0:T(8,128)(2,1)S(1)} %collective-permute-done.10.refs_1_, bf16[32,768]{1,0:T(8,128)(2,1)S(1)} %collective-permute-done.11.refs_2_, ...), custom_call_target="tpu_custom_call" | custom-call | flops 50000000 | bytes 540672 | tf_op jit(solution)/shard_map/pallas_call | solution.py:211
  23.2 0.7 %collective-permute-start.12 = (bf16[32,896]{1,0:T(8,128)(2,1)S(1)}, bf16[32,896]{1,0:T(8,128)(2,1)S(1)}, u32[]{:S(2)}, u32[]{:S(2)}) collective-permute-start(bf16[32,896]{1,0:T(8,128)(2,1)S(1)} %get-tuple-element.18), channel_id=1, source_target_pairs={{0,4},{4,0},{8,12},{12,8},{1,5},{5,1},{9,13},{13,9},{2,6},{6,2},{1... | collective-permute-start | bytes 172040 | tf_op jit(solution)/shard_map/ppermute | solution.py:230
  23.9 2.4 %collective-permute-start.13 = (bf16[32,896]{1,0:T(8,128)(2,1)S(1)}, bf16[32,896]{1,0:T(8,128)(2,1)S(1)}, u32[]{:S(2)}, u32[]{:S(2)}) collective-permute-start(bf16[32,896]{1,0:T(8,128)(2,1)S(1)} %get-tuple-element.19), channel_id=1, source_target_pairs={{0,8},{4,12},{8,0},{12,4},{1,9},{5,13},{9,1},{13,5},{2,10},{6,14},... | collective-permute-start | bytes 172040 | tf_op jit(solution)/shard_map/ppermute | solution.py:230
  26.3 1.5 %collective-permute-start.14 = (bf16[32,896]{1,0:T(8,128)(2,1)S(1)}, bf16[32,896]{1,0:T(8,128)(2,1)S(1)}, u32[]{:S(2)}, u32[]{:S(2)}) collective-permute-start(bf16[32,896]{1,0:T(8,128)(2,1)S(1)} %get-tuple-element.20), channel_id=1, source_target_pairs={{0,12},{4,8},{8,4},{12,0},{1,13},{5,9},{9,5},{13,1},{2,14},{6,10},... | collective-permute-start | bytes 172040 | tf_op jit(solution)/shard_map/ppermute | solution.py:230
  27.7 0.3 collective-permute-done.12.refs_14_
  28.1 0.9 %collective-permute-done.13.refs_15_ = bf16[32,896]{1,0:T(8,128)(2,1)S(1)} collective-permute-done((bf16[32,896]{1,0:T(8,128)(2,1)S(1)}, bf16[32,896]{1,0:T(8,128)(2,1)S(1)}, u32[]{:S(2)}, u32[]{:S(2)}) %collective-permute-start.13) | collective-permute-done | bytes 57376 | tf_op jit(solution)/shard_map/ppermute | solution.py:230
  29.0 3.3 %collective-permute-done.14.refs_16_ = bf16[32,896]{1,0:T(8,128)(2,1)S(1)} collective-permute-done((bf16[32,896]{1,0:T(8,128)(2,1)S(1)}, bf16[32,896]{1,0:T(8,128)(2,1)S(1)}, u32[]{:S(2)}, u32[]{:S(2)}) %collective-permute-start.14) | collective-permute-done | bytes 57376 | tf_op jit(solution)/shard_map/ppermute | solution.py:230
  32.3 0.0 collective-permute-done.5.refs_9_
  32.3 4.8 %shard_map.48 = bf16[128,768]{1,0:T(8,128)(2,1)} custom-call(s32[12]{0:T(128)S(1)} %copy-done.4, bf16[128,768]{1,0:T(8,128)(2,1)S(1)} %get-tuple-element.13.refs_1_, bf16[32,1536]{1,0:T(8,128)(2,1)S(1)} %get-tuple-element.14.refs_3_.refs_2_, bf16[32,1536]{1,0:T(8,128)(2,1)S(1)} %collective-permute-done.refs_4_.refs_3_, ...), custom_call_target="tpu_custom_call" | custom-call | flops 200000000 | bytes 1941528 | tf_op jit(solution)/shard_map/pallas_call | solution.py:211
  (11 shorter events, 0.0 us)
Async XLA Ops:
  0.0 0.9 %copy-start = (bf16[128,768]{1,0:T(8,128)(2,1)S(1)}, bf16[128,768]{1,0:T(8,128)(2,1)}, u32[]{:S(2)}) copy-start(bf16[128,768]{1,0:T(8,128)(2,1)} %q_ref.1) | copy-start | bytes 589828
  0.9 0.9 %copy-start.1 = (bf16[128,768]{1,0:T(8,128)(2,1)S(1)}, bf16[128,768]{1,0:T(8,128)(2,1)}, u32[]{:S(2)}) copy-start(bf16[128,768]{1,0:T(8,128)(2,1)} %k_ref.1) | copy-start | bytes 589828
  1.9 0.9 %copy-start.2 = (bf16[128,768]{1,0:T(8,128)(2,1)S(1)}, bf16[128,768]{1,0:T(8,128)(2,1)}, u32[]{:S(2)}) copy-start(bf16[128,768]{1,0:T(8,128)(2,1)} %v_ref.1) | copy-start | bytes 589828
  2.8 0.7 %copy-start.3 = (s32[12]{0:T(128)S(1)}, s32[12]{0:T(128)}, u32[]{:S(2)}) copy-start(s32[12]{0:T(128)} %refs_0_.1) | copy-start | bytes 148
  4.4 7.3 %collective-permute-start.11 = (bf16[32,768]{1,0:T(8,128)(2,1)S(1)}, bf16[32,768]{1,0:T(8,128)(2,1)S(1)}, u32[]{:S(2)}, u32[]{:S(2)}) collective-permute-start(bf16[32,768]{1,0:T(8,128)(2,1)S(1)} %get-tuple-element.17), channel_id=1, source_target_pairs={{0,12},{4,8},{8,4},{12,0},{1,13},{5,9},{9,5},{13,1},{2,14},{6,10},... | collective-permute-start | bytes 147464 | tf_op jit(solution)/shard_map/ppermute | solution.py:230
  9.6 5.0 %collective-permute-start.10 = (bf16[32,768]{1,0:T(8,128)(2,1)S(1)}, bf16[32,768]{1,0:T(8,128)(2,1)S(1)}, u32[]{:S(2)}, u32[]{:S(2)}) collective-permute-start(bf16[32,768]{1,0:T(8,128)(2,1)S(1)} %get-tuple-element.17), channel_id=1, source_target_pairs={{0,8},{4,12},{8,0},{12,4},{1,9},{5,13},{9,1},{13,5},{2,10},{6,14},... | collective-permute-start | bytes 147464 | tf_op jit(solution)/shard_map/ppermute | solution.py:230
  9.6 9.1 %collective-permute-start.1 = (bf16[32,1536]{1,0:T(8,128)(2,1)S(1)}, bf16[32,1536]{1,0:T(8,128)(2,1)S(1)}, u32[]{:S(2)}, u32[]{:S(2)}) collective-permute-start(bf16[32,1536]{1,0:T(8,128)(2,1)S(1)} %get-tuple-element.14.refs_3_.refs_2_), channel_id=1, source_target_pairs={{0,1},{1,0},{2,3},{3,2},{4,5},{5,4},{6,7},{7,6},{8,9},{9,8},{10,11... | collective-permute-start | bytes 294920 | tf_op jit(solution)/shard_map/ppermute | solution.py:230
  9.6 11.5 %collective-permute-start.3 = (bf16[96,768]{1,0:T(8,128)(2,1)S(1)}, bf16[96,768]{1,0:T(8,128)(2,1)S(1)}, u32[]{:S(2)}, u32[]{:S(2)}) collective-permute-start(bf16[96,768]{1,0:T(8,128)(2,1)S(1)} %get-tuple-element.15.refs_6_), channel_id=1, source_target_pairs={{0,2},{1,3},{2,0},{3,1},{4,6},{5,7},{6,4},{7,5},{8,10},{9,11},{10,... | collective-permute-start | bytes 442376 | tf_op jit(solution)/shard_map/ppermute | solution.py:230
  11.1 10.6 %collective-permute-start.6 = (bf16[96,768]{1,0:T(8,128)(2,1)S(1)}, bf16[96,768]{1,0:T(8,128)(2,1)S(1)}, u32[]{:S(2)}, u32[]{:S(2)}) collective-permute-start(bf16[96,768]{1,0:T(8,128)(2,1)S(1)} %get-tuple-element.16.refs_10_), channel_id=1, source_target_pairs={{0,2},{1,3},{2,0},{3,1},{4,6},{5,7},{6,4},{7,5},{8,10},{9,11},{10,... | collective-permute-start | bytes 442376 | tf_op jit(solution)/shard_map/ppermute | solution.py:230
  11.8 9.3 %collective-permute-start = (bf16[32,1536]{1,0:T(8,128)(2,1)S(1)}, bf16[32,1536]{1,0:T(8,128)(2,1)S(1)}, u32[]{:S(2)}, u32[]{:S(2)}) collective-permute-start(bf16[32,1536]{1,0:T(8,128)(2,1)S(1)} %get-tuple-element.14.refs_3_.refs_2_), channel_id=1, source_target_pairs={{0,2},{1,3},{2,0},{3,1},{4,6},{5,7},{6,4},{7,5},{8,10},{9,11},{10,... | collective-permute-start | bytes 294920 | tf_op jit(solution)/shard_map/ppermute | solution.py:230
  14.5 4.1 %collective-permute-start.9 = (bf16[32,768]{1,0:T(8,128)(2,1)S(1)}, bf16[32,768]{1,0:T(8,128)(2,1)S(1)}, u32[]{:S(2)}, u32[]{:S(2)}) collective-permute-start(bf16[32,768]{1,0:T(8,128)(2,1)S(1)} %get-tuple-element.17), channel_id=1, source_target_pairs={{0,4},{4,0},{8,12},{12,8},{1,5},{5,1},{9,13},{13,9},{2,6},{6,2},{1... | collective-permute-start | bytes 147464 | tf_op jit(solution)/shard_map/ppermute | solution.py:230
  18.6 5.3 %collective-permute-start.4 = (bf16[96,768]{1,0:T(8,128)(2,1)S(1)}, bf16[96,768]{1,0:T(8,128)(2,1)S(1)}, u32[]{:S(2)}, u32[]{:S(2)}) collective-permute-start(bf16[96,768]{1,0:T(8,128)(2,1)S(1)} %get-tuple-element.15.refs_6_), channel_id=1, source_target_pairs={{0,1},{1,0},{2,3},{3,2},{4,5},{5,4},{6,7},{7,6},{8,9},{9,8},{10,11... | collective-permute-start | bytes 442376 | tf_op jit(solution)/shard_map/ppermute | solution.py:230
  18.6 7.6 %collective-permute-start.7 = (bf16[96,768]{1,0:T(8,128)(2,1)S(1)}, bf16[96,768]{1,0:T(8,128)(2,1)S(1)}, u32[]{:S(2)}, u32[]{:S(2)}) collective-permute-start(bf16[96,768]{1,0:T(8,128)(2,1)S(1)} %get-tuple-element.16.refs_10_), channel_id=1, source_target_pairs={{0,1},{1,0},{2,3},{3,2},{4,5},{5,4},{6,7},{7,6},{8,9},{9,8},{10,11... | collective-permute-start | bytes 442376 | tf_op jit(solution)/shard_map/ppermute | solution.py:230
  21.1 1.3 %collective-permute-start.2 = (bf16[32,1536]{1,0:T(8,128)(2,1)S(1)}, bf16[32,1536]{1,0:T(8,128)(2,1)S(1)}, u32[]{:S(2)}, u32[]{:S(2)}) collective-permute-start(bf16[32,1536]{1,0:T(8,128)(2,1)S(1)} %collective-permute-done.refs_4_.refs_3_), channel_id=1, source_target_pairs={{0,1},{1,0},{2,3},{3,2},{4,5},{5,4},{6,7},{7,6},{8,9},{9,8},{10,11... | collective-permute-start | bytes 294920 | tf_op jit(solution)/shard_map/ppermute | solution.py:230
  21.1 11.2 %collective-permute-start.5 = (bf16[96,768]{1,0:T(8,128)(2,1)S(1)}, bf16[96,768]{1,0:T(8,128)(2,1)S(1)}, u32[]{:S(2)}, u32[]{:S(2)}) collective-permute-start(bf16[96,768]{1,0:T(8,128)(2,1)S(1)} %collective-permute-done.3.refs_7_), channel_id=1, source_target_pairs={{0,1},{1,0},{2,3},{3,2},{4,5},{5,4},{6,7},{7,6},{8,9},{9,8},{10,11... | collective-permute-start | bytes 442376 | tf_op jit(solution)/shard_map/ppermute | solution.py:230
  21.6 10.7 %collective-permute-start.8 = (bf16[96,768]{1,0:T(8,128)(2,1)S(1)}, bf16[96,768]{1,0:T(8,128)(2,1)S(1)}, u32[]{:S(2)}, u32[]{:S(2)}) collective-permute-start(bf16[96,768]{1,0:T(8,128)(2,1)S(1)} %collective-permute-done.6.refs_11_), channel_id=1, source_target_pairs={{0,1},{1,0},{2,3},{3,2},{4,5},{5,4},{6,7},{7,6},{8,9},{9,8},{10,11... | collective-permute-start | bytes 442376 | tf_op jit(solution)/shard_map/ppermute | solution.py:230
  23.2 4.9 %collective-permute-start.12 = (bf16[32,896]{1,0:T(8,128)(2,1)S(1)}, bf16[32,896]{1,0:T(8,128)(2,1)S(1)}, u32[]{:S(2)}, u32[]{:S(2)}) collective-permute-start(bf16[32,896]{1,0:T(8,128)(2,1)S(1)} %get-tuple-element.18), channel_id=1, source_target_pairs={{0,4},{4,0},{8,12},{12,8},{1,5},{5,1},{9,13},{13,9},{2,6},{6,2},{1... | collective-permute-start | bytes 172040 | tf_op jit(solution)/shard_map/ppermute | solution.py:230
  23.9 5.1 %collective-permute-start.13 = (bf16[32,896]{1,0:T(8,128)(2,1)S(1)}, bf16[32,896]{1,0:T(8,128)(2,1)S(1)}, u32[]{:S(2)}, u32[]{:S(2)}) collective-permute-start(bf16[32,896]{1,0:T(8,128)(2,1)S(1)} %get-tuple-element.19), channel_id=1, source_target_pairs={{0,8},{4,12},{8,0},{12,4},{1,9},{5,13},{9,1},{13,5},{2,10},{6,14},... | collective-permute-start | bytes 172040 | tf_op jit(solution)/shard_map/ppermute | solution.py:230
  26.3 6.0 %copy-start.4 = (s32[12]{0:T(128)S(1)}, s32[12]{0:T(128)}, u32[]{:S(2)}) copy-start(s32[12]{0:T(128)} %refs_0_.1) | copy-start | bytes 148
  26.3 6.0 %collective-permute-start.14 = (bf16[32,896]{1,0:T(8,128)(2,1)S(1)}, bf16[32,896]{1,0:T(8,128)(2,1)S(1)}, u32[]{:S(2)}, u32[]{:S(2)}) collective-permute-start(bf16[32,896]{1,0:T(8,128)(2,1)S(1)} %get-tuple-element.20), channel_id=1, source_target_pairs={{0,12},{4,8},{8,4},{12,0},{1,13},{5,9},{9,5},{13,1},{2,14},{6,10},... | collective-permute-start | bytes 172040 | tf_op jit(solution)/shard_map/ppermute | solution.py:230

commit v2 on v1

v2 whole, which is shorter than its diff:
```python
import functools

import jax
import jax.numpy as jnp
from jax import lax
from jax.experimental import pallas as pl
from jax.experimental.pallas import tpu as pltpu
from jax.sharding import PartitionSpec as P

ATTENTION_HEADS = 12
HEAD_DIMENSION = 64
PAIR = 2 * HEAD_DIMENSION
LOWEST = -1e30
LIMIT = 56
LEAD = 32
COST = (10**6, 10**6, 10**6, 10**6, 10**10, 10**6)


def round_up(count, step):
    return -(-count // step) * step


class Sizes:
    def __init__(self, rows, dilation, sub):
        self.rows, self.dilation, self.sub = rows, dilation, sub
        self.kept = rows // dilation
        self.rest = rows - self.kept
        self.kept_pad = round_up(self.kept, 16)
        self.rest_pad = round_up(self.rest, 16)
        self.all_pad = self.kept_pad + self.rest_pad
        self.first = 2 * self.kept_pad + LEAD * rows // 128
        self.second = 2 * self.all_pad - self.first
        self.shift = dilation.bit_length() - 1
        self.kept_keys = sub * self.kept_pad
        self.keys = sub * self.all_pad
        self.padded = self.kept_pad != self.kept or self.rest_pad != self.rest


def target_rows(sizes, position, offset):
    residue = jnp.bitwise_and(position, sizes.dilation - 1)
    group = jnp.right_shift(position, sizes.shift)
    slab = jnp.bitwise_and(residue - offset + sizes.dilation, sizes.dilation - 1)
    return jnp.where(slab == 0, group, sizes.kept_pad + (slab - 1) * sizes.kept + group)


def order_rows(sizes, offset):
    shape = (sizes.all_pad, sizes.rows)
    place = lax.broadcasted_iota(jnp.int32, shape, 0)
    target = target_rows(sizes, lax.broadcasted_iota(jnp.int32, (1, sizes.rows), 1), offset)
    return jnp.where(place == target, 1.0, 0.0).astype(jnp.bfloat16)


def restore_rows(sizes, offset):
    shape = (sizes.rows, sizes.all_pad)
    place = lax.broadcasted_iota(jnp.int32, shape, 1)
    target = target_rows(sizes, lax.broadcasted_iota(jnp.int32, shape, 0), offset)
    return jnp.where(place == target, 1.0, 0.0).astype(jnp.bfloat16)


def first_head(shape):
    return lax.broadcasted_iota(jnp.int32, shape, 1) < HEAD_DIMENSION


def dot(a, b):
    return jnp.dot(a, b, preferred_element_type=jnp.float32)


def dot_rows(a, b):
    return lax.dot_general(a, b, (((1,), (1,)), ((), ())), preferred_element_type=jnp.float32)


def select(both, rows, columns=slice(0, PAIR)):
    return jnp.where(first_head((rows, PAIR)), both[:rows, columns], both[rows:, columns])


def order_rows_of_pair(sizes, offset, pair, count):
    return jnp.concatenate([order_rows(sizes, offset(2 * pair + n))[:count] for n in range(2)], 0)


def fetch(sources, targets, sems):
    copies = [pltpu.make_async_copy(s, t, sems.at[n]) for n, (s, t) in enumerate(zip(sources, targets))]
    for copy in copies:
        copy.start()
    for copy in copies:
        copy.wait()


def first_kernel(sizes, *refs):
    qd_ref, first_ref, lanes_ref = refs[4:7]
    off_ref, q_ref, k_ref, v_ref, sems = refs[7:]
    fetch(refs[:4], (off_ref, q_ref, k_ref, v_ref), sems)
    kept = sizes.kept_pad
    count = sizes.first - kept
    scale = HEAD_DIMENSION ** (-0.5)
    lanes = lax.broadcasted_iota(jnp.int32, lanes_ref.shape, 0)
    spread_out = jnp.zeros(lanes_ref.shape, jnp.int32)
    for head in range(q_ref.shape[1] // HEAD_DIMENSION):
        spread_out = jnp.where(lanes == head, off_ref[head], spread_out)
    lanes_ref[...] = spread_out
    for pair in range(q_ref.shape[1] // PAIR):
        cols = slice(pair * PAIR, (pair + 1) * PAIR)
        chosen = order_rows_of_pair(sizes, lambda head: off_ref[head], pair, count)
        both = dot(chosen, jnp.concatenate([q_ref[:, cols], k_ref[:, cols], v_ref[:, cols]], 1))
        k = select(both, count, slice(PAIR, 2 * PAIR)).astype(jnp.bfloat16)
        qd_ref[:, cols] = (select(both, count)[:kept] * scale).astype(jnp.bfloat16)
        first_ref[:kept, cols] = k[:kept]
        first_ref[kept : 2 * kept, cols] = select(both, count, slice(2 * PAIR, 3 * PAIR))[:kept].astype(jnp.bfloat16)
        first_ref[2 * kept :, cols] = k[kept:]


def order_kernel(sizes, off_ref, q_ref, k_ref, v_ref, qs_ref, own_ref, second_ref):
    kept, count = sizes.kept_pad, sizes.all_pad
    scale = HEAD_DIMENSION ** (-0.5)
    for pair in range(q_ref.shape[1] // PAIR):
        cols = slice(pair * PAIR, (pair + 1) * PAIR)
        chosen = order_rows_of_pair(sizes, lambda head: off_ref[head], pair, count)
        both = dot(chosen, jnp.concatenate([q_ref[:, cols], k_ref[:, cols], v_ref[:, cols]], 1))
        qs_ref[:, cols] = (select(both, count) * scale).astype(jnp.bfloat16)
        k = select(both, count, slice(PAIR, 2 * PAIR)).astype(jnp.bfloat16)
        v = select(both, count, slice(2 * PAIR, 3 * PAIR)).astype(jnp.bfloat16)
        own = jnp.concatenate([k[:kept], v[:kept], k[kept:], v[kept:]], 0)
        own_ref[:, cols] = own
        second_ref[:, cols] = own[sizes.first :]


def rows_of(device, begin, count, cols):
    found = []
    for ref, base, size in device:
        low, high = max(begin, 0), min(begin + count, size)
        if low < high:
            found.append(ref[base + low : base + high, cols])
        begin -= size
    return found


def both_heads(q):
    mask = first_head(q.shape)
    zero = jnp.zeros_like(q)
    return jnp.concatenate([jnp.where(mask, q, zero), jnp.where(mask, zero, q)], 0)


def with_ones(v):
    return jnp.concatenate([v, jnp.ones_like(v)], 1)


def hide(col, step, used):
    return jnp.where(lax.rem(col + step, step) < used, 0.0, LOWEST)


def weigh(scores, top, v):
    weights = jnp.exp(scores - top).astype(jnp.bfloat16)
    return dot(weights, with_ones(v))


def sources(refs, parts):
    found = [[(r, 0, r.shape[0])] for r in refs[:2]]
    for n in range(2, len(refs), parts):
        for core in range(2):
            sizes = [(r, r.shape[0] // 2) for r in refs[n : n + parts]]
            found.append([(r, core * size, size) for r, size in sizes])
    return found


def join(devices, begin, count, cols):
    return [x for d in devices for x in rows_of(d, begin, count, cols)]


def collect_kernel(count, *refs):
    for n, r in enumerate(refs[:count]):
        refs[-1][n * r.shape[0] : (n + 1) * r.shape[0]] = r[...]


def partial_kernel(sizes, others, q_ref, *refs):
    out_refs = refs[-others:]
    devices = sources(refs[:-others], 1)
    width = q_ref.shape[1]
    kept = sizes.kept_pad
    rows = others * kept
    lane = lax.broadcasted_iota(jnp.int32, (rows, PAIR), 1)
    stats = jnp.zeros((rows, PAIR), jnp.float32)
    for pair in range(width // PAIR):
        cols = slice(pair * PAIR, (pair + 1) * PAIR)
        q = q_ref[:, cols]
        k = jnp.concatenate(join(devices, 0, kept, cols), 0)
        v = jnp.concatenate(join(devices, kept, kept, cols), 0)
        scores = dot_rows(both_heads(q), k)
        if sizes.padded:
            scores += hide(lax.broadcasted_iota(jnp.int32, (1, sizes.kept_keys), 1), kept, sizes.kept)
        top = jnp.max(scores, 1, keepdims=True).astype(jnp.bfloat16).astype(jnp.float32)
        both = weigh(scores, top, v)
        lead, follow = both[:rows], both[rows:]
        out = select(both, rows).astype(jnp.bfloat16)
        for n, r in enumerate(out_refs):
            r[:, cols] = out[n * kept : (n + 1) * kept]
        for n, part in enumerate((lead, follow)):
            head = 3 * (2 * pair + n)
            total = part[:, PAIR:]
            coarse = total.astype(jnp.bfloat16).astype(jnp.float32)
            stats = jnp.where(lane == head, top[n * rows : (n + 1) * rows], stats)
            stats = jnp.where(lane == head + 1, coarse, stats)
            stats = jnp.where(lane == head + 2, total - coarse, stats)
    stats = stats.astype(jnp.bfloat16)
    for n, r in enumerate(out_refs):
        r[:, width:] = stats[n * kept : (n + 1) * kept]


def dense_kernel(sizes, *refs):
    off_ref, q_ref = refs[:2]
    devices = sources(refs[2:-4], 2)
    out_ref, total_ref, top_ref, back_ref = refs[-4:]
    width = q_ref.shape[1]
    kept, rest, rows = sizes.kept_pad, sizes.rest_pad, sizes.all_pad
    begin = sizes.kept_keys
    for pair in range(width // PAIR):
        cols = slice(pair * PAIR, (pair + 1) * PAIR)
        k = jnp.concatenate(join(devices, 0, kept, cols) + join(devices, 2 * kept, rest, cols), 0)
        v = jnp.concatenate(join(devices, kept, kept, cols) + join(devices, kept + rows, rest, cols), 0)
        scores = dot_rows(both_heads(q_ref[:, cols]), k)
        if sizes.padded:
            col = lax.broadcasted_iota(jnp.int32, (1, sizes.keys), 1)
            here = hide(col, kept, sizes.kept)
            there = hide(col - begin + sizes.keys * rest, rest, sizes.rest)
            scores += jnp.where(col < begin, here, there)
        top = jnp.max(scores, 1, keepdims=True)
        weights = jnp.exp(scores - top)
        near, far = weights[:, :begin], weights[:, begin:]
        near = jnp.concatenate(
            [near[:kept] * 2.0, near[kept:rows], near[rows : rows + kept] * 2.0, near[rows + kept :]], 0
        )
        weights = jnp.concatenate([near, far], 1).astype(jnp.bfloat16)
        both = dot(weights, with_ones(v))
        out_ref[:, cols] = select(both, rows)
        total_ref[:, cols] = select(both, rows, slice(PAIR, 2 * PAIR))
        top_ref[:, cols] = jnp.where(first_head((kept, PAIR)), top[:kept], top[rows : rows + kept])
        for n in range(2):
            place = 2 * pair + n
            back_ref[place * sizes.rows : (place + 1) * sizes.rows] = restore_rows(sizes, off_ref[place : place + 1, 0:1])


def spread(width, lanes):
    lane = lax.broadcasted_iota(jnp.int32, (PAIR, width), 0)
    head = jnp.right_shift(lax.broadcasted_iota(jnp.int32, (PAIR, width), 1), HEAD_DIMENSION.bit_length() - 1)
    hits = [jnp.where(lane == 3 * head + n, 1.0, 0.0) for n in lanes]
    return sum(hits).astype(jnp.bfloat16)


def merge_kernel(sizes, *refs):
    out_ref, total_ref, top_ref, back_ref = refs[:4]
    part_refs, done_ref = refs[4:-1], refs[-1]
    others = len(part_refs)
    width = out_ref.shape[1]
    kept = sizes.kept_pad
    stats = jnp.concatenate([r[:, width:] for r in part_refs], 0)
    tops = dot(stats, spread(width, (0,)))
    totals = dot(stats, spread(width, (1, 2)))
    results = []
    for pair in range(width // PAIR):
        cols = slice(pair * PAIR, (pair + 1) * PAIR)
        out, total = out_ref[:, cols], total_ref[:, cols]
        top = top_ref[:, cols]
        theirs = [tops[n * kept : (n + 1) * kept, cols] for n in range(others)]
        best = functools.reduce(jnp.maximum, theirs, top)
        factor = jnp.exp(top - best)
        kept_out, kept_total = out[:kept] * factor, total[:kept] * factor
        for n, r in enumerate(part_refs):
            factor = jnp.exp(theirs[n] - best)
            kept_out += r[:, cols].astype(jnp.float32) * factor
            kept_total += totals[n * kept : (n + 1) * kept, cols] * factor
        result = jnp.concatenate([kept_out / kept_total, out[kept:] / total[kept:]], 0)
        results.append(result.astype(jnp.bfloat16))
    for pair, result in enumerate(results):
        cols = slice(pair * PAIR, (pair + 1) * PAIR)
        back = dot(back_ref[2 * sizes.rows * pair : 2 * sizes.rows * (pair + 1)], result)
        done_ref[:, cols] = select(back, sizes.rows).astype(jnp.bfloat16)


def call(kernel, out_shape, operands, flops, place=pltpu.VMEM, scratch=(), limit=24):
    spec = pl.BlockSpec(memory_space=place)
    smem = pl.BlockSpec(memory_space=pltpu.SMEM)
    in_specs = [smem if x.ndim == 1 and place == pltpu.VMEM else spec for x in operands]
    out_specs = jax.tree.map(lambda _: pl.BlockSpec(memory_space=pltpu.VMEM), out_shape)
    size = sum(x.size * 2 for x in operands)
    return pl.pallas_call(
        kernel,
        out_shape=out_shape,
        in_specs=in_specs,
        out_specs=out_specs,
        scratch_shapes=scratch,
        cost_estimate=pl.CostEstimate(flops=flops, bytes_accessed=size, transcendentals=0),
        compiler_params=pltpu.CompilerParams(vmem_limit_bytes=limit * 1024 * 1024),
    )(*operands)


def per_device(queries, keys, values, offsets):
    rows, width = queries.shape
    seq, sub = lax.axis_size("seq"), lax.axis_size("sub")
    sizes = Sizes(rows, seq, sub)

    def array(count, columns=width, dtype=jnp.bfloat16):
        return jax.ShapeDtypeStruct((count, columns), dtype)

    def swap(x, axis, mask):
        return lax.ppermute(x, axis, [(n, n ^ mask) for n in range(lax.axis_size(axis))])

    def after(x, *earlier):
        return lax.optimization_barrier((x, *earlier))[0]

    def far(x):
        return [swap(x, "sub", mask) for mask in range(2, sub, 2)]

    def both_cores(lines):
        chips = [[n, n + 1] for n in range(0, sub, 2)]
        return [lax.all_gather(x, "sub", axis=0, tiled=True, axis_index_groups=chips) for x in lines]

    masks = range(1, seq)
    heads = width // HEAD_DIMENSION
    q_kept, first, lanes = call(
        functools.partial(first_kernel, sizes),
        [array(sizes.kept_pad), array(sizes.first), array(round_up(heads, 8), 128, jnp.int32)],
        (offsets, queries, keys, values),
        COST[0],
        pltpu.HBM,
        [pltpu.SMEM(offsets.shape, jnp.int32)]
        + [pltpu.VMEM((rows, width), jnp.bfloat16)] * 3
        + [pltpu.SemaphoreType.DMA((4,))],
        LIMIT,
    )
    far_first = far(first)
    visitors = [swap(q_kept, "seq", mask) for mask in masks]
    q, own, second = call(
        functools.partial(order_kernel, sizes),
        [array(n) for n in (sizes.all_pad, 2 * sizes.all_pad, sizes.second)],
        (offsets, queries, keys, values),
        COST[5],
    )
    far_second = far(after(second, *far_first))
    own = [own, swap(own, "sub", 1)]
    far_first = both_cores(far_first)
    visitors = call(
        functools.partial(collect_kernel, len(masks)),
        array(len(masks) * sizes.kept_pad),
        (*visitors, *far_first),
        COST[4],
    )
    parts = call(
        functools.partial(partial_kernel, sizes, len(masks)),
        [array(sizes.kept_pad, width + PAIR)] * len(masks),
        (visitors, *own, *far_first),
        COST[1],
    )
    returned = [swap(part, "seq", mask) for mask, part in zip(masks, parts)]
    far_second = both_cores([after(x, parts[0]) for x in far_second])
    dense = call(
        functools.partial(dense_kernel, sizes),
        [
            array(sizes.all_pad, dtype=jnp.float32),
            array(sizes.all_pad, dtype=jnp.float32),
            array(sizes.kept_pad, dtype=jnp.float32),
            array(width // PAIR * 2 * rows, sizes.all_pad),
        ],
        (lanes, q, *own, *(x for both in zip(far_first, far_second) for x in both)),
        COST[2],
    )
    return call(functools.partial(merge_kernel, sizes), array(rows), (*dense, *returned), COST[3])


def solution(mesh):
    placed = P(("rep", "seq", "sub"), None)
    return jax.shard_map(
        per_device,
        mesh=mesh,
        in_specs=(placed, placed, placed, P()),
        out_specs=placed,
        check_vma=False,
    )
```

time: 37.3 us -> 24.6 us (0.66)
  waiting for transfers between devices: 12.5 us -> 1.86 us
  blocking collectives: 0 us -> 4.28 us
  local copies, waits for them, and re-layouts: 3.44 us -> 0.02 us
  starting transfers between devices: 14.6 us -> 11.4 us
    ppermute x15 -> x9, waiting for transfers between devices: 12.5 us -> 1.86 us  [swap(): lax.ppermute(x, axis, [(n, n ^ mask) for n in range(lax.axis_size(axis))])]
    all_gather x0 -> x2, blocking collectives: none -> 4.28 us  [both_cores(): lax.all_gather(x, 'sub', axis=0, tiled=True, axis_index_groups=chips)]
    unnamed x10, local copies, waits for them, and re-layouts: 3.44 us -> 0.02 us
    ppermute x15 -> x9, starting transfers between devices: 14.6 us -> 11.4 us  [swap(): lax.ppermute(x, axis, [(n, n ^ mask) for n in range(lax.axis_size(axis))])]
    pallas_call x3 -> x6, Pallas kernels: 6.59 us -> 6.77 us  [call(): pl.pallas_call(kernel, out_shape=out_shape, in_specs=in_specs, out_specs=...]
  transfers between devices with their start and end apart: 15 -> 9, of which waited for: 8 -> 4; matrix products, arithmetic and copies ran while one was open for 0% -> 0% of each run, Pallas kernels for 2% -> 14%
where the time goes in v2:
time: 24.6 us; the launch traced here: 24.4 us
  starting transfers between devices  11.4 us (46%)
  Pallas kernels  6.77 us (28%)
  blocking collectives  4.28 us (17%)
  waiting for transfers between devices  1.86 us (8%)
    ppermute x9, starting transfers between devices, swap(): lax.ppermute(x, axis, [(n, n ^ mask) for n in range(lax.axis_size(axis))])  11.4 us
    pallas_call x6, Pallas kernels, call(): pl.pallas_call(kernel, out_shape=out_shape, in_specs=in_specs, out_specs=...  6.77 us
    all_gather x2, blocking collectives, both_cores(): lax.all_gather(x, 'sub', axis=0, tiled=True, axis_index_groups=chips)  4.28 us
    ppermute x9, waiting for transfers between devices, swap(): lax.ppermute(x, axis, [(n, n ^ mask) for n in range(lax.axis_size(axis))])  1.86 us
  transfers between devices with their start and end apart: 9, of which 4 were waited for; matrix products, arithmetic and copies ran while one was open for 0% of the time, Pallas kernels for 14%

profile of v2, /device:TPU:0, one launch (start us, length us, event | category | flops | bytes accessed | tf_op | source)
XLA Modules:
  0.0 24.4 jit_solution(16530612946198507027)
XLA Ops:
  0.0 0.0 copy-start.2
  0.0 2.2 %shard_map.46 = (bf16[32,768]{1,0:T(8,128)(2,1)}, bf16[96,768]{1,0:T(8,128)(2,1)}, s32[16,128]{1,0:T(8,128)}) custom-call(s32[12]{0:T(128)} %off_ref.1, bf16[128,768]{1,0:T(8,128)(2,1)} %q_ref.1, bf16[128,768]{1,0:T(8,128)(2,1)} %k_ref.1, bf16[128,768]{1,0:T(8,128)(2,1)} %v_ref.1), custom_call_target="tpu_custom_call" | custom-call | flops 1000000 | bytes 589848 | tf_op jit(solution)/shard_map/pallas_call | solution.py:283
  2.2 0.0 copy-start.4
  2.2 3.0 %collective-permute-start.1 = (bf16[96,768]{1,0:T(8,128)(2,1)}, bf16[96,768]{1,0:T(8,128)(2,1)S(1)}, u32[]{:S(2)}, u32[]{:S(2)}) collective-permute-start(bf16[96,768]{1,0:T(8,128)(2,1)} %get-tuple-element.23), channel_id=1, source_target_pairs={{0,2},{1,3},{2,0},{3,1},{4,6},{5,7},{6,4},{7,5},{8,10},{9,11},{10,... | collective-permute-start | bytes 442376 | tf_op jit(solution)/shard_map/ppermute | solution.py:303
  5.2 3.6 %collective-permute-start.5 = (bf16[32,768]{1,0:T(8,128)(2,1)}, bf16[32,768]{1,0:T(8,128)(2,1)S(1)}, u32[]{:S(2)}, u32[]{:S(2)}) collective-permute-start(bf16[32,768]{1,0:T(8,128)(2,1)} %get-tuple-element.26), channel_id=1, source_target_pairs={{0,12},{4,8},{8,4},{12,0},{1,13},{5,9},{9,5},{13,1},{2,14},{6,10},... | collective-permute-start | bytes 147464 | tf_op jit(solution)/shard_map/ppermute | solution.py:303
  8.8 0.0 collective-permute-start.4
  8.8 0.8 %collective-permute-start.3 = (bf16[32,768]{1,0:T(8,128)(2,1)}, bf16[32,768]{1,0:T(8,128)(2,1)S(1)}, u32[]{:S(2)}, u32[]{:S(2)}) collective-permute-start(bf16[32,768]{1,0:T(8,128)(2,1)} %get-tuple-element.26), channel_id=1, source_target_pairs={{0,4},{4,0},{8,12},{12,8},{1,5},{5,1},{9,13},{13,9},{2,6},{6,2},{1... | collective-permute-start | bytes 147464 | tf_op jit(solution)/shard_map/ppermute | solution.py:303
  9.6 0.0 copy-done.2
  9.6 0.0 copy-done.1
  9.6 0.0 copy-done
  9.6 0.0 copy-done.4
  9.6 1.0 %shard_map.47 = (bf16[128,768]{1,0:T(8,128)(2,1)S(1)}, bf16[256,768]{1,0:T(8,128)(2,1)S(1)}, bf16[160,768]{1,0:T(8,128)(2,1)S(1)}) custom-call(s32[12]{0:T(128)S(1)} %copy-done.4, bf16[128,768]{1,0:T(8,128)(2,1)S(1)} %copy-done, bf16[128,768]{1,0:T(8,128)(2,1)S(1)} %copy-done.1, bf16[128,768]{1,0:T(8,128)(2,1)S(1)} %copy-done.2), custom_call_target="tpu_custom_call" | custom-call | flops 1000000 | bytes 589848 | tf_op jit(solution)/shard_map/pallas_call | solution.py:283
  10.6 0.1 collective-permute-start
  10.7 0.0 collective-permute-done.1
  10.7 0.4 %collective-permute-start.2 = (bf16[160,768]{1,0:T(8,128)(2,1)S(1)}, bf16[160,768]{1,0:T(8,128)(2,1)S(1)}, u32[]{:S(2)}, u32[]{:S(2)}) collective-permute-start(bf16[160,768]{1,0:T(8,128)(2,1)S(1)} %get-tuple-element.25), channel_id=1, source_target_pairs={{0,2},{1,3},{2,0},{3,1},{4,6},{5,7},{6,4},{7,5},{8,10},{9,11},{10,... | collective-permute-start | bytes 737288 | tf_op jit(solution)/shard_map/ppermute | solution.py:303
  11.1 2.0 %all_gather.6.refs_3_.refs_2_.refs_4_ = bf16[192,768]{1,0:T(8,128)(2,1)S(1)} all-gather(bf16[96,768]{1,0:T(8,128)(2,1)S(1)} %collective-permute-done.1), channel_id=1, replica_groups={{0,1},{2,3},{4,5},{6,7},{8,9},{10,11},{12,13},{14,15},{16,17},{18,19},{..., dimensions={0}, use_global_device_ids=true | all-gather | bytes 442368 | tf_op jit(solution)/shard_map/all_gather | solution.py:313
  13.1 0.0 collective-permute-done.5.refs_2_
  13.1 0.9 %collective-permute-done.4.refs_1_ = bf16[32,768]{1,0:T(8,128)(2,1)S(1)} collective-permute-done((bf16[32,768]{1,0:T(8,128)(2,1)}, bf16[32,768]{1,0:T(8,128)(2,1)S(1)}, u32[]{:S(2)}, u32[]{:S(2)}) %collective-permute-start.4) | collective-permute-done | bytes 49184 | tf_op jit(solution)/shard_map/ppermute | solution.py:303
  14.0 0.0 collective-permute-done.3.refs_0_
  14.0 0.0 collective-permute-done.refs_1_.refs_3_
  14.1 0.8 %shard_map.49 = (bf16[32,896]{1,0:T(8,128)(2,1)S(1)}, bf16[32,896]{1,0:T(8,128)(2,1)S(1)}, bf16[32,896]{1,0:T(8,128)(2,1)S(1)}) custom-call(bf16[96,768]{1,0:T(8,128)(2,1)S(1)} %shard_map.48.q_ref, bf16[256,768]{1,0:T(8,128)(2,1)S(1)} %get-tuple-element.22.refs_0_.refs_2_, bf16[256,768]{1,0:T(8,128)(2,1)S(1)} %collective-permute-done.refs_1_.refs_3_, ...), custom_call_target="tpu_custom_call" | custom-call | flops 1000000 | bytes 1228800 | tf_op jit(solution)/shard_map/pallas_call | solution.py:283
  14.9 2.1 %collective-permute-start.7 = (bf16[32,896]{1,0:T(8,128)(2,1)S(1)}, bf16[32,896]{1,0:T(8,128)(2,1)S(1)}, u32[]{:S(2)}, u32[]{:S(2)}) collective-permute-start(bf16[32,896]{1,0:T(8,128)(2,1)S(1)} %get-tuple-element.33), channel_id=1, source_target_pairs={{0,8},{4,12},{8,0},{12,4},{1,9},{5,13},{9,1},{13,5},{2,10},{6,14},... | collective-permute-start | bytes 172040 | tf_op jit(solution)/shard_map/ppermute | solution.py:303
  17.0 1.0 %collective-permute-start.8 = (bf16[32,896]{1,0:T(8,128)(2,1)S(1)}, bf16[32,896]{1,0:T(8,128)(2,1)S(1)}, u32[]{:S(2)}, u32[]{:S(2)}) collective-permute-start(bf16[32,896]{1,0:T(8,128)(2,1)S(1)} %get-tuple-element.34), channel_id=1, source_target_pairs={{0,12},{4,8},{8,4},{12,0},{1,13},{5,9},{9,5},{13,1},{2,14},{6,10},... | collective-permute-start | bytes 172040 | tf_op jit(solution)/shard_map/ppermute | solution.py:303
  17.9 0.5 %collective-permute-start.6 = (bf16[32,896]{1,0:T(8,128)(2,1)S(1)}, bf16[32,896]{1,0:T(8,128)(2,1)S(1)}, u32[]{:S(2)}, u32[]{:S(2)}) collective-permute-start(bf16[32,896]{1,0:T(8,128)(2,1)S(1)} %get-tuple-element.27), channel_id=1, source_target_pairs={{0,4},{4,0},{8,12},{12,8},{1,5},{5,1},{9,13},{13,9},{2,6},{6,2},{1... | collective-permute-start | bytes 172040 | tf_op jit(solution)/shard_map/ppermute | solution.py:303
  18.4 0.7 %collective-permute-done.2 = bf16[160,768]{1,0:T(8,128)(2,1)S(1)} collective-permute-done((bf16[160,768]{1,0:T(8,128)(2,1)S(1)}, bf16[160,768]{1,0:T(8,128)(2,1)S(1)}, u32[]{:S(2)}, u32[]{:S(2)}) %collective-permute-start.2) | collective-permute-done | bytes 245792 | tf_op jit(solution)/shard_map/ppermute | solution.py:303
  19.1 2.3 %all_gather.7.refs_5_ = bf16[320,768]{1,0:T(8,128)(2,1)S(1)} all-gather(bf16[160,768]{1,0:T(8,128)(2,1)S(1)} %collective-permute-done.2), channel_id=1, replica_groups={{0,1},{2,3},{4,5},{6,7},{8,9},{10,11},{12,13},{14,15},{16,17},{18,19},{..., dimensions={0}, use_global_device_ids=true | all-gather | bytes 737280 | tf_op jit(solution)/shard_map/all_gather | solution.py:313
  21.4 0.0 copy-done.3
  21.4 1.6 %shard_map.50 = (f32[128,768]{1,0:T(8,128)S(1)}, f32[128,768]{1,0:T(8,128)S(1)}, f32[32,768]{1,0:T(8,128)S(1)}, bf16[1536,128]{1,0:T(8,128)(2,1)S(1)}) custom-call(s32[16,128]{1,0:T(8,128)S(1)} %copy-done.3, bf16[128,768]{1,0:T(8,128)(2,1)S(1)} %get-tuple-element.21.refs_1_, bf16[256,768]{1,0:T(8,128)(2,1)S(1)} %get-tuple-element.22.refs_0_.refs_2_, ...), custom_call_target="tpu_custom_call" | custom-call | flops 1000000 | bytes 1773568 | tf_op jit(solution)/shard_map/pallas_call | solution.py:283
  22.9 0.0 collective-permute-done.7.refs_5_
  22.9 0.1 collective-permute-done.8.refs_6_
  23.1 0.1 collective-permute-done.6.refs_4_
  23.2 1.2 %shard_map.51 = bf16[128,768]{1,0:T(8,128)(2,1)} custom-call(f32[128,768]{1,0:T(8,128)S(1)} %get-tuple-element.29.refs_0_, f32[128,768]{1,0:T(8,128)S(1)} %get-tuple-element.30.refs_1_, f32[32,768]{1,0:T(8,128)S(1)} %get-tuple-element.31.refs_2_, bf16[1536,128]{1,0:T(8,128)(2,1)S(1)} %get-tuple-element.32.refs_3_, ...), custom_call_target="tpu_custom_call" | custom-call | flops 1000000 | bytes 1007616 | tf_op jit(solution)/shard_map/pallas_call | solution.py:283
  (4 shorter events, 0.0 us)
Async XLA Ops:
  0.0 9.6 %copy-start.2 = (bf16[128,768]{1,0:T(8,128)(2,1)S(1)}, bf16[128,768]{1,0:T(8,128)(2,1)}, u32[]{:S(2)}) copy-start(bf16[128,768]{1,0:T(8,128)(2,1)} %v_ref.1) | copy-start | bytes 589828
  0.0 9.6 %copy-start.1 = (bf16[128,768]{1,0:T(8,128)(2,1)S(1)}, bf16[128,768]{1,0:T(8,128)(2,1)}, u32[]{:S(2)}) copy-start(bf16[128,768]{1,0:T(8,128)(2,1)} %k_ref.1) | copy-start | bytes 589828
  0.0 9.6 %copy-start = (bf16[128,768]{1,0:T(8,128)(2,1)S(1)}, bf16[128,768]{1,0:T(8,128)(2,1)}, u32[]{:S(2)}) copy-start(bf16[128,768]{1,0:T(8,128)(2,1)} %q_ref.1) | copy-start | bytes 589828
  2.2 7.4 %copy-start.4 = (s32[12]{0:T(128)S(1)}, s32[12]{0:T(128)}, u32[]{:S(2)}) copy-start(s32[12]{0:T(128)} %off_ref.1) | copy-start | bytes 148
  2.2 8.5 %collective-permute-start.1 = (bf16[96,768]{1,0:T(8,128)(2,1)}, bf16[96,768]{1,0:T(8,128)(2,1)S(1)}, u32[]{:S(2)}, u32[]{:S(2)}) collective-permute-start(bf16[96,768]{1,0:T(8,128)(2,1)} %get-tuple-element.23), channel_id=1, source_target_pairs={{0,2},{1,3},{2,0},{3,1},{4,6},{5,7},{6,4},{7,5},{8,10},{9,11},{10,... | collective-permute-start | bytes 442376 | tf_op jit(solution)/shard_map/ppermute | solution.py:303
  5.2 7.9 %collective-permute-start.5 = (bf16[32,768]{1,0:T(8,128)(2,1)}, bf16[32,768]{1,0:T(8,128)(2,1)S(1)}, u32[]{:S(2)}, u32[]{:S(2)}) collective-permute-start(bf16[32,768]{1,0:T(8,128)(2,1)} %get-tuple-element.26), channel_id=1, source_target_pairs={{0,12},{4,8},{8,4},{12,0},{1,13},{5,9},{9,5},{13,1},{2,14},{6,10},... | collective-permute-start | bytes 147464 | tf_op jit(solution)/shard_map/ppermute | solution.py:303
  8.8 5.2 %collective-permute-start.4 = (bf16[32,768]{1,0:T(8,128)(2,1)}, bf16[32,768]{1,0:T(8,128)(2,1)S(1)}, u32[]{:S(2)}, u32[]{:S(2)}) collective-permute-start(bf16[32,768]{1,0:T(8,128)(2,1)} %get-tuple-element.26), channel_id=1, source_target_pairs={{0,8},{4,12},{8,0},{12,4},{1,9},{5,13},{9,1},{13,5},{2,10},{6,14},... | collective-permute-start | bytes 147464 | tf_op jit(solution)/shard_map/ppermute | solution.py:303
  8.8 5.2 %collective-permute-start.3 = (bf16[32,768]{1,0:T(8,128)(2,1)}, bf16[32,768]{1,0:T(8,128)(2,1)S(1)}, u32[]{:S(2)}, u32[]{:S(2)}) collective-permute-start(bf16[32,768]{1,0:T(8,128)(2,1)} %get-tuple-element.26), channel_id=1, source_target_pairs={{0,4},{4,0},{8,12},{12,8},{1,5},{5,1},{9,13},{13,9},{2,6},{6,2},{1... | collective-permute-start | bytes 147464 | tf_op jit(solution)/shard_map/ppermute | solution.py:303
  10.6 3.4 %collective-permute-start = (bf16[256,768]{1,0:T(8,128)(2,1)S(1)}, bf16[256,768]{1,0:T(8,128)(2,1)S(1)}, u32[]{:S(2)}, u32[]{:S(2)}) collective-permute-start(bf16[256,768]{1,0:T(8,128)(2,1)S(1)} %get-tuple-element.22.refs_0_.refs_2_), channel_id=1, source_target_pairs={{0,1},{1,0},{2,3},{3,2},{4,5},{5,4},{6,7},{7,6},{8,9},{9,8},{10,11... | collective-permute-start | bytes 1179656 | tf_op jit(solution)/shard_map/ppermute | solution.py:303
  10.7 8.4 %collective-permute-start.2 = (bf16[160,768]{1,0:T(8,128)(2,1)S(1)}, bf16[160,768]{1,0:T(8,128)(2,1)S(1)}, u32[]{:S(2)}, u32[]{:S(2)}) collective-permute-start(bf16[160,768]{1,0:T(8,128)(2,1)S(1)} %get-tuple-element.25), channel_id=1, source_target_pairs={{0,2},{1,3},{2,0},{3,1},{4,6},{5,7},{6,4},{7,5},{8,10},{9,11},{10,... | collective-permute-start | bytes 737288 | tf_op jit(solution)/shard_map/ppermute | solution.py:303
  14.9 8.1 %collective-permute-start.7 = (bf16[32,896]{1,0:T(8,128)(2,1)S(1)}, bf16[32,896]{1,0:T(8,128)(2,1)S(1)}, u32[]{:S(2)}, u32[]{:S(2)}) collective-permute-start(bf16[32,896]{1,0:T(8,128)(2,1)S(1)} %get-tuple-element.33), channel_id=1, source_target_pairs={{0,8},{4,12},{8,0},{12,4},{1,9},{5,13},{9,1},{13,5},{2,10},{6,14},... | collective-permute-start | bytes 172040 | tf_op jit(solution)/shard_map/ppermute | solution.py:303
  17.0 6.1 %collective-permute-start.8 = (bf16[32,896]{1,0:T(8,128)(2,1)S(1)}, bf16[32,896]{1,0:T(8,128)(2,1)S(1)}, u32[]{:S(2)}, u32[]{:S(2)}) collective-permute-start(bf16[32,896]{1,0:T(8,128)(2,1)S(1)} %get-tuple-element.34), channel_id=1, source_target_pairs={{0,12},{4,8},{8,4},{12,0},{1,13},{5,9},{9,5},{13,1},{2,14},{6,10},... | collective-permute-start | bytes 172040 | tf_op jit(solution)/shard_map/ppermute | solution.py:303
  17.9 5.3 %collective-permute-start.6 = (bf16[32,896]{1,0:T(8,128)(2,1)S(1)}, bf16[32,896]{1,0:T(8,128)(2,1)S(1)}, u32[]{:S(2)}, u32[]{:S(2)}) collective-permute-start(bf16[32,896]{1,0:T(8,128)(2,1)S(1)} %get-tuple-element.27), channel_id=1, source_target_pairs={{0,4},{4,0},{8,12},{12,8},{1,5},{5,1},{9,13},{13,9},{2,6},{6,2},{1... | collective-permute-start | bytes 172040 | tf_op jit(solution)/shard_map/ppermute | solution.py:303
  19.1 2.3 %copy-start.3 = (s32[16,128]{1,0:T(8,128)S(1)}, s32[16,128]{1,0:T(8,128)}, u32[]{:S(2)}) copy-start(s32[16,128]{1,0:T(8,128)} %get-tuple-element.20.refs_0_) | copy-start | bytes 24580

commit v3 on v2

--- a/solution.py
+++ b/solution.py
@@ -12,8 +12,7 @@
 PAIR = 2 * HEAD_DIMENSION
 LOWEST = -1e30
 LIMIT = 56
-LEAD = 32
-COST = (10**6, 10**6, 10**6, 10**6, 10**10, 10**6)
+COST = (10**6, 10**6, 10**10, 0, 0, 10**6, 10**6, 10**6)
 
 
 def round_up(count, step):
@@ -28,8 +27,8 @@
         self.kept_pad = round_up(self.kept, 16)
         self.rest_pad = round_up(self.rest, 16)
         self.all_pad = self.kept_pad + self.rest_pad
-        self.first = 2 * self.kept_pad + LEAD * rows // 128
-        self.second = 2 * self.all_pad - self.first
+        self.first = 2 * self.kept_pad
+        self.second = 2 * self.rest_pad
         self.shift = dilation.bit_length() - 1
         self.kept_keys = sub * self.kept_pad
         self.keys = sub * self.all_pad
@@ -86,11 +85,10 @@
 
 
 def first_kernel(sizes, *refs):
-    qd_ref, first_ref, lanes_ref = refs[4:7]
-    off_ref, q_ref, k_ref, v_ref, sems = refs[7:]
+    qd_ref, first_ref, second_ref, lanes_ref = refs[4:8]
+    off_ref, q_ref, k_ref, v_ref, sems = refs[8:]
     fetch(refs[:4], (off_ref, q_ref, k_ref, v_ref), sems)
-    kept = sizes.kept_pad
-    count = sizes.first - kept
+    kept, rest, count = sizes.kept_pad, sizes.rest_pad, sizes.all_pad
     scale = HEAD_DIMENSION ** (-0.5)
     lanes = lax.broadcasted_iota(jnp.int32, lanes_ref.shape, 0)
     spread_out = jnp.zeros(lanes_ref.shape, jnp.int32)
@@ -101,14 +99,17 @@
         cols = slice(pair * PAIR, (pair + 1) * PAIR)
         chosen = order_rows_of_pair(sizes, lambda head: off_ref[head], pair, count)
         both = dot(chosen, jnp.concatenate([q_ref[:, cols], k_ref[:, cols], v_ref[:, cols]], 1))
+        q = select(both, count)[:kept] * scale
         k = select(both, count, slice(PAIR, 2 * PAIR)).astype(jnp.bfloat16)
-        qd_ref[:, cols] = (select(both, count)[:kept] * scale).astype(jnp.bfloat16)
+        v = select(both, count, slice(2 * PAIR, 3 * PAIR)).astype(jnp.bfloat16)
+        qd_ref[:, cols] = q.astype(jnp.bfloat16)
         first_ref[:kept, cols] = k[:kept]
-        first_ref[kept : 2 * kept, cols] = select(both, count, slice(2 * PAIR, 3 * PAIR))[:kept].astype(jnp.bfloat16)
-        first_ref[2 * kept :, cols] = k[kept:]
-
-
-def order_kernel(sizes, off_ref, q_ref, k_ref, v_ref, qs_ref, own_ref, second_ref):
+        first_ref[kept:, cols] = v[:kept]
+        second_ref[:rest, cols] = k[kept:]
+        second_ref[rest:, cols] = v[kept:]
+
+
+def order_kernel(sizes, off_ref, q_ref, k_ref, v_ref, qs_ref, own_ref):
     kept, count = sizes.kept_pad, sizes.all_pad
     scale = HEAD_DIMENSION ** (-0.5)
     for pair in range(q_ref.shape[1] // PAIR):
@@ -118,9 +119,7 @@
         qs_ref[:, cols] = (select(both, count) * scale).astype(jnp.bfloat16)
         k = select(both, count, slice(PAIR, 2 * PAIR)).astype(jnp.bfloat16)
         v = select(both, count, slice(2 * PAIR, 3 * PAIR)).astype(jnp.bfloat16)
-        own = jnp.concatenate([k[:kept], v[:kept], k[kept:], v[kept:]], 0)
-        own_ref[:, cols] = own
-        second_ref[:, cols] = own[sizes.first :]
+        own_ref[:, cols] = jnp.concatenate([k[:kept], v[:kept], k[kept:], v[kept:]], 0)
 
 
 def rows_of(device, begin, count, cols):
@@ -152,13 +151,15 @@
     return dot(weights, with_ones(v))
 
 
-def sources(refs, parts):
-    found = [[(r, 0, r.shape[0])] for r in refs[:2]]
-    for n in range(2, len(refs), parts):
-        for core in range(2):
-            sizes = [(r, r.shape[0] // 2) for r in refs[n : n + parts]]
-            found.append([(r, core * size, size) for r, size in sizes])
-    return found
+def whole(ref):
+    return [(ref, 0, ref.shape[0])]
+
+
+def in_turn(sizes, ref):
+    far = (sizes.sub - 2) // 2
+    half = ref.shape[0] // 2
+    lots = [[(ref, core * half + n * sizes.first, sizes.first)] for n in range(2 * far + 1) for core in range(2)]
+    return lots[: 2 * far], lots[2 * far :]
 
 
 def join(devices, begin, count, cols):
@@ -166,26 +167,35 @@
 
 
 def collect_kernel(count, *refs):
-    for n, r in enumerate(refs[:count]):
-        refs[-1][n * r.shape[0] : (n + 1) * r.shape[0]] = r[...]
-
-
-def partial_kernel(sizes, others, q_ref, *refs):
-    out_refs = refs[-others:]
-    devices = sources(refs[:-others], 1)
+    inputs, outputs = refs[:-2], refs[-2:]
+    for found, out in zip((inputs[:count], inputs[count:]), outputs):
+        begin = 0
+        for r in found:
+            out[begin : begin + r.shape[0]] = r[...]
+            begin += r.shape[0]
+
+
+def partial_kernel(sizes, others, q_ref, visitor_ref, own_ref, core_ref, first_ref, *out_refs):
+    here, beside = in_turn(sizes, first_ref)
+    devices = [whole(own_ref), whole(core_ref)] + here + beside
     width = q_ref.shape[1]
     kept = sizes.kept_pad
-    rows = others * kept
+    rows = (others + 1) * kept
+    col = lax.broadcasted_iota(jnp.int32, (2 * rows, 2 * sizes.kept_keys), 1)
+    row = lax.broadcasted_iota(jnp.int32, (2 * rows, 2 * sizes.kept_keys), 0)
+    row = jnp.where(row < rows, row, row - rows)
+    known = jnp.where(row >= others * kept, 1, 0) * jnp.where(col < sizes.kept_keys, 1, 0)
+    hidden = jnp.where(known == 1, LOWEST, 0.0)
+    if sizes.padded:
+        hidden += hide(col, kept, sizes.kept)
     lane = lax.broadcasted_iota(jnp.int32, (rows, PAIR), 1)
     stats = jnp.zeros((rows, PAIR), jnp.float32)
     for pair in range(width // PAIR):
         cols = slice(pair * PAIR, (pair + 1) * PAIR)
-        q = q_ref[:, cols]
+        q = jnp.concatenate([visitor_ref[:, cols], q_ref[:kept, cols]], 0)
         k = jnp.concatenate(join(devices, 0, kept, cols), 0)
         v = jnp.concatenate(join(devices, kept, kept, cols), 0)
-        scores = dot_rows(both_heads(q), k)
-        if sizes.padded:
-            scores += hide(lax.broadcasted_iota(jnp.int32, (1, sizes.kept_keys), 1), kept, sizes.kept)
+        scores = dot_rows(both_heads(q), k) + hidden
         top = jnp.max(scores, 1, keepdims=True).astype(jnp.bfloat16).astype(jnp.float32)
         both = weigh(scores, top, v)
         lead, follow = both[:rows], both[rows:]
@@ -206,7 +216,11 @@
 
 def dense_kernel(sizes, *refs):
     off_ref, q_ref = refs[:2]
-    devices = sources(refs[2:-4], 2)
+    own_refs, first_ref, second_refs = refs[2:4], refs[4], refs[5:-4]
+    devices = [whole(r) for r in own_refs]
+    for n, d in enumerate(in_turn(sizes, first_ref)[0]):
+        r = second_refs[n // 2]
+        devices.append(d + [(r, n % 2 * sizes.second, sizes.second)])
     out_ref, total_ref, top_ref, back_ref = refs[-4:]
     width = q_ref.shape[1]
     kept, rest, rows = sizes.kept_pad, sizes.rest_pad, sizes.all_pad
@@ -312,11 +326,16 @@
         chips = [[n, n + 1] for n in range(0, sub, 2)]
         return [lax.all_gather(x, "sub", axis=0, tiled=True, axis_index_groups=chips) for x in lines]
 
-    masks = range(1, seq)
+    def swap_both(x, mask):
+        size = seq * sub
+        return lax.ppermute(x, ("seq", "sub"), [(n, n ^ sub ^ mask) for n in range(size)])
+
+    masks, far_masks = range(2, seq, 2), range(2, sub, 2)
     heads = width // HEAD_DIMENSION
-    q_kept, first, lanes = call(
+    q_kept, first, second, lanes = call(
         functools.partial(first_kernel, sizes),
-        [array(sizes.kept_pad), array(sizes.first), array(round_up(heads, 8), 128, jnp.int32)],
+        [array(n) for n in (sizes.kept_pad, sizes.first, sizes.second)]
+        + [array(round_up(heads, 8), 128, jnp.int32)],
         (offsets, queries, keys, values),
         COST[0],
         pltpu.HBM,
@@ -325,31 +344,31 @@
         + [pltpu.SemaphoreType.DMA((4,))],
         LIMIT,
     )
-    far_first = far(first)
+    lot = far(first) + [swap(first, "seq", 1)] + [swap_both(first, mask) for mask in far_masks]
     visitors = [swap(q_kept, "seq", mask) for mask in masks]
-    q, own, second = call(
+    far_second = far(second)
+    q, own = call(
         functools.partial(order_kernel, sizes),
-        [array(n) for n in (sizes.all_pad, 2 * sizes.all_pad, sizes.second)],
+        [array(n) for n in (sizes.all_pad, 2 * sizes.all_pad)],
         (offsets, queries, keys, values),
+        COST[1],
+    )
+    own = [own, swap(own, "sub", 1)]
+    lot, visitors = call(
+        functools.partial(collect_kernel, len(lot)),
+        [array(len(lot) * sizes.first), array(len(masks) * sizes.kept_pad)],
+        (*lot, *visitors),
+        COST[2],
+    )
+    (lot,) = both_cores([lot])
+    *parts, own_part = call(
+        functools.partial(partial_kernel, sizes, len(masks)),
+        [array(sizes.kept_pad, width + PAIR)] * (len(masks) + 1),
+        (q, visitors, *own, lot),
         COST[5],
     )
-    far_second = far(after(second, *far_first))
-    own = [own, swap(own, "sub", 1)]
-    far_first = both_cores(far_first)
-    visitors = call(
-        functools.partial(collect_kernel, len(masks)),
-        array(len(masks) * sizes.kept_pad),
-        (*visitors, *far_first),
-        COST[4],
-    )
-    parts = call(
-        functools.partial(partial_kernel, sizes, len(masks)),
-        [array(sizes.kept_pad, width + PAIR)] * len(masks),
-        (visitors, *own, *far_first),
-        COST[1],
-    )
     returned = [swap(part, "seq", mask) for mask, part in zip(masks, parts)]
-    far_second = both_cores([after(x, parts[0]) for x in far_second])
+    far_second = both_cores([after(x, *parts) for x in far_second])
     dense = call(
         functools.partial(dense_kernel, sizes),
         [
@@ -358,10 +377,10 @@
             array(sizes.kept_pad, dtype=jnp.float32),
             array(width // PAIR * 2 * rows, sizes.all_pad),
         ],
-        (lanes, q, *own, *(x for both in zip(far_first, far_second) for x in both)),
-        COST[2],
-    )
-    return call(functools.partial(merge_kernel, sizes), array(rows), (*dense, *returned), COST[3])
+        (lanes, q, *own, lot, *far_second),
+        COST[6],
+    )
+    return call(functools.partial(merge_kernel, sizes), array(rows), (*dense, *returned, own_part), COST[7])
 
 
 def solution(mesh):

time: 24.6 us -> 23.5 us (0.955)
  waiting for transfers between devices: 1.86 us -> 0.24 us
  starting transfers between devices: 11.4 us -> 11.8 us
    ppermute x0 -> x1, starting transfers between devices: none -> 4.02 us  [swap_both(): lax.ppermute(x, ('seq', 'sub'), [(n, n ^ sub ^ mask) for n in range(size)])]
    ppermute x9 -> x6, starting transfers between devices: 11.4 us -> 7.8 us  [swap(): lax.ppermute(x, axis, [(n, n ^ mask) for n in range(lax.axis_size(axis))])]
    ppermute x9 -> x6, waiting for transfers between devices: 1.86 us -> 0.24 us  [swap(): lax.ppermute(x, axis, [(n, n ^ mask) for n in range(lax.axis_size(axis))])]
  transfers between devices with their start and end apart: 9 -> 7, of which waited for: 4 -> 1; matrix products, arithmetic and copies ran while one was open for 0% -> 0% of each run, Pallas kernels for 14% -> 13%
where the time goes in v3:
time: 23.5 us; the launch traced here: 23.3 us
  starting transfers between devices  11.8 us (50%)
  Pallas kernels  6.73 us (29%)
  blocking collectives  4.44 us (19%)
  waiting for transfers between devices  0.24 us (1%)
    ppermute x6, starting transfers between devices, swap(): lax.ppermute(x, axis, [(n, n ^ mask) for n in range(lax.axis_size(axis))])  7.8 us
    pallas_call x6, Pallas kernels, call(): pl.pallas_call(kernel, out_shape=out_shape, in_specs=in_specs, out_specs=...  6.73 us
    all_gather x2, blocking collectives, both_cores(): lax.all_gather(x, 'sub', axis=0, tiled=True, axis_index_groups=chips)  4.44 us
    ppermute x1, starting transfers between devices, swap_both(): lax.ppermute(x, ('seq', 'sub'), [(n, n ^ sub ^ mask) for n in range(size)])  4.02 us
  transfers between devices with their start and end apart: 7, of which 1 were waited for; matrix products, arithmetic and copies ran while one was open for 0% of the time, Pallas kernels for 13%

profile of v3, /device:TPU:0, one launch (start us, length us, event | category | flops | bytes accessed | tf_op | source)
XLA Modules:
  0.0 23.3 jit_solution(17404426099853369416)
XLA Ops:
  0.0 0.0 copy-start.2
  0.0 0.0 copy-start.1
  0.0 0.0 copy-start
  0.0 2.4 %shard_map.46 = (bf16[32,768]{1,0:T(8,128)(2,1)}, bf16[64,768]{1,0:T(8,128)(2,1)}, bf16[192,768]{1,0:T(8,128)(2,1)}, s32[16,128]{1,0:T(8,128)}) custom-call(s32[12]{0:T(128)} %off_ref.1, bf16[128,768]{1,0:T(8,128)(2,1)} %q_ref.1, bf16[128,768]{1,0:T(8,128)(2,1)} %k_ref.1, bf16[128,768]{1,0:T(8,128)(2,1)} %v_ref.1), custom_call_target="tpu_custom_call" | custom-call | flops 1000000 | bytes 589848 | tf_op jit(solution)/shard_map/pallas_call | solution.py:297
  2.4 4.0 %collective-permute-start.3 = (bf16[64,768]{1,0:T(8,128)(2,1)}, bf16[64,768]{1,0:T(8,128)(2,1)S(1)}, u32[]{:S(2)}, u32[]{:S(2)}) collective-permute-start(bf16[64,768]{1,0:T(8,128)(2,1)} %get-tuple-element.23), channel_id=1, source_target_pairs={{0,6},{1,7},{2,4},{3,5},{4,2},{5,3},{6,0},{7,1},{8,14},{9,15},{10,... | collective-permute-start | bytes 294920 | tf_op jit(solution)/shard_map/ppermute | solution.py:331
  6.4 0.5 %collective-permute-start.2 = (bf16[64,768]{1,0:T(8,128)(2,1)}, bf16[64,768]{1,0:T(8,128)(2,1)S(1)}, u32[]{:S(2)}, u32[]{:S(2)}) collective-permute-start(bf16[64,768]{1,0:T(8,128)(2,1)} %get-tuple-element.23), channel_id=1, source_target_pairs={{0,4},{4,0},{8,12},{12,8},{1,5},{5,1},{9,13},{13,9},{2,6},{6,2},{1... | collective-permute-start | bytes 294920 | tf_op jit(solution)/shard_map/ppermute | solution.py:317
  6.9 0.2 collective-permute-start.1
  7.1 0.0 copy-start.4
  7.1 2.9 %collective-permute-start.4 = (bf16[32,768]{1,0:T(8,128)(2,1)}, bf16[32,768]{1,0:T(8,128)(2,1)S(1)}, u32[]{:S(2)}, u32[]{:S(2)}) collective-permute-start(bf16[32,768]{1,0:T(8,128)(2,1)} %get-tuple-element.24), channel_id=1, source_target_pairs={{0,8},{4,12},{8,0},{12,4},{1,9},{5,13},{9,1},{13,5},{2,10},{6,14},... | collective-permute-start | bytes 147464 | tf_op jit(solution)/shard_map/ppermute | solution.py:317
  10.0 1.5 %collective-permute-start.5 = (bf16[192,768]{1,0:T(8,128)(2,1)}, bf16[192,768]{1,0:T(8,128)(2,1)S(1)}, u32[]{:S(2)}, u32[]{:S(2)}) collective-permute-start(bf16[192,768]{1,0:T(8,128)(2,1)} %get-tuple-element.26), channel_id=1, source_target_pairs={{0,2},{1,3},{2,0},{3,1},{4,6},{5,7},{6,4},{7,5},{8,10},{9,11},{10,... | collective-permute-start | bytes 884744 | tf_op jit(solution)/shard_map/ppermute | solution.py:317
  11.5 0.0 copy-done.2
  11.5 0.0 copy-done.1
  11.5 0.0 copy-done
  11.5 0.0 copy-done.4
  11.5 1.0 %shard_map.47 = (bf16[128,768]{1,0:T(8,128)(2,1)S(1)}, bf16[256,768]{1,0:T(8,128)(2,1)S(1)}) custom-call(s32[12]{0:T(128)S(1)} %copy-done.4, bf16[128,768]{1,0:T(8,128)(2,1)S(1)} %copy-done, bf16[128,768]{1,0:T(8,128)(2,1)S(1)} %copy-done.1, bf16[128,768]{1,0:T(8,128)(2,1)S(1)} %copy-done.2), custom_call_target="tpu_custom_call" | custom-call | flops 1000000 | bytes 589848 | tf_op jit(solution)/shard_map/pallas_call | solution.py:297
  12.5 0.0 collective-permute-done.4.refs_3_
  12.5 0.1 collective-permute-start
  12.6 0.0 collective-permute-done.3.refs_2_
  12.6 0.2 collective-permute-done.2.refs_1_
  12.9 0.0 collective-permute-done.1.refs_0_
  12.9 2.2 %all_gather.6.first_ref.refs_4_ = bf16[384,768]{1,0:T(8,128)(2,1)S(1)} all-gather(bf16[192,768]{1,0:T(8,128)(2,1)S(1)} %get-tuple-element.25), channel_id=1, replica_groups={{0,1},{2,3},{4,5},{6,7},{8,9},{10,11},{12,13},{14,15},{16,17},{18,19},{..., dimensions={0}, use_global_device_ids=true | all-gather | bytes 884736 | tf_op jit(solution)/shard_map/all_gather | solution.py:327
  15.1 0.0 collective-permute-done.core_ref.refs_3_
  15.1 0.6 %shard_map.49 = (bf16[32,896]{1,0:T(8,128)(2,1)S(1)}, bf16[32,896]{1,0:T(8,128)(2,1)S(1)}) custom-call(bf16[128,768]{1,0:T(8,128)(2,1)S(1)} %get-tuple-element.21.q_ref.refs_1_, bf16[32,768]{1,0:T(8,128)(2,1)S(1)} %get-tuple-element.27.visitor_ref, bf16[256,768]{1,0:T(8,128)(2,1)S(1)} %get-tuple-element.22.own_ref.refs_2_, ...), custom_call_target="tpu_custom_call" | custom-call | flops 1000000 | bytes 1622016 | tf_op jit(solution)/shard_map/pallas_call | solution.py:297
  15.7 0.0 copy-start.3
  15.7 2.7 %collective-permute-start.6 = (bf16[32,896]{1,0:T(8,128)(2,1)S(1)}, bf16[32,896]{1,0:T(8,128)(2,1)S(1)}, u32[]{:S(2)}, u32[]{:S(2)}) collective-permute-start(bf16[32,896]{1,0:T(8,128)(2,1)S(1)} %get-tuple-element.28), channel_id=1, source_target_pairs={{0,8},{4,12},{8,0},{12,4},{1,9},{5,13},{9,1},{13,5},{2,10},{6,14},... | collective-permute-start | bytes 172040 | tf_op jit(solution)/shard_map/ppermute | solution.py:317
  18.4 0.0 collective-permute-done.5
  18.4 2.2 %all_gather.7.refs_5_ = bf16[384,768]{1,0:T(8,128)(2,1)S(1)} all-gather(bf16[192,768]{1,0:T(8,128)(2,1)S(1)} %collective-permute-done.5), channel_id=1, replica_groups={{0,1},{2,3},{4,5},{6,7},{8,9},{10,11},{12,13},{14,15},{16,17},{18,19},{..., dimensions={0}, use_global_device_ids=true | all-gather | bytes 884736 | tf_op jit(solution)/shard_map/all_gather | solution.py:327
  20.6 0.0 copy-done.3
  20.6 1.5 %shard_map.50 = (f32[128,768]{1,0:T(8,128)S(1)}, f32[128,768]{1,0:T(8,128)S(1)}, f32[32,768]{1,0:T(8,128)S(1)}, bf16[1536,128]{1,0:T(8,128)(2,1)S(1)}) custom-call(s32[16,128]{1,0:T(8,128)S(1)} %copy-done.3, bf16[128,768]{1,0:T(8,128)(2,1)S(1)} %get-tuple-element.21.q_ref.refs_1_, bf16[256,768]{1,0:T(8,128)(2,1)S(1)} %get-tuple-element.22.own_ref.refs_2_, ...), custom_call_target="tpu_custom_call" | custom-call | flops 1000000 | bytes 2166784 | tf_op jit(solution)/shard_map/pallas_call | solution.py:297
  22.1 0.0 collective-permute-done.6.refs_4_
  22.2 1.2 %shard_map.51 = bf16[128,768]{1,0:T(8,128)(2,1)} custom-call(f32[128,768]{1,0:T(8,128)S(1)} %get-tuple-element.30.refs_0_, f32[128,768]{1,0:T(8,128)S(1)} %get-tuple-element.31.refs_1_, f32[32,768]{1,0:T(8,128)S(1)} %get-tuple-element.32.refs_2_, bf16[1536,128]{1,0:T(8,128)(2,1)S(1)} %get-tuple-element.33.refs_3_, ...), custom_call_target="tpu_custom_call" | custom-call | flops 1000000 | bytes 950272 | tf_op jit(solution)/shard_map/pallas_call | solution.py:297
  (1 shorter events, 0.0 us)
Async XLA Ops:
  0.0 11.5 %copy-start.2 = (bf16[128,768]{1,0:T(8,128)(2,1)S(1)}, bf16[128,768]{1,0:T(8,128)(2,1)}, u32[]{:S(2)}) copy-start(bf16[128,768]{1,0:T(8,128)(2,1)} %v_ref.1) | copy-start | bytes 589828
  0.0 11.5 %copy-start.1 = (bf16[128,768]{1,0:T(8,128)(2,1)S(1)}, bf16[128,768]{1,0:T(8,128)(2,1)}, u32[]{:S(2)}) copy-start(bf16[128,768]{1,0:T(8,128)(2,1)} %k_ref.1) | copy-start | bytes 589828
  0.0 11.5 %copy-start = (bf16[128,768]{1,0:T(8,128)(2,1)S(1)}, bf16[128,768]{1,0:T(8,128)(2,1)}, u32[]{:S(2)}) copy-start(bf16[128,768]{1,0:T(8,128)(2,1)} %q_ref.1) | copy-start | bytes 589828
  2.4 10.2 %collective-permute-start.3 = (bf16[64,768]{1,0:T(8,128)(2,1)}, bf16[64,768]{1,0:T(8,128)(2,1)S(1)}, u32[]{:S(2)}, u32[]{:S(2)}) collective-permute-start(bf16[64,768]{1,0:T(8,128)(2,1)} %get-tuple-element.23), channel_id=1, source_target_pairs={{0,6},{1,7},{2,4},{3,5},{4,2},{5,3},{6,0},{7,1},{8,14},{9,15},{10,... | collective-permute-start | bytes 294920 | tf_op jit(solution)/shard_map/ppermute | solution.py:331
  6.4 6.4 %collective-permute-start.2 = (bf16[64,768]{1,0:T(8,128)(2,1)}, bf16[64,768]{1,0:T(8,128)(2,1)S(1)}, u32[]{:S(2)}, u32[]{:S(2)}) collective-permute-start(bf16[64,768]{1,0:T(8,128)(2,1)} %get-tuple-element.23), channel_id=1, source_target_pairs={{0,4},{4,0},{8,12},{12,8},{1,5},{5,1},{9,13},{13,9},{2,6},{6,2},{1... | collective-permute-start | bytes 294920 | tf_op jit(solution)/shard_map/ppermute | solution.py:317
  6.9 6.0 %collective-permute-start.1 = (bf16[64,768]{1,0:T(8,128)(2,1)}, bf16[64,768]{1,0:T(8,128)(2,1)S(1)}, u32[]{:S(2)}, u32[]{:S(2)}) collective-permute-start(bf16[64,768]{1,0:T(8,128)(2,1)} %get-tuple-element.23), channel_id=1, source_target_pairs={{0,2},{1,3},{2,0},{3,1},{4,6},{5,7},{6,4},{7,5},{8,10},{9,11},{10,... | collective-permute-start | bytes 294920 | tf_op jit(solution)/shard_map/ppermute | solution.py:317
  7.1 4.4 %copy-start.4 = (s32[12]{0:T(128)S(1)}, s32[12]{0:T(128)}, u32[]{:S(2)}) copy-start(s32[12]{0:T(128)} %off_ref.1) | copy-start | bytes 148
  7.1 5.4 %collective-permute-start.4 = (bf16[32,768]{1,0:T(8,128)(2,1)}, bf16[32,768]{1,0:T(8,128)(2,1)S(1)}, u32[]{:S(2)}, u32[]{:S(2)}) collective-permute-start(bf16[32,768]{1,0:T(8,128)(2,1)} %get-tuple-element.24), channel_id=1, source_target_pairs={{0,8},{4,12},{8,0},{12,4},{1,9},{5,13},{9,1},{13,5},{2,10},{6,14},... | collective-permute-start | bytes 147464 | tf_op jit(solution)/shard_map/ppermute | solution.py:317
  10.0 8.4 %collective-permute-start.5 = (bf16[192,768]{1,0:T(8,128)(2,1)}, bf16[192,768]{1,0:T(8,128)(2,1)S(1)}, u32[]{:S(2)}, u32[]{:S(2)}) collective-permute-start(bf16[192,768]{1,0:T(8,128)(2,1)} %get-tuple-element.26), channel_id=1, source_target_pairs={{0,2},{1,3},{2,0},{3,1},{4,6},{5,7},{6,4},{7,5},{8,10},{9,11},{10,... | collective-permute-start | bytes 884744 | tf_op jit(solution)/shard_map/ppermute | solution.py:317
  12.5 2.6 %collective-permute-start = (bf16[256,768]{1,0:T(8,128)(2,1)S(1)}, bf16[256,768]{1,0:T(8,128)(2,1)S(1)}, u32[]{:S(2)}, u32[]{:S(2)}) collective-permute-start(bf16[256,768]{1,0:T(8,128)(2,1)S(1)} %get-tuple-element.22.own_ref.refs_2_), channel_id=1, source_target_pairs={{0,1},{1,0},{2,3},{3,2},{4,5},{5,4},{6,7},{7,6},{8,9},{9,8},{10,11... | collective-permute-start | bytes 1179656 | tf_op jit(solution)/shard_map/ppermute | solution.py:317
  15.7 4.9 %copy-start.3 = (s32[16,128]{1,0:T(8,128)S(1)}, s32[16,128]{1,0:T(8,128)}, u32[]{:S(2)}) copy-start(s32[16,128]{1,0:T(8,128)} %get-tuple-element.20.refs_0_) | copy-start | bytes 24580
  15.7 6.4 %collective-permute-start.6 = (bf16[32,896]{1,0:T(8,128)(2,1)S(1)}, bf16[32,896]{1,0:T(8,128)(2,1)S(1)}, u32[]{:S(2)}, u32[]{:S(2)}) collective-permute-start(bf16[32,896]{1,0:T(8,128)(2,1)S(1)} %get-tuple-element.28), channel_id=1, source_target_pairs={{0,8},{4,12},{8,0},{12,4},{1,9},{5,13},{9,1},{13,5},{2,10},{6,14},... | collective-permute-start | bytes 172040 | tf_op jit(solution)/shard_map/ppermute | solution.py:317

commit v4 on v3

--- a/solution.py
+++ b/solution.py
@@ -112,10 +112,13 @@
 def order_kernel(sizes, off_ref, q_ref, k_ref, v_ref, qs_ref, own_ref):
     kept, count = sizes.kept_pad, sizes.all_pad
     scale = HEAD_DIMENSION ** (-0.5)
+    found = []
     for pair in range(q_ref.shape[1] // PAIR):
         cols = slice(pair * PAIR, (pair + 1) * PAIR)
         chosen = order_rows_of_pair(sizes, lambda head: off_ref[head], pair, count)
-        both = dot(chosen, jnp.concatenate([q_ref[:, cols], k_ref[:, cols], v_ref[:, cols]], 1))
+        found.append(dot(chosen, jnp.concatenate([q_ref[:, cols], k_ref[:, cols], v_ref[:, cols]], 1)))
+    for pair, both in enumerate(found):
+        cols = slice(pair * PAIR, (pair + 1) * PAIR)
         qs_ref[:, cols] = (select(both, count) * scale).astype(jnp.bfloat16)
         k = select(both, count, slice(PAIR, 2 * PAIR)).astype(jnp.bfloat16)
         v = select(both, count, slice(2 * PAIR, 3 * PAIR)).astype(jnp.bfloat16)
@@ -155,11 +158,9 @@
     return [(ref, 0, ref.shape[0])]
 
 
-def in_turn(sizes, ref):
-    far = (sizes.sub - 2) // 2
-    half = ref.shape[0] // 2
-    lots = [[(ref, core * half + n * sizes.first, sizes.first)] for n in range(2 * far + 1) for core in range(2)]
-    return lots[: 2 * far], lots[2 * far :]
+def in_turn(sizes, refs):
+    found = [[(r, 0, sizes.first)] for r in refs]
+    return found[: sizes.sub - 2], found[sizes.sub - 2 :]
 
 
 def join(devices, begin, count, cols):
@@ -167,16 +168,15 @@
 
 
 def collect_kernel(count, *refs):
-    inputs, outputs = refs[:-2], refs[-2:]
-    for found, out in zip((inputs[:count], inputs[count:]), outputs):
-        begin = 0
-        for r in found:
-            out[begin : begin + r.shape[0]] = r[...]
-            begin += r.shape[0]
-
-
-def partial_kernel(sizes, others, q_ref, visitor_ref, own_ref, core_ref, first_ref, *out_refs):
-    here, beside = in_turn(sizes, first_ref)
+    begin = 0
+    for r in refs[:count]:
+        refs[-1][begin : begin + r.shape[0]] = r[...]
+        begin += r.shape[0]
+
+
+def partial_kernel(sizes, others, q_ref, visitor_ref, own_ref, core_ref, *refs):
+    first_refs, out_refs = refs[: -others - 1], refs[-others - 1 :]
+    here, beside = in_turn(sizes, first_refs)
     devices = [whole(own_ref), whole(core_ref)] + here + beside
     width = q_ref.shape[1]
     kept = sizes.kept_pad
@@ -216,15 +216,16 @@
 
 def dense_kernel(sizes, *refs):
     off_ref, q_ref = refs[:2]
-    own_refs, first_ref, second_refs = refs[2:4], refs[4], refs[5:-4]
+    own_refs, first_refs, second_refs = refs[2:4], refs[4 : 2 + sizes.sub], refs[2 + sizes.sub : -5]
     devices = [whole(r) for r in own_refs]
-    for n, d in enumerate(in_turn(sizes, first_ref)[0]):
+    for n, d in enumerate(in_turn(sizes, first_refs)[0]):
         r = second_refs[n // 2]
         devices.append(d + [(r, n % 2 * sizes.second, sizes.second)])
-    out_ref, total_ref, top_ref, back_ref = refs[-4:]
+    base_ref, out_ref, total_ref, top_ref, back_ref = refs[-5:]
     width = q_ref.shape[1]
     kept, rest, rows = sizes.kept_pad, sizes.rest_pad, sizes.all_pad
     begin = sizes.kept_keys
+    results = []
     for pair in range(width // PAIR):
         cols = slice(pair * PAIR, (pair + 1) * PAIR)
         k = jnp.concatenate(join(devices, 0, kept, cols) + join(devices, 2 * kept, rest, cols), 0)
@@ -243,12 +244,24 @@
         )
         weights = jnp.concatenate([near, far], 1).astype(jnp.bfloat16)
         both = dot(weights, with_ones(v))
-        out_ref[:, cols] = select(both, rows)
-        total_ref[:, cols] = select(both, rows, slice(PAIR, 2 * PAIR))
+        out, total = select(both, rows), select(both, rows, slice(PAIR, 2 * PAIR))
+        out_ref[:, cols], total_ref[:, cols] = out[:kept], total[:kept]
         top_ref[:, cols] = jnp.where(first_head((kept, PAIR)), top[:kept], top[rows : rows + kept])
-        for n in range(2):
-            place = 2 * pair + n
-            back_ref[place * sizes.rows : (place + 1) * sizes.rows] = restore_rows(sizes, off_ref[place : place + 1, 0:1])
+        results.append((out[kept:] / total[kept:]).astype(jnp.bfloat16))
+    for pair, result in enumerate(results):
+        cols = slice(pair * PAIR, (pair + 1) * PAIR)
+        back = [restore_rows(sizes, off_ref[2 * pair + n : 2 * pair + n + 1, 0:1]) for n in range(2)]
+        back = jnp.concatenate(back, 0)
+        back_ref[2 * sizes.rows * pair : 2 * sizes.rows * (pair + 1)] = back[:, :kept]
+        whole_rows = jnp.concatenate([jnp.zeros((kept, PAIR), jnp.bfloat16), result], 0)
+        base_ref[:, cols] = select(dot(back, whole_rows), sizes.rows).astype(jnp.bfloat16)
+
+
+def dense_shapes(sizes, width):
+    shapes = [(sizes.rows, width, jnp.bfloat16)]
+    shapes += [(sizes.kept_pad, width, jnp.float32)] * 3
+    shapes += [(width // PAIR * 2 * sizes.rows, sizes.kept_pad, jnp.bfloat16)]
+    return [jax.ShapeDtypeStruct(s[:2], s[2]) for s in shapes]
 
 
 def spread(width, lanes):
@@ -259,33 +272,28 @@
 
 
 def merge_kernel(sizes, *refs):
-    out_ref, total_ref, top_ref, back_ref = refs[:4]
-    part_refs, done_ref = refs[4:-1], refs[-1]
+    base_ref, out_ref, total_ref, top_ref, back_ref = refs[:5]
+    part_refs, done_ref = refs[5:-1], refs[-1]
     others = len(part_refs)
     width = out_ref.shape[1]
     kept = sizes.kept_pad
     stats = jnp.concatenate([r[:, width:] for r in part_refs], 0)
     tops = dot(stats, spread(width, (0,)))
     totals = dot(stats, spread(width, (1, 2)))
-    results = []
+    theirs = [tops[n * kept : (n + 1) * kept] for n in range(others)]
+    top = top_ref[...]
+    best = functools.reduce(jnp.maximum, theirs, top)
+    factor = jnp.exp(top - best)
+    out, total = out_ref[...] * factor, total_ref[...] * factor
+    for n, r in enumerate(part_refs):
+        factor = jnp.exp(theirs[n] - best)
+        out += r[:, :width].astype(jnp.float32) * factor
+        total += totals[n * kept : (n + 1) * kept] * factor
+    result = (out / total).astype(jnp.bfloat16)
     for pair in range(width // PAIR):
         cols = slice(pair * PAIR, (pair + 1) * PAIR)
-        out, total = out_ref[:, cols], total_ref[:, cols]
-        top = top_ref[:, cols]
-        theirs = [tops[n * kept : (n + 1) * kept, cols] for n in range(others)]
-        best = functools.reduce(jnp.maximum, theirs, top)
-        factor = jnp.exp(top - best)
-        kept_out, kept_total = out[:kept] * factor, total[:kept] * factor
-        for n, r in enumerate(part_refs):
-            factor = jnp.exp(theirs[n] - best)
-            kept_out += r[:, cols].astype(jnp.float32) * factor
-            kept_total += totals[n * kept : (n + 1) * kept, cols] * factor
-        result = jnp.concatenate([kept_out / kept_total, out[kept:] / total[kept:]], 0)
-        results.append(result.astype(jnp.bfloat16))
-    for pair, result in enumerate(results):
-        cols = slice(pair * PAIR, (pair + 1) * PAIR)
-        back = dot(back_ref[2 * sizes.rows * pair : 2 * sizes.rows * (pair + 1)], result)
-        done_ref[:, cols] = select(back, sizes.rows).astype(jnp.bfloat16)
+        back = dot(back_ref[2 * sizes.rows * pair : 2 * sizes.rows * (pair + 1)], result[:, cols])
+        done_ref[:, cols] = (select(back, sizes.rows) + base_ref[:, cols].astype(jnp.float32)).astype(jnp.bfloat16)
 
 
 def call(kernel, out_shape, operands, flops, place=pltpu.VMEM, scratch=(), limit=24):
@@ -301,7 +309,7 @@
         out_specs=out_specs,
         scratch_shapes=scratch,
         cost_estimate=pl.CostEstimate(flops=flops, bytes_accessed=size, transcendentals=0),
-        compiler_params=pltpu.CompilerParams(vmem_limit_bytes=limit * 1024 * 1024),
+        compiler_params=pltpu.CompilerParams(vmem_limit_bytes=int(limit * 1024 * 1024)),
     )(*operands)
 
 
@@ -354,30 +362,25 @@
         COST[1],
     )
     own = [own, swap(own, "sub", 1)]
-    lot, visitors = call(
-        functools.partial(collect_kernel, len(lot)),
-        [array(len(lot) * sizes.first), array(len(masks) * sizes.kept_pad)],
-        (*lot, *visitors),
+    visitors = call(
+        functools.partial(collect_kernel, len(masks)),
+        array(len(masks) * sizes.kept_pad),
+        (*visitors, *lot),
         COST[2],
     )
-    (lot,) = both_cores([lot])
+    lot = [y for x in lot for y in (x, swap(after(x, visitors), "sub", 1))]
     *parts, own_part = call(
         functools.partial(partial_kernel, sizes, len(masks)),
         [array(sizes.kept_pad, width + PAIR)] * (len(masks) + 1),
-        (q, visitors, *own, lot),
+        (q, visitors, *own, *lot),
         COST[5],
     )
     returned = [swap(part, "seq", mask) for mask, part in zip(masks, parts)]
     far_second = both_cores([after(x, *parts) for x in far_second])
     dense = call(
         functools.partial(dense_kernel, sizes),
-        [
-            array(sizes.all_pad, dtype=jnp.float32),
-            array(sizes.all_pad, dtype=jnp.float32),
-            array(sizes.kept_pad, dtype=jnp.float32),
-            array(width // PAIR * 2 * rows, sizes.all_pad),
-        ],
-        (lanes, q, *own, lot, *far_second),
+        dense_shapes(sizes, width),
+        (lanes, q, *own, *lot[: sub - 2], *far_second),
         COST[6],
     )
     return call(functools.partial(merge_kernel, sizes), array(rows), (*dense, *returned, own_part), COST[7])

time: 23.5 us -> 23.1 us (0.983)
  blocking collectives: 4.44 us -> 2.22 us
  waiting for transfers between devices: 0.24 us -> 1.27 us
  starting transfers between devices: 11.8 us -> 12.8 us
    all_gather x2 -> x1, blocking collectives: 4.44 us -> 2.22 us  [both_cores(): lax.all_gather(x, 'sub', axis=0, tiled=True, axis_index_groups=chips)]
    ppermute x6 -> x9, waiting for transfers between devices: 0.24 us -> 1.27 us  [swap(): lax.ppermute(x, axis, [(n, n ^ mask) for n in range(lax.axis_size(axis))])]
    ppermute x6 -> x9, starting transfers between devices: 7.8 us -> 8.74 us  [swap(): lax.ppermute(x, axis, [(n, n ^ mask) for n in range(lax.axis_size(axis))])]
  transfers between devices with their start and end apart: 7 -> 10, of which waited for: 1 -> 4; matrix products, arithmetic and copies ran while one was open for 0% -> 0% of each run, Pallas kernels for 13% -> 14%
where the time goes in v4:
time: 23.1 us; the launch traced here: 23 us
  starting transfers between devices  12.8 us (55%)
  Pallas kernels  6.65 us (29%)
  blocking collectives  2.22 us (10%)
  waiting for transfers between devices  1.27 us (5%)
    ppermute x9, starting transfers between devices, swap(): lax.ppermute(x, axis, [(n, n ^ mask) for n in range(lax.axis_size(axis))])  8.74 us
    pallas_call x6, Pallas kernels, call(): pl.pallas_call(kernel, out_shape=out_shape, in_specs=in_specs, out_specs=...  6.65 us
    ppermute x1, starting transfers between devices, swap_both(): lax.ppermute(x, ('seq', 'sub'), [(n, n ^ sub ^ mask) for n in range(size)])  4.02 us
    all_gather x1, blocking collectives, both_cores(): lax.all_gather(x, 'sub', axis=0, tiled=True, axis_index_groups=chips)  2.22 us
    ppermute x9, waiting for transfers between devices, swap(): lax.ppermute(x, axis, [(n, n ^ mask) for n in range(lax.axis_size(axis))])  1.27 us
  transfers between devices with their start and end apart: 10, of which 4 were waited for; matrix products, arithmetic and copies ran while one was open for 0% of the time, Pallas kernels for 14%

profile of v4, /device:TPU:0, one launch (start us, length us, event | category | flops | bytes accessed | tf_op | source)
XLA Modules:
  0.0 23.0 jit_solution(3232528351478902420)
XLA Ops:
  0.0 2.4 %shard_map.46 = (bf16[32,768]{1,0:T(8,128)(2,1)}, bf16[64,768]{1,0:T(8,128)(2,1)}, bf16[192,768]{1,0:T(8,128)(2,1)}, s32[16,128]{1,0:T(8,128)}) custom-call(s32[12]{0:T(128)} %off_ref.1, bf16[128,768]{1,0:T(8,128)(2,1)} %q_ref.1, bf16[128,768]{1,0:T(8,128)(2,1)} %k_ref.1, bf16[128,768]{1,0:T(8,128)(2,1)} %v_ref.1), custom_call_target="tpu_custom_call" | custom-call | flops 1000000 | bytes 589848 | tf_op jit(solution)/shard_map/pallas_call | solution.py:305
  2.4 4.0 %collective-permute-start.4 = (bf16[64,768]{1,0:T(8,128)(2,1)}, bf16[64,768]{1,0:T(8,128)(2,1)S(1)}, u32[]{:S(2)}, u32[]{:S(2)}) collective-permute-start(bf16[64,768]{1,0:T(8,128)(2,1)} %get-tuple-element.25), channel_id=1, source_target_pairs={{0,6},{1,7},{2,4},{3,5},{4,2},{5,3},{6,0},{7,1},{8,14},{9,15},{10,... | collective-permute-start | bytes 294920 | tf_op jit(solution)/shard_map/ppermute | solution.py:339
  6.4 0.5 %collective-permute-start.3 = (bf16[64,768]{1,0:T(8,128)(2,1)}, bf16[64,768]{1,0:T(8,128)(2,1)S(1)}, u32[]{:S(2)}, u32[]{:S(2)}) collective-permute-start(bf16[64,768]{1,0:T(8,128)(2,1)} %get-tuple-element.25), channel_id=1, source_target_pairs={{0,4},{4,0},{8,12},{12,8},{1,5},{5,1},{9,13},{13,9},{2,6},{6,2},{1... | collective-permute-start | bytes 294920 | tf_op jit(solution)/shard_map/ppermute | solution.py:325
  6.9 0.2 collective-permute-start.1
  7.1 2.9 %collective-permute-start.2 = (bf16[32,768]{1,0:T(8,128)(2,1)}, bf16[32,768]{1,0:T(8,128)(2,1)S(1)}, u32[]{:S(2)}, u32[]{:S(2)}) collective-permute-start(bf16[32,768]{1,0:T(8,128)(2,1)} %get-tuple-element.26), channel_id=1, source_target_pairs={{0,8},{4,12},{8,0},{12,4},{1,9},{5,13},{9,1},{13,5},{2,10},{6,14},... | collective-permute-start | bytes 147464 | tf_op jit(solution)/shard_map/ppermute | solution.py:325
  10.0 1.5 %collective-permute-start.6 = (bf16[192,768]{1,0:T(8,128)(2,1)}, bf16[192,768]{1,0:T(8,128)(2,1)S(1)}, u32[]{:S(2)}, u32[]{:S(2)}) collective-permute-start(bf16[192,768]{1,0:T(8,128)(2,1)} %get-tuple-element.28), channel_id=1, source_target_pairs={{0,2},{1,3},{2,0},{3,1},{4,6},{5,7},{6,4},{7,5},{8,10},{9,11},{10,... | collective-permute-start | bytes 884744 | tf_op jit(solution)/shard_map/ppermute | solution.py:325
  11.5 0.0 copy-done.2
  11.5 0.0 copy-done.1
  11.5 0.0 copy-done
  11.5 0.0 copy-done.4
  11.5 1.0 %shard_map.47 = (bf16[128,768]{1,0:T(8,128)(2,1)S(1)}, bf16[256,768]{1,0:T(8,128)(2,1)S(1)}) custom-call(s32[12]{0:T(128)S(1)} %copy-done.4, bf16[128,768]{1,0:T(8,128)(2,1)S(1)} %copy-done, bf16[128,768]{1,0:T(8,128)(2,1)S(1)} %copy-done.1, bf16[128,768]{1,0:T(8,128)(2,1)S(1)} %copy-done.2), custom_call_target="tpu_custom_call" | custom-call | flops 1000000 | bytes 589848 | tf_op jit(solution)/shard_map/pallas_call | solution.py:305
  12.5 0.0 collective-permute-done.2.refs_0_
  12.5 0.1 collective-permute-start
  12.6 0.0 collective-permute-done.4.refs_3_.refs_4_
  12.6 0.2 collective-permute-done.3.refs_2_
  12.9 0.0 collective-permute-done.1.refs_1_.refs_0_.refs_4_
  12.9 0.3 %collective-permute-start.5 = (bf16[64,768]{1,0:T(8,128)(2,1)S(1)}, bf16[64,768]{1,0:T(8,128)(2,1)S(1)}, u32[]{:S(2)}, u32[]{:S(2)}) collective-permute-start(bf16[64,768]{1,0:T(8,128)(2,1)S(1)} %collective-permute-done.1.refs_1_.refs_0_.refs_4_), channel_id=1, source_target_pairs={{0,1},{1,0},{2,3},{3,2},{4,5},{5,4},{6,7},{7,6},{8,9},{9,8},{10,11... | collective-permute-start | bytes 294920 | tf_op jit(solution)/shard_map/ppermute | solution.py:325
  13.2 0.2 %collective-permute-start.7 = (bf16[64,768]{1,0:T(8,128)(2,1)S(1)}, bf16[64,768]{1,0:T(8,128)(2,1)S(1)}, u32[]{:S(2)}, u32[]{:S(2)}) collective-permute-start(bf16[64,768]{1,0:T(8,128)(2,1)S(1)} %collective-permute-done.3.refs_2_), channel_id=1, source_target_pairs={{0,1},{1,0},{2,3},{3,2},{4,5},{5,4},{6,7},{7,6},{8,9},{9,8},{10,11... | collective-permute-start | bytes 294920 | tf_op jit(solution)/shard_map/ppermute | solution.py:325
  13.4 0.3 %collective-permute-start.8 = (bf16[64,768]{1,0:T(8,128)(2,1)S(1)}, bf16[64,768]{1,0:T(8,128)(2,1)S(1)}, u32[]{:S(2)}, u32[]{:S(2)}) collective-permute-start(bf16[64,768]{1,0:T(8,128)(2,1)S(1)} %collective-permute-done.4.refs_3_.refs_4_), channel_id=1, source_target_pairs={{0,1},{1,0},{2,3},{3,2},{4,5},{5,4},{6,7},{7,6},{8,9},{9,8},{10,11... | collective-permute-start | bytes 294920 | tf_op jit(solution)/shard_map/ppermute | solution.py:325
  13.7 0.8 %collective-permute-done.5.refs_1_.refs_5_ = bf16[64,768]{1,0:T(8,128)(2,1)S(1)} collective-permute-done((bf16[64,768]{1,0:T(8,128)(2,1)S(1)}, bf16[64,768]{1,0:T(8,128)(2,1)S(1)}, u32[]{:S(2)}, u32[]{:S(2)}) %collective-permute-start.5) | collective-permute-done | bytes 98336 | tf_op jit(solution)/shard_map/ppermute | solution.py:325
  14.5 0.1 collective-permute-done.7.refs_3_
  14.6 0.1 collective-permute-done.8.refs_5_
  14.7 0.0 collective-permute-done.core_ref.refs_3_
  14.7 0.6 %shard_map.49 = (bf16[32,896]{1,0:T(8,128)(2,1)S(1)}, bf16[32,896]{1,0:T(8,128)(2,1)S(1)}) custom-call(bf16[128,768]{1,0:T(8,128)(2,1)S(1)} %get-tuple-element.23.q_ref.refs_1_, bf16[32,768]{1,0:T(8,128)(2,1)S(1)} %shard_map.48.visitor_ref, bf16[256,768]{1,0:T(8,128)(2,1)S(1)} %get-tuple-element.24.own_ref.refs_2_, ...), custom_call_target="tpu_custom_call" | custom-call | flops 1000000 | bytes 1622016 | tf_op jit(solution)/shard_map/pallas_call | solution.py:305
  15.3 0.0 copy-start.3
  15.3 2.8 %collective-permute-start.9 = (bf16[32,896]{1,0:T(8,128)(2,1)S(1)}, bf16[32,896]{1,0:T(8,128)(2,1)S(1)}, u32[]{:S(2)}, u32[]{:S(2)}) collective-permute-start(bf16[32,896]{1,0:T(8,128)(2,1)S(1)} %get-tuple-element.31), channel_id=1, source_target_pairs={{0,8},{4,12},{8,0},{12,4},{1,9},{5,13},{9,1},{13,5},{2,10},{6,14},... | collective-permute-start | bytes 172040 | tf_op jit(solution)/shard_map/ppermute | solution.py:325
  18.1 0.0 collective-permute-done.6
  18.1 2.2 %all_gather.3.refs_6_ = bf16[384,768]{1,0:T(8,128)(2,1)S(1)} all-gather(bf16[192,768]{1,0:T(8,128)(2,1)S(1)} %collective-permute-done.6), channel_id=1, replica_groups={{0,1},{2,3},{4,5},{6,7},{8,9},{10,11},{12,13},{14,15},{16,17},{18,19},{..., dimensions={0}, use_global_device_ids=true | all-gather | bytes 884736 | tf_op jit(solution)/shard_map/all_gather | solution.py:335
  20.3 0.0 copy-done.3
  20.3 1.5 %shard_map.50 = (bf16[128,768]{1,0:T(8,128)(2,1)S(1)}, f32[32,768]{1,0:T(8,128)S(1)}, f32[32,768]{1,0:T(8,128)S(1)}, f32[32,768]{1,0:T(8,128)S(1)}, bf16[1536,32]{1,0:T(8,128)(2,1)S(1)}) custom-call(s32[16,128]{1,0:T(8,128)S(1)} %copy-done.3, bf16[128,768]{1,0:T(8,128)(2,1)S(1)} %get-tuple-element.23.q_ref.refs_1_, ...), custom_call_target="tpu_custom_call" | custom-call | flops 1000000 | bytes 1773568 | tf_op jit(solution)/shard_map/pallas_call | solution.py:305
  21.9 0.0 collective-permute-done.9.refs_5_
  21.9 1.1 %shard_map.51 = bf16[128,768]{1,0:T(8,128)(2,1)} custom-call(bf16[128,768]{1,0:T(8,128)(2,1)S(1)} %get-tuple-element.33.refs_0_, f32[32,768]{1,0:T(8,128)S(1)} %get-tuple-element.34.refs_1_, f32[32,768]{1,0:T(8,128)S(1)} %get-tuple-element.35.refs_2_, f32[32,768]{1,0:T(8,128)S(1)} %get-tuple-element.36.refs_3_, ...), custom_call_target="tpu_custom_call" | custom-call | flops 1000000 | bytes 557056 | tf_op jit(solution)/shard_map/pallas_call | solution.py:305
  (5 shorter events, 0.0 us)
Async XLA Ops:
  0.0 11.5 %copy-start.2 = (bf16[128,768]{1,0:T(8,128)(2,1)S(1)}, bf16[128,768]{1,0:T(8,128)(2,1)}, u32[]{:S(2)}) copy-start(bf16[128,768]{1,0:T(8,128)(2,1)} %v_ref.1) | copy-start | bytes 589828
  0.0 11.5 %copy-start.1 = (bf16[128,768]{1,0:T(8,128)(2,1)S(1)}, bf16[128,768]{1,0:T(8,128)(2,1)}, u32[]{:S(2)}) copy-start(bf16[128,768]{1,0:T(8,128)(2,1)} %k_ref.1) | copy-start | bytes 589828
  0.0 11.5 %copy-start = (bf16[128,768]{1,0:T(8,128)(2,1)S(1)}, bf16[128,768]{1,0:T(8,128)(2,1)}, u32[]{:S(2)}) copy-start(bf16[128,768]{1,0:T(8,128)(2,1)} %q_ref.1) | copy-start | bytes 589828
  2.4 10.2 %collective-permute-start.4 = (bf16[64,768]{1,0:T(8,128)(2,1)}, bf16[64,768]{1,0:T(8,128)(2,1)S(1)}, u32[]{:S(2)}, u32[]{:S(2)}) collective-permute-start(bf16[64,768]{1,0:T(8,128)(2,1)} %get-tuple-element.25), channel_id=1, source_target_pairs={{0,6},{1,7},{2,4},{3,5},{4,2},{5,3},{6,0},{7,1},{8,14},{9,15},{10,... | collective-permute-start | bytes 294920 | tf_op jit(solution)/shard_map/ppermute | solution.py:339
  6.4 6.4 %collective-permute-start.3 = (bf16[64,768]{1,0:T(8,128)(2,1)}, bf16[64,768]{1,0:T(8,128)(2,1)S(1)}, u32[]{:S(2)}, u32[]{:S(2)}) collective-permute-start(bf16[64,768]{1,0:T(8,128)(2,1)} %get-tuple-element.25), channel_id=1, source_target_pairs={{0,4},{4,0},{8,12},{12,8},{1,5},{5,1},{9,13},{13,9},{2,6},{6,2},{1... | collective-permute-start | bytes 294920 | tf_op jit(solution)/shard_map/ppermute | solution.py:325
  6.9 6.0 %collective-permute-start.1 = (bf16[64,768]{1,0:T(8,128)(2,1)}, bf16[64,768]{1,0:T(8,128)(2,1)S(1)}, u32[]{:S(2)}, u32[]{:S(2)}) collective-permute-start(bf16[64,768]{1,0:T(8,128)(2,1)} %get-tuple-element.25), channel_id=1, source_target_pairs={{0,2},{1,3},{2,0},{3,1},{4,6},{5,7},{6,4},{7,5},{8,10},{9,11},{10,... | collective-permute-start | bytes 294920 | tf_op jit(solution)/shard_map/ppermute | solution.py:325
  7.1 4.4 %copy-start.4 = (s32[12]{0:T(128)S(1)}, s32[12]{0:T(128)}, u32[]{:S(2)}) copy-start(s32[12]{0:T(128)} %off_ref.1) | copy-start | bytes 148
  7.1 5.4 %collective-permute-start.2 = (bf16[32,768]{1,0:T(8,128)(2,1)}, bf16[32,768]{1,0:T(8,128)(2,1)S(1)}, u32[]{:S(2)}, u32[]{:S(2)}) collective-permute-start(bf16[32,768]{1,0:T(8,128)(2,1)} %get-tuple-element.26), channel_id=1, source_target_pairs={{0,8},{4,12},{8,0},{12,4},{1,9},{5,13},{9,1},{13,5},{2,10},{6,14},... | collective-permute-start | bytes 147464 | tf_op jit(solution)/shard_map/ppermute | solution.py:325
  10.0 8.1 %collective-permute-start.6 = (bf16[192,768]{1,0:T(8,128)(2,1)}, bf16[192,768]{1,0:T(8,128)(2,1)S(1)}, u32[]{:S(2)}, u32[]{:S(2)}) collective-permute-start(bf16[192,768]{1,0:T(8,128)(2,1)} %get-tuple-element.28), channel_id=1, source_target_pairs={{0,2},{1,3},{2,0},{3,1},{4,6},{5,7},{6,4},{7,5},{8,10},{9,11},{10,... | collective-permute-start | bytes 884744 | tf_op jit(solution)/shard_map/ppermute | solution.py:325
  12.5 2.2 %collective-permute-start = (bf16[256,768]{1,0:T(8,128)(2,1)S(1)}, bf16[256,768]{1,0:T(8,128)(2,1)S(1)}, u32[]{:S(2)}, u32[]{:S(2)}) collective-permute-start(bf16[256,768]{1,0:T(8,128)(2,1)S(1)} %get-tuple-element.24.own_ref.refs_2_), channel_id=1, source_target_pairs={{0,1},{1,0},{2,3},{3,2},{4,5},{5,4},{6,7},{7,6},{8,9},{9,8},{10,11... | collective-permute-start | bytes 1179656 | tf_op jit(solution)/shard_map/ppermute | solution.py:325
  12.9 1.6 %collective-permute-start.5 = (bf16[64,768]{1,0:T(8,128)(2,1)S(1)}, bf16[64,768]{1,0:T(8,128)(2,1)S(1)}, u32[]{:S(2)}, u32[]{:S(2)}) collective-permute-start(bf16[64,768]{1,0:T(8,128)(2,1)S(1)} %collective-permute-done.1.refs_1_.refs_0_.refs_4_), channel_id=1, source_target_pairs={{0,1},{1,0},{2,3},{3,2},{4,5},{5,4},{6,7},{7,6},{8,9},{9,8},{10,11... | collective-permute-start | bytes 294920 | tf_op jit(solution)/shard_map/ppermute | solution.py:325
  13.2 1.4 %collective-permute-start.7 = (bf16[64,768]{1,0:T(8,128)(2,1)S(1)}, bf16[64,768]{1,0:T(8,128)(2,1)S(1)}, u32[]{:S(2)}, u32[]{:S(2)}) collective-permute-start(bf16[64,768]{1,0:T(8,128)(2,1)S(1)} %collective-permute-done.3.refs_2_), channel_id=1, source_target_pairs={{0,1},{1,0},{2,3},{3,2},{4,5},{5,4},{6,7},{7,6},{8,9},{9,8},{10,11... | collective-permute-start | bytes 294920 | tf_op jit(solution)/shard_map/ppermute | solution.py:325
  13.4 1.3 %collective-permute-start.8 = (bf16[64,768]{1,0:T(8,128)(2,1)S(1)}, bf16[64,768]{1,0:T(8,128)(2,1)S(1)}, u32[]{:S(2)}, u32[]{:S(2)}) collective-permute-start(bf16[64,768]{1,0:T(8,128)(2,1)S(1)} %collective-permute-done.4.refs_3_.refs_4_), channel_id=1, source_target_pairs={{0,1},{1,0},{2,3},{3,2},{4,5},{5,4},{6,7},{7,6},{8,9},{9,8},{10,11... | collective-permute-start | bytes 294920 | tf_op jit(solution)/shard_map/ppermute | solution.py:325
  15.3 5.0 %copy-start.3 = (s32[16,128]{1,0:T(8,128)S(1)}, s32[16,128]{1,0:T(8,128)}, u32[]{:S(2)}) copy-start(s32[16,128]{1,0:T(8,128)} %get-tuple-element.22.refs_0_) | copy-start | bytes 24580
  15.3 6.5 %collective-permute-start.9 = (bf16[32,896]{1,0:T(8,128)(2,1)S(1)}, bf16[32,896]{1,0:T(8,128)(2,1)S(1)}, u32[]{:S(2)}, u32[]{:S(2)}) collective-permute-start(bf16[32,896]{1,0:T(8,128)(2,1)S(1)} %get-tuple-element.31), channel_id=1, source_target_pairs={{0,8},{4,12},{8,0},{12,4},{1,9},{5,13},{9,1},{13,5},{2,10},{6,14},... | collective-permute-start | bytes 172040 | tf_op jit(solution)/shard_map/ppermute | solution.py:325

commit v5 on v4

--- a/solution.py
+++ b/solution.py
@@ -12,7 +12,7 @@
 PAIR = 2 * HEAD_DIMENSION
 LOWEST = -1e30
 LIMIT = 56
-COST = (10**6, 10**6, 10**10, 0, 0, 10**6, 10**6, 10**6)
+COST = (10**6, 10**6, 10**10, 10**10, 0, 10**6, 10**6, 10**6)
 
 
 def round_up(count, step):
@@ -85,16 +85,11 @@
 
 
 def first_kernel(sizes, *refs):
-    qd_ref, first_ref, second_ref, lanes_ref = refs[4:8]
-    off_ref, q_ref, k_ref, v_ref, sems = refs[8:]
+    qd_ref, first_ref, second_ref = refs[4:7]
+    off_ref, q_ref, k_ref, v_ref, sems = refs[7:]
     fetch(refs[:4], (off_ref, q_ref, k_ref, v_ref), sems)
     kept, rest, count = sizes.kept_pad, sizes.rest_pad, sizes.all_pad
     scale = HEAD_DIMENSION ** (-0.5)
-    lanes = lax.broadcasted_iota(jnp.int32, lanes_ref.shape, 0)
-    spread_out = jnp.zeros(lanes_ref.shape, jnp.int32)
-    for head in range(q_ref.shape[1] // HEAD_DIMENSION):
-        spread_out = jnp.where(lanes == head, off_ref[head], spread_out)
-    lanes_ref[...] = spread_out
     for pair in range(q_ref.shape[1] // PAIR):
         cols = slice(pair * PAIR, (pair + 1) * PAIR)
         chosen = order_rows_of_pair(sizes, lambda head: off_ref[head], pair, count)
@@ -109,20 +104,17 @@
         second_ref[rest:, cols] = v[kept:]
 
 
-def order_kernel(sizes, off_ref, q_ref, k_ref, v_ref, qs_ref, own_ref):
-    kept, count = sizes.kept_pad, sizes.all_pad
+def order_kernel(sizes, off_ref, q_ref, qs_ref, back_ref, spread_ref):
+    width = q_ref.shape[1]
     scale = HEAD_DIMENSION ** (-0.5)
-    found = []
-    for pair in range(q_ref.shape[1] // PAIR):
-        cols = slice(pair * PAIR, (pair + 1) * PAIR)
-        chosen = order_rows_of_pair(sizes, lambda head: off_ref[head], pair, count)
-        found.append(dot(chosen, jnp.concatenate([q_ref[:, cols], k_ref[:, cols], v_ref[:, cols]], 1)))
-    for pair, both in enumerate(found):
-        cols = slice(pair * PAIR, (pair + 1) * PAIR)
-        qs_ref[:, cols] = (select(both, count) * scale).astype(jnp.bfloat16)
-        k = select(both, count, slice(PAIR, 2 * PAIR)).astype(jnp.bfloat16)
-        v = select(both, count, slice(2 * PAIR, 3 * PAIR)).astype(jnp.bfloat16)
-        own_ref[:, cols] = jnp.concatenate([k[:kept], v[:kept], k[kept:], v[kept:]], 0)
+    for pair in range(width // PAIR):
+        cols = slice(pair * PAIR, (pair + 1) * PAIR)
+        chosen = order_rows_of_pair(sizes, lambda head: off_ref[head], pair, sizes.all_pad)
+        qs_ref[:, cols] = (select(dot(chosen, q_ref[:, cols]), sizes.all_pad) * scale).astype(jnp.bfloat16)
+        for head in (2 * pair, 2 * pair + 1):
+            back_ref[head * sizes.rows : (head + 1) * sizes.rows] = restore_rows(sizes, off_ref[head])
+    spread_ref[:, :width] = spread(width, (0,))
+    spread_ref[:, width:] = spread(width, (1, 2))
 
 
 def rows_of(device, begin, count, cols):
@@ -159,8 +151,8 @@
 
 
 def in_turn(sizes, refs):
-    found = [[(r, 0, sizes.first)] for r in refs]
-    return found[: sizes.sub - 2], found[sizes.sub - 2 :]
+    found = [[(r, n * sizes.first, sizes.first)] for n in range(sizes.sub) for r in refs]
+    return found[: sizes.sub], found[sizes.sub :]
 
 
 def join(devices, begin, count, cols):
@@ -174,10 +166,9 @@
         begin += r.shape[0]
 
 
-def partial_kernel(sizes, others, q_ref, visitor_ref, own_ref, core_ref, *refs):
-    first_refs, out_refs = refs[: -others - 1], refs[-others - 1 :]
-    here, beside = in_turn(sizes, first_refs)
-    devices = [whole(own_ref), whole(core_ref)] + here + beside
+def partial_kernel(sizes, others, q_ref, visitor_ref, lot_ref, other_lot_ref, *out_refs):
+    here, beside = in_turn(sizes, (lot_ref, other_lot_ref))
+    devices = here + beside
     width = q_ref.shape[1]
     kept = sizes.kept_pad
     rows = (others + 1) * kept
@@ -215,13 +206,12 @@
 
 
 def dense_kernel(sizes, *refs):
-    off_ref, q_ref = refs[:2]
-    own_refs, first_refs, second_refs = refs[2:4], refs[4 : 2 + sizes.sub], refs[2 + sizes.sub : -5]
-    devices = [whole(r) for r in own_refs]
-    for n, d in enumerate(in_turn(sizes, first_refs)[0]):
-        r = second_refs[n // 2]
-        devices.append(d + [(r, n % 2 * sizes.second, sizes.second)])
-    base_ref, out_ref, total_ref, top_ref, back_ref = refs[-5:]
+    back_ref, q_ref = refs[:2]
+    lot_refs, near_refs, far_refs = refs[2:4], refs[4:6], refs[6:-4]
+    second = [whole(r) for r in near_refs]
+    second += [[(r, core * sizes.second, sizes.second)] for r in far_refs for core in range(2)]
+    devices = [d + more for d, more in zip(in_turn(sizes, lot_refs)[0], second)]
+    base_ref, out_ref, total_ref, top_ref = refs[-4:]
     width = q_ref.shape[1]
     kept, rest, rows = sizes.kept_pad, sizes.rest_pad, sizes.all_pad
     begin = sizes.kept_keys
@@ -250,9 +240,7 @@
         results.append((out[kept:] / total[kept:]).astype(jnp.bfloat16))
     for pair, result in enumerate(results):
         cols = slice(pair * PAIR, (pair + 1) * PAIR)
-        back = [restore_rows(sizes, off_ref[2 * pair + n : 2 * pair + n + 1, 0:1]) for n in range(2)]
-        back = jnp.concatenate(back, 0)
-        back_ref[2 * sizes.rows * pair : 2 * sizes.rows * (pair + 1)] = back[:, :kept]
+        back = back_ref[2 * sizes.rows * pair : 2 * sizes.rows * (pair + 1)]
         whole_rows = jnp.concatenate([jnp.zeros((kept, PAIR), jnp.bfloat16), result], 0)
         base_ref[:, cols] = select(dot(back, whole_rows), sizes.rows).astype(jnp.bfloat16)
 
@@ -260,7 +248,6 @@
 def dense_shapes(sizes, width):
     shapes = [(sizes.rows, width, jnp.bfloat16)]
     shapes += [(sizes.kept_pad, width, jnp.float32)] * 3
-    shapes += [(width // PAIR * 2 * sizes.rows, sizes.kept_pad, jnp.bfloat16)]
     return [jax.ShapeDtypeStruct(s[:2], s[2]) for s in shapes]
 
 
@@ -272,14 +259,14 @@
 
 
 def merge_kernel(sizes, *refs):
-    base_ref, out_ref, total_ref, top_ref, back_ref = refs[:5]
-    part_refs, done_ref = refs[5:-1], refs[-1]
+    back_ref, spread_ref, base_ref, out_ref, total_ref, top_ref = refs[:6]
+    part_refs, done_ref = refs[6:-1], refs[-1]
     others = len(part_refs)
     width = out_ref.shape[1]
     kept = sizes.kept_pad
     stats = jnp.concatenate([r[:, width:] for r in part_refs], 0)
-    tops = dot(stats, spread(width, (0,)))
-    totals = dot(stats, spread(width, (1, 2)))
+    tops = dot(stats, spread_ref[:, :width])
+    totals = dot(stats, spread_ref[:, width:])
     theirs = [tops[n * kept : (n + 1) * kept] for n in range(others)]
     top = top_ref[...]
     best = functools.reduce(jnp.maximum, theirs, top)
@@ -292,7 +279,7 @@
     result = (out / total).astype(jnp.bfloat16)
     for pair in range(width // PAIR):
         cols = slice(pair * PAIR, (pair + 1) * PAIR)
-        back = dot(back_ref[2 * sizes.rows * pair : 2 * sizes.rows * (pair + 1)], result[:, cols])
+        back = dot(back_ref[2 * sizes.rows * pair : 2 * sizes.rows * (pair + 1), :kept], result[:, cols])
         done_ref[:, cols] = (select(back, sizes.rows) + base_ref[:, cols].astype(jnp.float32)).astype(jnp.bfloat16)
 
 
@@ -340,10 +327,9 @@
 
     masks, far_masks = range(2, seq, 2), range(2, sub, 2)
     heads = width // HEAD_DIMENSION
-    q_kept, first, second, lanes = call(
+    q_kept, first, second = call(
         functools.partial(first_kernel, sizes),
-        [array(n) for n in (sizes.kept_pad, sizes.first, sizes.second)]
-        + [array(round_up(heads, 8), 128, jnp.int32)],
+        [array(n) for n in (sizes.kept_pad, sizes.first, sizes.second)],
         (offsets, queries, keys, values),
         COST[0],
         pltpu.HBM,
@@ -352,27 +338,31 @@
         + [pltpu.SemaphoreType.DMA((4,))],
         LIMIT,
     )
-    lot = far(first) + [swap(first, "seq", 1)] + [swap_both(first, mask) for mask in far_masks]
+    far_first = far(first)
+    lot = [first] + far_first + [swap(first, "seq", 1)] + [swap_both(first, mask) for mask in far_masks]
+    far_second = far(second)
+    q, back, spreads = call(
+        functools.partial(order_kernel, sizes),
+        [array(sizes.all_pad), array(heads * rows, sizes.all_pad), array(PAIR, 2 * width)],
+        (offsets, queries),
+        COST[1],
+    )
     visitors = [swap(q_kept, "seq", mask) for mask in masks]
-    far_second = far(second)
-    q, own = call(
-        functools.partial(order_kernel, sizes),
-        [array(n) for n in (sizes.all_pad, 2 * sizes.all_pad)],
-        (offsets, queries, keys, values),
-        COST[1],
-    )
-    own = [own, swap(own, "sub", 1)]
+    lot = call(
+        functools.partial(collect_kernel, len(lot)), array(len(lot) * sizes.first), (*lot, q), COST[2]
+    )
+    near_second = [second, swap(after(second, lot), "sub", 1)]
+    lot = [lot, swap(lot, "sub", 1)]
     visitors = call(
         functools.partial(collect_kernel, len(masks)),
         array(len(masks) * sizes.kept_pad),
-        (*visitors, *lot),
-        COST[2],
-    )
-    lot = [y for x in lot for y in (x, swap(after(x, visitors), "sub", 1))]
+        visitors,
+        COST[3],
+    )
     *parts, own_part = call(
         functools.partial(partial_kernel, sizes, len(masks)),
         [array(sizes.kept_pad, width + PAIR)] * (len(masks) + 1),
-        (q, visitors, *own, *lot),
+        (q, visitors, *lot),
         COST[5],
     )
     returned = [swap(part, "seq", mask) for mask, part in zip(masks, parts)]
@@ -380,10 +370,10 @@
     dense = call(
         functools.partial(dense_kernel, sizes),
         dense_shapes(sizes, width),
-        (lanes, q, *own, *lot[: sub - 2], *far_second),
+        (back, q, *lot, *near_second, *far_second),
         COST[6],
     )
-    return call(functools.partial(merge_kernel, sizes), array(rows), (*dense, *returned, own_part), COST[7])
+    return call(functools.partial(merge_kernel, sizes), array(rows), (back, spreads, *dense, *returned, own_part), COST[7])
 
 
 def solution(mesh):

time: 23.1 us -> 22.9 us (level)
  starting transfers between devices: 12.8 us -> 11.8 us
  local copies, waits for them, and re-layouts: 0.02 us -> 0.86 us
    ppermute x9 -> x7, starting transfers between devices: 8.74 us -> 7.76 us  [swap(): lax.ppermute(x, axis, [(n, n ^ mask) for n in range(lax.axis_size(axis))])]
    unnamed x10 -> x8, local copies, waits for them, and re-layouts: 0.02 us -> 0.86 us
    ppermute x9 -> x7, waiting for transfers between devices: 1.27 us -> 1.11 us  [swap(): lax.ppermute(x, axis, [(n, n ^ mask) for n in range(lax.axis_size(axis))])]
    pallas_call x6 -> x7, Pallas kernels: 6.65 us -> 6.71 us  [call(): pl.pallas_call(kernel, out_shape=out_shape, in_specs=in_specs, out_specs=...]
  transfers between devices with their start and end apart: 10 -> 8, of which waited for: 4 -> 3; matrix products, arithmetic and copies ran while one was open for 0% -> 0% of each run, Pallas kernels for 14% -> 14%
where the time goes in v5:
time: 22.9 us; the launch traced here: 22.8 us
  starting transfers between devices  11.8 us (52%)
  Pallas kernels  6.71 us (29%)
  blocking collectives  2.22 us (10%)
  waiting for transfers between devices  1.11 us (5%)
  local copies, waits for them, and re-layouts  0.86 us (4%)
    ppermute x7, starting transfers between devices, swap(): lax.ppermute(x, axis, [(n, n ^ mask) for n in range(lax.axis_size(axis))])  7.76 us
    pallas_call x7, Pallas kernels, call(): pl.pallas_call(kernel, out_shape=out_shape, in_specs=in_specs, out_specs=...  6.71 us
    ppermute x1, starting transfers between devices, swap_both(): lax.ppermute(x, ('seq', 'sub'), [(n, n ^ sub ^ mask) for n in range(size)])  4.02 us
    all_gather x1, blocking collectives, both_cores(): lax.all_gather(x, 'sub', axis=0, tiled=True, axis_index_groups=chips)  2.22 us
    ppermute x7, waiting for transfers between devices, swap(): lax.ppermute(x, axis, [(n, n ^ mask) for n in range(lax.axis_size(axis))])  1.11 us
    unnamed x8, local copies, waits for them, and re-layouts  0.86 us
  transfers between devices with their start and end apart: 8, of which 3 were waited for; matrix products, arithmetic and copies ran while one was open for 0% of the time, Pallas kernels for 14%

profile of v5, /device:TPU:0, one launch (start us, length us, event | category | flops | bytes accessed | tf_op | source)
XLA Modules:
  0.0 22.8 jit_solution(5387859679284719294)
XLA Ops:
  0.0 0.0 copy-start
  0.0 2.4 %shard_map.47 = (bf16[32,768]{1,0:T(8,128)(2,1)}, bf16[64,768]{1,0:T(8,128)(2,1)}, bf16[192,768]{1,0:T(8,128)(2,1)}) custom-call(s32[12]{0:T(128)} %refs_0_.1, bf16[128,768]{1,0:T(8,128)(2,1)} %refs_1_.1, bf16[128,768]{1,0:T(8,128)(2,1)} %refs_2_.1, bf16[128,768]{1,0:T(8,128)(2,1)} %refs_3_.1), custom_call_target="tpu_custom_call" | custom-call | flops 1000000 | bytes 589848 | tf_op jit(solution)/shard_map/pallas_call | solution.py:292
  2.4 4.0 %collective-permute-start.2 = (bf16[64,768]{1,0:T(8,128)(2,1)}, bf16[64,768]{1,0:T(8,128)(2,1)S(1)}, u32[]{:S(2)}, u32[]{:S(2)}) collective-permute-start(bf16[64,768]{1,0:T(8,128)(2,1)} %get-tuple-element.22.refs_0_), channel_id=1, source_target_pairs={{0,6},{1,7},{2,4},{3,5},{4,2},{5,3},{6,0},{7,1},{8,14},{9,15},{10,... | collective-permute-start | bytes 294920 | tf_op jit(solution)/shard_map/ppermute | solution.py:326
  6.4 0.4 %collective-permute-start.1 = (bf16[64,768]{1,0:T(8,128)(2,1)}, bf16[64,768]{1,0:T(8,128)(2,1)S(1)}, u32[]{:S(2)}, u32[]{:S(2)}) collective-permute-start(bf16[64,768]{1,0:T(8,128)(2,1)} %get-tuple-element.22.refs_0_), channel_id=1, source_target_pairs={{0,4},{4,0},{8,12},{12,8},{1,5},{5,1},{9,13},{13,9},{2,6},{6,2},{1... | collective-permute-start | bytes 294920 | tf_op jit(solution)/shard_map/ppermute | solution.py:312
  6.8 0.2 collective-permute-start
  7.0 0.0 copy-start.2
  7.0 2.9 %collective-permute-start.6 = (bf16[32,768]{1,0:T(8,128)(2,1)}, bf16[32,768]{1,0:T(8,128)(2,1)S(1)}, u32[]{:S(2)}, u32[]{:S(2)}) collective-permute-start(bf16[32,768]{1,0:T(8,128)(2,1)} %get-tuple-element.25), channel_id=1, source_target_pairs={{0,8},{4,12},{8,0},{12,4},{1,9},{5,13},{9,1},{13,5},{2,10},{6,14},... | collective-permute-start | bytes 147464 | tf_op jit(solution)/shard_map/ppermute | solution.py:312
  10.0 0.0 copy-start.3
  10.0 1.5 %collective-permute-start.5 = (bf16[192,768]{1,0:T(8,128)(2,1)}, bf16[192,768]{1,0:T(8,128)(2,1)S(1)}, u32[]{:S(2)}, u32[]{:S(2)}) collective-permute-start(bf16[192,768]{1,0:T(8,128)(2,1)} %get-tuple-element.24.refs_4_), channel_id=1, source_target_pairs={{0,2},{1,3},{2,0},{3,1},{4,6},{5,7},{6,4},{7,5},{8,10},{9,11},{10,... | collective-permute-start | bytes 884744 | tf_op jit(solution)/shard_map/ppermute | solution.py:312
  11.5 0.0 copy-done
  11.5 0.0 copy-done.2
  11.5 1.2 %shard_map.46 = (bf16[128,768]{1,0:T(8,128)(2,1)S(1)}, bf16[1536,128]{1,0:T(8,128)(2,1)S(1)}, bf16[128,1536]{1,0:T(8,128)(2,1)S(1)}) custom-call(s32[12]{0:T(128)S(1)} %copy-done.2, bf16[128,768]{1,0:T(8,128)(2,1)S(1)} %copy-done), custom_call_target="tpu_custom_call" | custom-call | flops 1000000 | bytes 196632 | tf_op jit(solution)/shard_map/pallas_call | solution.py:292
  12.7 0.0 collective-permute-done.2.refs_3_
  12.7 0.1 collective-permute-done.1.refs_2_
  12.8 0.0 collective-permute-done.refs_1_
  12.8 0.0 copy-done.3
  12.8 0.0 copy-start.1
  12.9 0.1 collective-permute-start.3
  12.9 0.8 %copy-done.1 = bf16[192,768]{1,0:T(8,128)(2,1)S(1)} copy-done((bf16[192,768]{1,0:T(8,128)(2,1)S(1)}, bf16[192,768]{1,0:T(8,128)(2,1)}, u32[]{:S(2)}) %copy-start.1) | copy-done | bytes 294936
  13.8 0.0 collective-permute-start.4
  13.8 0.0 collective-permute-done.6.refs_0_
  13.8 0.9 %collective-permute-done.3.other_lot_ref.refs_3_ = bf16[256,768]{1,0:T(8,128)(2,1)S(1)} collective-permute-done((bf16[256,768]{1,0:T(8,128)(2,1)S(1)}, bf16[256,768]{1,0:T(8,128)(2,1)S(1)}, u32[]{:S(2)}, u32[]{:S(2)}) %collective-permute-start.3) | collective-permute-done | bytes 393248 | tf_op jit(solution)/shard_map/ppermute | solution.py:312
  14.6 0.6 %shard_map.50 = (bf16[32,896]{1,0:T(8,128)(2,1)S(1)}, bf16[32,896]{1,0:T(8,128)(2,1)S(1)}) custom-call(bf16[128,768]{1,0:T(8,128)(2,1)S(1)} %get-tuple-element.21.refs_4_.q_ref.refs_1_, bf16[32,768]{1,0:T(8,128)(2,1)S(1)} %shard_map.49.visitor_ref, bf16[256,768]{1,0:T(8,128)(2,1)S(1)} %shard_map.48.lot_ref.refs_2_, ...), custom_call_target="tpu_custom_call" | custom-call | flops 1000000 | bytes 1032192 | tf_op jit(solution)/shard_map/pallas_call | solution.py:292
  15.2 2.6 %collective-permute-start.7 = (bf16[32,896]{1,0:T(8,128)(2,1)S(1)}, bf16[32,896]{1,0:T(8,128)(2,1)S(1)}, u32[]{:S(2)}, u32[]{:S(2)}) collective-permute-start(bf16[32,896]{1,0:T(8,128)(2,1)S(1)} %get-tuple-element.26), channel_id=1, source_target_pairs={{0,8},{4,12},{8,0},{12,4},{1,9},{5,13},{9,1},{13,5},{2,10},{6,14},... | collective-permute-start | bytes 172040 | tf_op jit(solution)/shard_map/ppermute | solution.py:312
  17.8 0.2 collective-permute-done.5
  18.0 2.2 %all_gather.3.refs_6_ = bf16[384,768]{1,0:T(8,128)(2,1)S(1)} all-gather(bf16[192,768]{1,0:T(8,128)(2,1)S(1)} %collective-permute-done.5), channel_id=1, replica_groups={{0,1},{2,3},{4,5},{6,7},{8,9},{10,11},{12,13},{14,15},{16,17},{18,19},{..., dimensions={0}, use_global_device_ids=true | all-gather | bytes 884736 | tf_op jit(solution)/shard_map/all_gather | solution.py:322
  20.2 0.0 collective-permute-done.4.refs_5_
  20.2 1.4 %shard_map.51 = (bf16[128,768]{1,0:T(8,128)(2,1)S(1)}, f32[32,768]{1,0:T(8,128)S(1)}, f32[32,768]{1,0:T(8,128)S(1)}, f32[32,768]{1,0:T(8,128)S(1)}) custom-call(bf16[1536,128]{1,0:T(8,128)(2,1)S(1)} %get-tuple-element.19.refs_0_, bf16[128,768]{1,0:T(8,128)(2,1)S(1)} %get-tuple-element.21.refs_4_.q_ref.refs_1_, ...), custom_call_target="tpu_custom_call" | custom-call | flops 1000000 | bytes 2555904 | tf_op jit(solution)/shard_map/pallas_call | solution.py:292
  21.6 0.0 collective-permute-done.7.refs_6_
  21.6 1.1 %shard_map.52 = bf16[128,768]{1,0:T(8,128)(2,1)} custom-call(bf16[1536,128]{1,0:T(8,128)(2,1)S(1)} %get-tuple-element.19.refs_0_, bf16[128,1536]{1,0:T(8,128)(2,1)S(1)} %get-tuple-element.20.refs_1_, bf16[128,768]{1,0:T(8,128)(2,1)S(1)} %get-tuple-element.28.refs_2_, f32[32,768]{1,0:T(8,128)S(1)} %get-tuple-element.29.refs_3_, ...), custom_call_target="tpu_custom_call" | custom-call | flops 1000000 | bytes 1245184 | tf_op jit(solution)/shard_map/pallas_call | solution.py:292
  (2 shorter events, 0.0 us)
Async XLA Ops:
  0.0 11.5 %copy-start = (bf16[128,768]{1,0:T(8,128)(2,1)S(1)}, bf16[128,768]{1,0:T(8,128)(2,1)}, u32[]{:S(2)}) copy-start(bf16[128,768]{1,0:T(8,128)(2,1)} %refs_1_.1) | copy-start | bytes 589828
  2.4 10.3 %collective-permute-start.2 = (bf16[64,768]{1,0:T(8,128)(2,1)}, bf16[64,768]{1,0:T(8,128)(2,1)S(1)}, u32[]{:S(2)}, u32[]{:S(2)}) collective-permute-start(bf16[64,768]{1,0:T(8,128)(2,1)} %get-tuple-element.22.refs_0_), channel_id=1, source_target_pairs={{0,6},{1,7},{2,4},{3,5},{4,2},{5,3},{6,0},{7,1},{8,14},{9,15},{10,... | collective-permute-start | bytes 294920 | tf_op jit(solution)/shard_map/ppermute | solution.py:326
  6.4 6.4 %collective-permute-start.1 = (bf16[64,768]{1,0:T(8,128)(2,1)}, bf16[64,768]{1,0:T(8,128)(2,1)S(1)}, u32[]{:S(2)}, u32[]{:S(2)}) collective-permute-start(bf16[64,768]{1,0:T(8,128)(2,1)} %get-tuple-element.22.refs_0_), channel_id=1, source_target_pairs={{0,4},{4,0},{8,12},{12,8},{1,5},{5,1},{9,13},{13,9},{2,6},{6,2},{1... | collective-permute-start | bytes 294920 | tf_op jit(solution)/shard_map/ppermute | solution.py:312
  6.8 6.0 %collective-permute-start = (bf16[64,768]{1,0:T(8,128)(2,1)}, bf16[64,768]{1,0:T(8,128)(2,1)S(1)}, u32[]{:S(2)}, u32[]{:S(2)}) collective-permute-start(bf16[64,768]{1,0:T(8,128)(2,1)} %get-tuple-element.22.refs_0_), channel_id=1, source_target_pairs={{0,2},{1,3},{2,0},{3,1},{4,6},{5,7},{6,4},{7,5},{8,10},{9,11},{10,... | collective-permute-start | bytes 294920 | tf_op jit(solution)/shard_map/ppermute | solution.py:312
  7.0 4.4 %copy-start.2 = (s32[12]{0:T(128)S(1)}, s32[12]{0:T(128)}, u32[]{:S(2)}) copy-start(s32[12]{0:T(128)} %refs_0_.1) | copy-start | bytes 148
  7.0 6.7 %collective-permute-start.6 = (bf16[32,768]{1,0:T(8,128)(2,1)}, bf16[32,768]{1,0:T(8,128)(2,1)S(1)}, u32[]{:S(2)}, u32[]{:S(2)}) collective-permute-start(bf16[32,768]{1,0:T(8,128)(2,1)} %get-tuple-element.25), channel_id=1, source_target_pairs={{0,8},{4,12},{8,0},{12,4},{1,9},{5,13},{9,1},{13,5},{2,10},{6,14},... | collective-permute-start | bytes 147464 | tf_op jit(solution)/shard_map/ppermute | solution.py:312
  10.0 2.8 %copy-start.3 = (bf16[64,768]{1,0:T(8,128)(2,1)S(1)}, bf16[64,768]{1,0:T(8,128)(2,1)}, u32[]{:S(2)}) copy-start(bf16[64,768]{1,0:T(8,128)(2,1)} %get-tuple-element.22.refs_0_) | copy-start | bytes 294916
  10.0 8.0 %collective-permute-start.5 = (bf16[192,768]{1,0:T(8,128)(2,1)}, bf16[192,768]{1,0:T(8,128)(2,1)S(1)}, u32[]{:S(2)}, u32[]{:S(2)}) collective-permute-start(bf16[192,768]{1,0:T(8,128)(2,1)} %get-tuple-element.24.refs_4_), channel_id=1, source_target_pairs={{0,2},{1,3},{2,0},{3,1},{4,6},{5,7},{6,4},{7,5},{8,10},{9,11},{10,... | collective-permute-start | bytes 884744 | tf_op jit(solution)/shard_map/ppermute | solution.py:312
  12.8 1.0 %copy-start.1 = (bf16[192,768]{1,0:T(8,128)(2,1)S(1)}, bf16[192,768]{1,0:T(8,128)(2,1)}, u32[]{:S(2)}) copy-start(bf16[192,768]{1,0:T(8,128)(2,1)} %get-tuple-element.24.refs_4_) | copy-start | bytes 884740
  12.9 1.8 %collective-permute-start.3 = (bf16[256,768]{1,0:T(8,128)(2,1)S(1)}, bf16[256,768]{1,0:T(8,128)(2,1)S(1)}, u32[]{:S(2)}, u32[]{:S(2)}) collective-permute-start(bf16[256,768]{1,0:T(8,128)(2,1)S(1)} %shard_map.48.lot_ref.refs_2_), channel_id=1, source_target_pairs={{0,1},{1,0},{2,3},{3,2},{4,5},{5,4},{6,7},{7,6},{8,9},{9,8},{10,11... | collective-permute-start | bytes 1179656 | tf_op jit(solution)/shard_map/ppermute | solution.py:312
  13.8 6.4 %collective-permute-start.4 = (bf16[192,768]{1,0:T(8,128)(2,1)S(1)}, bf16[192,768]{1,0:T(8,128)(2,1)S(1)}, u32[]{:S(2)}, u32[]{:S(2)}) collective-permute-start(bf16[192,768]{1,0:T(8,128)(2,1)S(1)} %copy-done.1), channel_id=1, source_target_pairs={{0,1},{1,0},{2,3},{3,2},{4,5},{5,4},{6,7},{7,6},{8,9},{9,8},{10,11... | collective-permute-start | bytes 884744 | tf_op jit(solution)/shard_map/ppermute | solution.py:312
  15.2 6.4 %collective-permute-start.7 = (bf16[32,896]{1,0:T(8,128)(2,1)S(1)}, bf16[32,896]{1,0:T(8,128)(2,1)S(1)}, u32[]{:S(2)}, u32[]{:S(2)}) collective-permute-start(bf16[32,896]{1,0:T(8,128)(2,1)S(1)} %get-tuple-element.26), channel_id=1, source_target_pairs={{0,8},{4,12},{8,0},{12,4},{1,9},{5,13},{9,1},{13,5},{2,10},{6,14},... | collective-permute-start | bytes 172040 | tf_op jit(solution)/shard_map/ppermute | solution.py:312

commit v6 on v5

--- a/solution.py
+++ b/solution.py
@@ -260,7 +260,7 @@
 
 def merge_kernel(sizes, *refs):
     back_ref, spread_ref, base_ref, out_ref, total_ref, top_ref = refs[:6]
-    part_refs, done_ref = refs[6:-1], refs[-1]
+    part_refs, done_hbm, done_ref, sems = refs[6:-3], refs[-3], refs[-2], refs[-1]
     others = len(part_refs)
     width = out_ref.shape[1]
     kept = sizes.kept_pad
@@ -277,17 +277,25 @@
         out += r[:, :width].astype(jnp.float32) * factor
         total += totals[n * kept : (n + 1) * kept] * factor
     result = (out / total).astype(jnp.bfloat16)
+    leaving, half = [], width // 2
     for pair in range(width // PAIR):
         cols = slice(pair * PAIR, (pair + 1) * PAIR)
         back = dot(back_ref[2 * sizes.rows * pair : 2 * sizes.rows * (pair + 1), :kept], result[:, cols])
         done_ref[:, cols] = (select(back, sizes.rows) + base_ref[:, cols].astype(jnp.float32)).astype(jnp.bfloat16)
-
-
-def call(kernel, out_shape, operands, flops, place=pltpu.VMEM, scratch=(), limit=24):
+        if (pair + 1) * PAIR in (half, width):
+            part = pl.ds(half * len(leaving), half)
+            copy = pltpu.make_async_copy(done_ref.at[:, part], done_hbm.at[:, part], sems.at[len(leaving)])
+            copy.start()
+            leaving.append(copy)
+    for copy in leaving:
+        copy.wait()
+
+
+def call(kernel, out_shape, operands, flops, place=pltpu.VMEM, scratch=(), limit=24, out_place=pltpu.VMEM):
     spec = pl.BlockSpec(memory_space=place)
     smem = pl.BlockSpec(memory_space=pltpu.SMEM)
     in_specs = [smem if x.ndim == 1 and place == pltpu.VMEM else spec for x in operands]
-    out_specs = jax.tree.map(lambda _: pl.BlockSpec(memory_space=pltpu.VMEM), out_shape)
+    out_specs = jax.tree.map(lambda _: pl.BlockSpec(memory_space=out_place), out_shape)
     size = sum(x.size * 2 for x in operands)
     return pl.pallas_call(
         kernel,
@@ -373,7 +381,14 @@
         (back, q, *lot, *near_second, *far_second),
         COST[6],
     )
-    return call(functools.partial(merge_kernel, sizes), array(rows), (back, spreads, *dense, *returned, own_part), COST[7])
+    return call(
+        functools.partial(merge_kernel, sizes),
+        array(rows),
+        (back, spreads, *dense, *returned, own_part),
+        COST[7],
+        scratch=[pltpu.VMEM((rows, width), jnp.bfloat16), pltpu.SemaphoreType.DMA((2,))],
+        out_place=pltpu.HBM,
+    )
 
 
 def solution(mesh):

time: 22.9 us -> 22.9 us (level)
  no operation moved by 1% of the time
where the time goes in v6:
time: 22.9 us; the launch traced here: 22.7 us
  starting transfers between devices  11.8 us (52%)
  Pallas kernels  6.69 us (29%)
  blocking collectives  2.22 us (10%)
  waiting for transfers between devices  1.11 us (5%)
  local copies, waits for them, and re-layouts  0.86 us (4%)
    ppermute x7, starting transfers between devices, swap(): lax.ppermute(x, axis, [(n, n ^ mask) for n in range(lax.axis_size(axis))])  7.76 us
    pallas_call x7, Pallas kernels, call(): pl.pallas_call(kernel, out_shape=out_shape, in_specs=in_specs, out_specs=...  6.69 us
    ppermute x1, starting transfers between devices, swap_both(): lax.ppermute(x, ('seq', 'sub'), [(n, n ^ sub ^ mask) for n in range(size)])  4.02 us
    all_gather x1, blocking collectives, both_cores(): lax.all_gather(x, 'sub', axis=0, tiled=True, axis_index_groups=chips)  2.22 us
    ppermute x7, waiting for transfers between devices, swap(): lax.ppermute(x, axis, [(n, n ^ mask) for n in range(lax.axis_size(axis))])  1.11 us
    unnamed x8, local copies, waits for them, and re-layouts  0.86 us
  transfers between devices with their start and end apart: 8, of which 3 were waited for; matrix products, arithmetic and copies ran while one was open for 0% of the time, Pallas kernels for 14%

profile of v6, /device:TPU:0, one launch (start us, length us, event | category | flops | bytes accessed | tf_op | source)
XLA Modules:
  0.0 22.7 jit_solution(16956253283680583795)
XLA Ops:
  0.0 0.0 copy-start
  0.0 2.4 %shard_map.47 = (bf16[32,768]{1,0:T(8,128)(2,1)}, bf16[64,768]{1,0:T(8,128)(2,1)}, bf16[192,768]{1,0:T(8,128)(2,1)}) custom-call(s32[12]{0:T(128)} %refs_0_.1, bf16[128,768]{1,0:T(8,128)(2,1)} %refs_1_.1, bf16[128,768]{1,0:T(8,128)(2,1)} %refs_2_.1, bf16[128,768]{1,0:T(8,128)(2,1)} %refs_3_.1), custom_call_target="tpu_custom_call" | custom-call | flops 1000000 | bytes 589848 | tf_op jit(solution)/shard_map/pallas_call | solution.py:300
  2.4 4.0 %collective-permute-start.2 = (bf16[64,768]{1,0:T(8,128)(2,1)}, bf16[64,768]{1,0:T(8,128)(2,1)S(1)}, u32[]{:S(2)}, u32[]{:S(2)}) collective-permute-start(bf16[64,768]{1,0:T(8,128)(2,1)} %get-tuple-element.22.refs_0_), channel_id=1, source_target_pairs={{0,6},{1,7},{2,4},{3,5},{4,2},{5,3},{6,0},{7,1},{8,14},{9,15},{10,... | collective-permute-start | bytes 294920 | tf_op jit(solution)/shard_map/ppermute | solution.py:334
  6.4 0.4 %collective-permute-start.1 = (bf16[64,768]{1,0:T(8,128)(2,1)}, bf16[64,768]{1,0:T(8,128)(2,1)S(1)}, u32[]{:S(2)}, u32[]{:S(2)}) collective-permute-start(bf16[64,768]{1,0:T(8,128)(2,1)} %get-tuple-element.22.refs_0_), channel_id=1, source_target_pairs={{0,4},{4,0},{8,12},{12,8},{1,5},{5,1},{9,13},{13,9},{2,6},{6,2},{1... | collective-permute-start | bytes 294920 | tf_op jit(solution)/shard_map/ppermute | solution.py:320
  6.8 0.2 collective-permute-start
  7.0 0.0 copy-start.2
  7.0 2.9 %collective-permute-start.6 = (bf16[32,768]{1,0:T(8,128)(2,1)}, bf16[32,768]{1,0:T(8,128)(2,1)S(1)}, u32[]{:S(2)}, u32[]{:S(2)}) collective-permute-start(bf16[32,768]{1,0:T(8,128)(2,1)} %get-tuple-element.25), channel_id=1, source_target_pairs={{0,8},{4,12},{8,0},{12,4},{1,9},{5,13},{9,1},{13,5},{2,10},{6,14},... | collective-permute-start | bytes 147464 | tf_op jit(solution)/shard_map/ppermute | solution.py:320
  10.0 0.0 copy-start.3
  10.0 1.5 %collective-permute-start.5 = (bf16[192,768]{1,0:T(8,128)(2,1)}, bf16[192,768]{1,0:T(8,128)(2,1)S(1)}, u32[]{:S(2)}, u32[]{:S(2)}) collective-permute-start(bf16[192,768]{1,0:T(8,128)(2,1)} %get-tuple-element.24.refs_4_), channel_id=1, source_target_pairs={{0,2},{1,3},{2,0},{3,1},{4,6},{5,7},{6,4},{7,5},{8,10},{9,11},{10,... | collective-permute-start | bytes 884744 | tf_op jit(solution)/shard_map/ppermute | solution.py:320
  11.5 0.0 copy-done
  11.5 0.0 copy-done.2
  11.5 1.2 %shard_map.46 = (bf16[128,768]{1,0:T(8,128)(2,1)S(1)}, bf16[1536,128]{1,0:T(8,128)(2,1)S(1)}, bf16[128,1536]{1,0:T(8,128)(2,1)S(1)}) custom-call(s32[12]{0:T(128)S(1)} %copy-done.2, bf16[128,768]{1,0:T(8,128)(2,1)S(1)} %copy-done), custom_call_target="tpu_custom_call" | custom-call | flops 1000000 | bytes 196632 | tf_op jit(solution)/shard_map/pallas_call | solution.py:300
  12.7 0.0 collective-permute-done.2.refs_3_
  12.7 0.1 collective-permute-done.1.refs_2_
  12.8 0.0 collective-permute-done.refs_1_
  12.8 0.0 copy-done.3
  12.8 0.0 copy-start.1
  12.9 0.1 collective-permute-start.3
  12.9 0.8 %copy-done.1 = bf16[192,768]{1,0:T(8,128)(2,1)S(1)} copy-done((bf16[192,768]{1,0:T(8,128)(2,1)S(1)}, bf16[192,768]{1,0:T(8,128)(2,1)}, u32[]{:S(2)}) %copy-start.1) | copy-done | bytes 294936
  13.8 0.0 collective-permute-start.4
  13.8 0.0 collective-permute-done.6.refs_0_
  13.8 0.9 %collective-permute-done.3.other_lot_ref.refs_3_ = bf16[256,768]{1,0:T(8,128)(2,1)S(1)} collective-permute-done((bf16[256,768]{1,0:T(8,128)(2,1)S(1)}, bf16[256,768]{1,0:T(8,128)(2,1)S(1)}, u32[]{:S(2)}, u32[]{:S(2)}) %collective-permute-start.3) | collective-permute-done | bytes 393248 | tf_op jit(solution)/shard_map/ppermute | solution.py:320
  14.6 0.6 %shard_map.50 = (bf16[32,896]{1,0:T(8,128)(2,1)S(1)}, bf16[32,896]{1,0:T(8,128)(2,1)S(1)}) custom-call(bf16[128,768]{1,0:T(8,128)(2,1)S(1)} %get-tuple-element.21.refs_4_.q_ref.refs_1_, bf16[32,768]{1,0:T(8,128)(2,1)S(1)} %shard_map.49.visitor_ref, bf16[256,768]{1,0:T(8,128)(2,1)S(1)} %shard_map.48.lot_ref.refs_2_, ...), custom_call_target="tpu_custom_call" | custom-call | flops 1000000 | bytes 1032192 | tf_op jit(solution)/shard_map/pallas_call | solution.py:300
  15.2 2.6 %collective-permute-start.7 = (bf16[32,896]{1,0:T(8,128)(2,1)S(1)}, bf16[32,896]{1,0:T(8,128)(2,1)S(1)}, u32[]{:S(2)}, u32[]{:S(2)}) collective-permute-start(bf16[32,896]{1,0:T(8,128)(2,1)S(1)} %get-tuple-element.26), channel_id=1, source_target_pairs={{0,8},{4,12},{8,0},{12,4},{1,9},{5,13},{9,1},{13,5},{2,10},{6,14},... | collective-permute-start | bytes 172040 | tf_op jit(solution)/shard_map/ppermute | solution.py:320
  17.8 0.2 collective-permute-done.5
  18.0 2.2 %all_gather.3.refs_6_ = bf16[384,768]{1,0:T(8,128)(2,1)S(1)} all-gather(bf16[192,768]{1,0:T(8,128)(2,1)S(1)} %collective-permute-done.5), channel_id=1, replica_groups={{0,1},{2,3},{4,5},{6,7},{8,9},{10,11},{12,13},{14,15},{16,17},{18,19},{..., dimensions={0}, use_global_device_ids=true | all-gather | bytes 884736 | tf_op jit(solution)/shard_map/all_gather | solution.py:330
  20.2 0.0 collective-permute-done.4.refs_5_
  20.2 1.4 %shard_map.51 = (bf16[128,768]{1,0:T(8,128)(2,1)S(1)}, f32[32,768]{1,0:T(8,128)S(1)}, f32[32,768]{1,0:T(8,128)S(1)}, f32[32,768]{1,0:T(8,128)S(1)}) custom-call(bf16[1536,128]{1,0:T(8,128)(2,1)S(1)} %get-tuple-element.19.refs_0_, bf16[128,768]{1,0:T(8,128)(2,1)S(1)} %get-tuple-element.21.refs_4_.q_ref.refs_1_, ...), custom_call_target="tpu_custom_call" | custom-call | flops 1000000 | bytes 2555904 | tf_op jit(solution)/shard_map/pallas_call | solution.py:300
  21.6 0.0 collective-permute-done.7.refs_6_
  21.6 1.1 %shard_map.52 = bf16[128,768]{1,0:T(8,128)(2,1)} custom-call(bf16[1536,128]{1,0:T(8,128)(2,1)S(1)} %get-tuple-element.19.refs_0_, bf16[128,1536]{1,0:T(8,128)(2,1)S(1)} %get-tuple-element.20.refs_1_, bf16[128,768]{1,0:T(8,128)(2,1)S(1)} %get-tuple-element.28.refs_2_, f32[32,768]{1,0:T(8,128)S(1)} %get-tuple-element.29.refs_3_, ...), custom_call_target="tpu_custom_call" | custom-call | flops 1000000 | bytes 1245184 | tf_op jit(solution)/shard_map/pallas_call | solution.py:300
  (2 shorter events, 0.0 us)
Async XLA Ops:
  0.0 11.5 %copy-start = (bf16[128,768]{1,0:T(8,128)(2,1)S(1)}, bf16[128,768]{1,0:T(8,128)(2,1)}, u32[]{:S(2)}) copy-start(bf16[128,768]{1,0:T(8,128)(2,1)} %refs_1_.1) | copy-start | bytes 589828
  2.4 10.3 %collective-permute-start.2 = (bf16[64,768]{1,0:T(8,128)(2,1)}, bf16[64,768]{1,0:T(8,128)(2,1)S(1)}, u32[]{:S(2)}, u32[]{:S(2)}) collective-permute-start(bf16[64,768]{1,0:T(8,128)(2,1)} %get-tuple-element.22.refs_0_), channel_id=1, source_target_pairs={{0,6},{1,7},{2,4},{3,5},{4,2},{5,3},{6,0},{7,1},{8,14},{9,15},{10,... | collective-permute-start | bytes 294920 | tf_op jit(solution)/shard_map/ppermute | solution.py:334
  6.4 6.4 %collective-permute-start.1 = (bf16[64,768]{1,0:T(8,128)(2,1)}, bf16[64,768]{1,0:T(8,128)(2,1)S(1)}, u32[]{:S(2)}, u32[]{:S(2)}) collective-permute-start(bf16[64,768]{1,0:T(8,128)(2,1)} %get-tuple-element.22.refs_0_), channel_id=1, source_target_pairs={{0,4},{4,0},{8,12},{12,8},{1,5},{5,1},{9,13},{13,9},{2,6},{6,2},{1... | collective-permute-start | bytes 294920 | tf_op jit(solution)/shard_map/ppermute | solution.py:320
  6.8 6.0 %collective-permute-start = (bf16[64,768]{1,0:T(8,128)(2,1)}, bf16[64,768]{1,0:T(8,128)(2,1)S(1)}, u32[]{:S(2)}, u32[]{:S(2)}) collective-permute-start(bf16[64,768]{1,0:T(8,128)(2,1)} %get-tuple-element.22.refs_0_), channel_id=1, source_target_pairs={{0,2},{1,3},{2,0},{3,1},{4,6},{5,7},{6,4},{7,5},{8,10},{9,11},{10,... | collective-permute-start | bytes 294920 | tf_op jit(solution)/shard_map/ppermute | solution.py:320
  7.0 4.4 %copy-start.2 = (s32[12]{0:T(128)S(1)}, s32[12]{0:T(128)}, u32[]{:S(2)}) copy-start(s32[12]{0:T(128)} %refs_0_.1) | copy-start | bytes 148
  7.0 6.7 %collective-permute-start.6 = (bf16[32,768]{1,0:T(8,128)(2,1)}, bf16[32,768]{1,0:T(8,128)(2,1)S(1)}, u32[]{:S(2)}, u32[]{:S(2)}) collective-permute-start(bf16[32,768]{1,0:T(8,128)(2,1)} %get-tuple-element.25), channel_id=1, source_target_pairs={{0,8},{4,12},{8,0},{12,4},{1,9},{5,13},{9,1},{13,5},{2,10},{6,14},... | collective-permute-start | bytes 147464 | tf_op jit(solution)/shard_map/ppermute | solution.py:320
  10.0 2.8 %copy-start.3 = (bf16[64,768]{1,0:T(8,128)(2,1)S(1)}, bf16[64,768]{1,0:T(8,128)(2,1)}, u32[]{:S(2)}) copy-start(bf16[64,768]{1,0:T(8,128)(2,1)} %get-tuple-element.22.refs_0_) | copy-start | bytes 294916
  10.0 8.0 %collective-permute-start.5 = (bf16[192,768]{1,0:T(8,128)(2,1)}, bf16[192,768]{1,0:T(8,128)(2,1)S(1)}, u32[]{:S(2)}, u32[]{:S(2)}) collective-permute-start(bf16[192,768]{1,0:T(8,128)(2,1)} %get-tuple-element.24.refs_4_), channel_id=1, source_target_pairs={{0,2},{1,3},{2,0},{3,1},{4,6},{5,7},{6,4},{7,5},{8,10},{9,11},{10,... | collective-permute-start | bytes 884744 | tf_op jit(solution)/shard_map/ppermute | solution.py:320
  12.8 1.0 %copy-start.1 = (bf16[192,768]{1,0:T(8,128)(2,1)S(1)}, bf16[192,768]{1,0:T(8,128)(2,1)}, u32[]{:S(2)}) copy-start(bf16[192,768]{1,0:T(8,128)(2,1)} %get-tuple-element.24.refs_4_) | copy-start | bytes 884740
  12.9 1.8 %collective-permute-start.3 = (bf16[256,768]{1,0:T(8,128)(2,1)S(1)}, bf16[256,768]{1,0:T(8,128)(2,1)S(1)}, u32[]{:S(2)}, u32[]{:S(2)}) collective-permute-start(bf16[256,768]{1,0:T(8,128)(2,1)S(1)} %shard_map.48.lot_ref.refs_2_), channel_id=1, source_target_pairs={{0,1},{1,0},{2,3},{3,2},{4,5},{5,4},{6,7},{7,6},{8,9},{9,8},{10,11... | collective-permute-start | bytes 1179656 | tf_op jit(solution)/shard_map/ppermute | solution.py:320
  13.8 6.4 %collective-permute-start.4 = (bf16[192,768]{1,0:T(8,128)(2,1)S(1)}, bf16[192,768]{1,0:T(8,128)(2,1)S(1)}, u32[]{:S(2)}, u32[]{:S(2)}) collective-permute-start(bf16[192,768]{1,0:T(8,128)(2,1)S(1)} %copy-done.1), channel_id=1, source_target_pairs={{0,1},{1,0},{2,3},{3,2},{4,5},{5,4},{6,7},{7,6},{8,9},{9,8},{10,11... | collective-permute-start | bytes 884744 | tf_op jit(solution)/shard_map/ppermute | solution.py:320
  15.2 6.4 %collective-permute-start.7 = (bf16[32,896]{1,0:T(8,128)(2,1)S(1)}, bf16[32,896]{1,0:T(8,128)(2,1)S(1)}, u32[]{:S(2)}, u32[]{:S(2)}) collective-permute-start(bf16[32,896]{1,0:T(8,128)(2,1)S(1)} %get-tuple-element.26), channel_id=1, source_target_pairs={{0,8},{4,12},{8,0},{12,4},{1,9},{5,13},{9,1},{13,5},{2,10},{6,14},... | collective-permute-start | bytes 172040 | tf_op jit(solution)/shard_map/ppermute | solution.py:320

commit v7 on v5

--- a/solution.py
+++ b/solution.py
@@ -104,13 +104,17 @@
         second_ref[rest:, cols] = v[kept:]
 
 
-def order_kernel(sizes, off_ref, q_ref, qs_ref, back_ref, spread_ref):
+def order_kernel(sizes, off_ref, q_ref, k_ref, v_ref, qs_ref, back_ref, spread_ref, near_ref):
     width = q_ref.shape[1]
     scale = HEAD_DIMENSION ** (-0.5)
     for pair in range(width // PAIR):
         cols = slice(pair * PAIR, (pair + 1) * PAIR)
         chosen = order_rows_of_pair(sizes, lambda head: off_ref[head], pair, sizes.all_pad)
-        qs_ref[:, cols] = (select(dot(chosen, q_ref[:, cols]), sizes.all_pad) * scale).astype(jnp.bfloat16)
+        both = dot(chosen, jnp.concatenate([r[:, cols] for r in (q_ref, k_ref, v_ref)], 1))
+        qs_ref[:, cols] = (select(both, sizes.all_pad) * scale).astype(jnp.bfloat16)
+        for n in (1, 2):
+            found = select(both, sizes.all_pad, slice(n * PAIR, (n + 1) * PAIR))[sizes.kept_pad :]
+            near_ref[(n - 1) * sizes.rest_pad : n * sizes.rest_pad, cols] = found.astype(jnp.bfloat16)
         for head in (2 * pair, 2 * pair + 1):
             back_ref[head * sizes.rows : (head + 1) * sizes.rows] = restore_rows(sizes, off_ref[head])
     spread_ref[:, :width] = spread(width, (0,))
@@ -341,17 +345,17 @@
     far_first = far(first)
     lot = [first] + far_first + [swap(first, "seq", 1)] + [swap_both(first, mask) for mask in far_masks]
     far_second = far(second)
-    q, back, spreads = call(
+    q, back, spreads, near = call(
         functools.partial(order_kernel, sizes),
-        [array(sizes.all_pad), array(heads * rows, sizes.all_pad), array(PAIR, 2 * width)],
-        (offsets, queries),
+        [array(sizes.all_pad), array(heads * rows, sizes.all_pad), array(PAIR, 2 * width), array(sizes.second)],
+        (offsets, queries, keys, values),
         COST[1],
     )
     visitors = [swap(q_kept, "seq", mask) for mask in masks]
     lot = call(
         functools.partial(collect_kernel, len(lot)), array(len(lot) * sizes.first), (*lot, q), COST[2]
     )
-    near_second = [second, swap(after(second, lot), "sub", 1)]
+    near_second = [near, swap(after(near, lot), "sub", 1)]
     lot = [lot, swap(lot, "sub", 1)]
     visitors = call(
         functools.partial(collect_kernel, len(masks)),

time: 22.9 us -> 23.1 us (level)
  local copies, waits for them, and re-layouts: 0.86 us -> 0.02 us
  waiting for transfers between devices: 1.11 us -> 1.49 us
  starting transfers between devices: 11.8 us -> 12.1 us
  Pallas kernels: 6.71 us -> 6.95 us
    unnamed x8 -> x10, local copies, waits for them, and re-layouts: 0.86 us -> 0.02 us
    ppermute x7, waiting for transfers between devices: 1.11 us -> 1.49 us  [swap(): lax.ppermute(x, axis, [(n, n ^ mask) for n in range(lax.axis_size(axis))])]
    ppermute x7, starting transfers between devices: 7.76 us -> 8.12 us  [swap(): lax.ppermute(x, axis, [(n, n ^ mask) for n in range(lax.axis_size(axis))])]
    pallas_call x7, Pallas kernels: 6.71 us -> 6.95 us  [call(): pl.pallas_call(kernel, out_shape=out_shape, in_specs=in_specs, out_specs=...]
  transfers between devices with their start and end apart: 8 -> 8, of which waited for: 3 -> 3; matrix products, arithmetic and copies ran while one was open for 0% -> 0% of each run, Pallas kernels for 14% -> 15%
where the time goes in v7:
time: 23.1 us; the launch traced here: 22.9 us
  starting transfers between devices  12.1 us (52%)
  Pallas kernels  6.95 us (30%)
  blocking collectives  2.22 us (10%)
  waiting for transfers between devices  1.49 us (6%)
    ppermute x7, starting transfers between devices, swap(): lax.ppermute(x, axis, [(n, n ^ mask) for n in range(lax.axis_size(axis))])  8.12 us
    pallas_call x7, Pallas kernels, call(): pl.pallas_call(kernel, out_shape=out_shape, in_specs=in_specs, out_specs=...  6.95 us
    ppermute x1, starting transfers between devices, swap_both(): lax.ppermute(x, ('seq', 'sub'), [(n, n ^ sub ^ mask) for n in range(size)])  4.02 us
    all_gather x1, blocking collectives, both_cores(): lax.all_gather(x, 'sub', axis=0, tiled=True, axis_index_groups=chips)  2.22 us
    ppermute x7, waiting for transfers between devices, swap(): lax.ppermute(x, axis, [(n, n ^ mask) for n in range(lax.axis_size(axis))])  1.49 us
  transfers between devices with their start and end apart: 8, of which 3 were waited for; matrix products, arithmetic and copies ran while one was open for 0% of the time, Pallas kernels for 15%

profile of v7, /device:TPU:0, one launch (start us, length us, event | category | flops | bytes accessed | tf_op | source)
XLA Modules:
  0.0 22.9 jit_solution(4075117744740180277)
XLA Ops:
  0.0 0.0 copy-start.2
  0.0 0.0 copy-start.1
  0.0 0.0 copy-start
  0.0 2.4 %shard_map.47 = (bf16[32,768]{1,0:T(8,128)(2,1)}, bf16[64,768]{1,0:T(8,128)(2,1)}, bf16[192,768]{1,0:T(8,128)(2,1)}) custom-call(s32[12]{0:T(128)} %refs_0_.1, bf16[128,768]{1,0:T(8,128)(2,1)} %refs_1_.1, bf16[128,768]{1,0:T(8,128)(2,1)} %refs_2_.1, bf16[128,768]{1,0:T(8,128)(2,1)} %refs_3_.1), custom_call_target="tpu_custom_call" | custom-call | flops 1000000 | bytes 589848 | tf_op jit(solution)/shard_map/pallas_call | solution.py:296
  2.4 4.0 %collective-permute-start.2 = (bf16[64,768]{1,0:T(8,128)(2,1)}, bf16[64,768]{1,0:T(8,128)(2,1)S(1)}, u32[]{:S(2)}, u32[]{:S(2)}) collective-permute-start(bf16[64,768]{1,0:T(8,128)(2,1)} %get-tuple-element.23.refs_0_), channel_id=1, source_target_pairs={{0,6},{1,7},{2,4},{3,5},{4,2},{5,3},{6,0},{7,1},{8,14},{9,15},{10,... | collective-permute-start | bytes 294920 | tf_op jit(solution)/shard_map/ppermute | solution.py:330
  6.4 0.5 %collective-permute-start.1 = (bf16[64,768]{1,0:T(8,128)(2,1)}, bf16[64,768]{1,0:T(8,128)(2,1)S(1)}, u32[]{:S(2)}, u32[]{:S(2)}) collective-permute-start(bf16[64,768]{1,0:T(8,128)(2,1)} %get-tuple-element.23.refs_0_), channel_id=1, source_target_pairs={{0,4},{4,0},{8,12},{12,8},{1,5},{5,1},{9,13},{13,9},{2,6},{6,2},{1... | collective-permute-start | bytes 294920 | tf_op jit(solution)/shard_map/ppermute | solution.py:316
  6.9 0.2 collective-permute-start
  7.1 0.0 copy-start.3
  7.1 2.9 %collective-permute-start.6 = (bf16[32,768]{1,0:T(8,128)(2,1)}, bf16[32,768]{1,0:T(8,128)(2,1)S(1)}, u32[]{:S(2)}, u32[]{:S(2)}) collective-permute-start(bf16[32,768]{1,0:T(8,128)(2,1)} %get-tuple-element.27), channel_id=1, source_target_pairs={{0,8},{4,12},{8,0},{12,4},{1,9},{5,13},{9,1},{13,5},{2,10},{6,14},... | collective-permute-start | bytes 147464 | tf_op jit(solution)/shard_map/ppermute | solution.py:316
  10.0 0.0 copy-start.4
  10.0 1.5 %collective-permute-start.5 = (bf16[192,768]{1,0:T(8,128)(2,1)}, bf16[192,768]{1,0:T(8,128)(2,1)S(1)}, u32[]{:S(2)}, u32[]{:S(2)}) collective-permute-start(bf16[192,768]{1,0:T(8,128)(2,1)} %get-tuple-element.26), channel_id=1, source_target_pairs={{0,2},{1,3},{2,0},{3,1},{4,6},{5,7},{6,4},{7,5},{8,10},{9,11},{10,... | collective-permute-start | bytes 884744 | tf_op jit(solution)/shard_map/ppermute | solution.py:316
  11.5 0.0 copy-done.2
  11.5 0.0 copy-done.1
  11.5 0.0 copy-done
  11.5 0.0 copy-done.3
  11.5 1.4 %shard_map.46 = (bf16[128,768]{1,0:T(8,128)(2,1)S(1)}, bf16[1536,128]{1,0:T(8,128)(2,1)S(1)}, bf16[128,1536]{1,0:T(8,128)(2,1)S(1)}, bf16[192,768]{1,0:T(8,128)(2,1)S(1)}) custom-call(s32[12]{0:T(128)S(1)} %copy-done.3, bf16[128,768]{1,0:T(8,128)(2,1)S(1)} %copy-done, bf16[128,768]{1,0:T(8,128)(2,1)S(1)} %copy-done.1, bf16[128,768]{1,0:T(8,128)(2,1)S(1)} %copy-done.2), custom_call_target="tpu_custom_call" | custom-call | flops 1000000 | bytes 589848 | tf_op jit(solution)/shard_map/pallas_call | solution.py:296
  13.0 0.0 collective-permute-done.2.refs_3_
  13.0 0.0 collective-permute-done.1.refs_2_
  13.0 0.0 collective-permute-done.refs_1_
  13.0 0.0 copy-done.4
  13.0 0.1 collective-permute-start.3
  13.1 0.5 %collective-permute-start.4 = (bf16[192,768]{1,0:T(8,128)(2,1)S(1)}, bf16[192,768]{1,0:T(8,128)(2,1)S(1)}, u32[]{:S(2)}, u32[]{:S(2)}) collective-permute-start(bf16[192,768]{1,0:T(8,128)(2,1)S(1)} %get-tuple-element.25.refs_4_), channel_id=1, source_target_pairs={{0,1},{1,0},{2,3},{3,2},{4,5},{5,4},{6,7},{7,6},{8,9},{9,8},{10,11... | collective-permute-start | bytes 884744 | tf_op jit(solution)/shard_map/ppermute | solution.py:316
  13.6 0.0 collective-permute-done.6.refs_0_
  13.6 1.2 %collective-permute-done.3.other_lot_ref.refs_3_ = bf16[256,768]{1,0:T(8,128)(2,1)S(1)} collective-permute-done((bf16[256,768]{1,0:T(8,128)(2,1)S(1)}, bf16[256,768]{1,0:T(8,128)(2,1)S(1)}, u32[]{:S(2)}, u32[]{:S(2)}) %collective-permute-start.3) | collective-permute-done | bytes 393248 | tf_op jit(solution)/shard_map/ppermute | solution.py:316
  14.8 0.6 %shard_map.50 = (bf16[32,896]{1,0:T(8,128)(2,1)S(1)}, bf16[32,896]{1,0:T(8,128)(2,1)S(1)}) custom-call(bf16[128,768]{1,0:T(8,128)(2,1)S(1)} %get-tuple-element.22.refs_4_.q_ref.refs_1_, bf16[32,768]{1,0:T(8,128)(2,1)S(1)} %shard_map.49.visitor_ref, bf16[256,768]{1,0:T(8,128)(2,1)S(1)} %shard_map.48.lot_ref.refs_2_, ...), custom_call_target="tpu_custom_call" | custom-call | flops 1000000 | bytes 1032192 | tf_op jit(solution)/shard_map/pallas_call | solution.py:296
  15.4 2.5 %collective-permute-start.7 = (bf16[32,896]{1,0:T(8,128)(2,1)S(1)}, bf16[32,896]{1,0:T(8,128)(2,1)S(1)}, u32[]{:S(2)}, u32[]{:S(2)}) collective-permute-start(bf16[32,896]{1,0:T(8,128)(2,1)S(1)} %get-tuple-element.28), channel_id=1, source_target_pairs={{0,8},{4,12},{8,0},{12,4},{1,9},{5,13},{9,1},{13,5},{2,10},{6,14},... | collective-permute-start | bytes 172040 | tf_op jit(solution)/shard_map/ppermute | solution.py:316
  17.9 0.2 collective-permute-done.5
  18.0 2.2 %all_gather.3.refs_6_ = bf16[384,768]{1,0:T(8,128)(2,1)S(1)} all-gather(bf16[192,768]{1,0:T(8,128)(2,1)S(1)} %collective-permute-done.5), channel_id=1, replica_groups={{0,1},{2,3},{4,5},{6,7},{8,9},{10,11},{12,13},{14,15},{16,17},{18,19},{..., dimensions={0}, use_global_device_ids=true | all-gather | bytes 884736 | tf_op jit(solution)/shard_map/all_gather | solution.py:326
  20.3 0.0 collective-permute-done.4.refs_5_
  20.3 1.4 %shard_map.51 = (bf16[128,768]{1,0:T(8,128)(2,1)S(1)}, f32[32,768]{1,0:T(8,128)S(1)}, f32[32,768]{1,0:T(8,128)S(1)}, f32[32,768]{1,0:T(8,128)S(1)}) custom-call(bf16[1536,128]{1,0:T(8,128)(2,1)S(1)} %get-tuple-element.20.refs_0_, bf16[128,768]{1,0:T(8,128)(2,1)S(1)} %get-tuple-element.22.refs_4_.q_ref.refs_1_, ...), custom_call_target="tpu_custom_call" | custom-call | flops 1000000 | bytes 2555904 | tf_op jit(solution)/shard_map/pallas_call | solution.py:296
  21.6 0.1 collective-permute-done.7.refs_6_
  21.8 1.1 %shard_map.52 = bf16[128,768]{1,0:T(8,128)(2,1)} custom-call(bf16[1536,128]{1,0:T(8,128)(2,1)S(1)} %get-tuple-element.20.refs_0_, bf16[128,1536]{1,0:T(8,128)(2,1)S(1)} %get-tuple-element.21.refs_1_, bf16[128,768]{1,0:T(8,128)(2,1)S(1)} %get-tuple-element.30.refs_2_, f32[32,768]{1,0:T(8,128)S(1)} %get-tuple-element.31.refs_3_, ...), custom_call_target="tpu_custom_call" | custom-call | flops 1000000 | bytes 1245184 | tf_op jit(solution)/shard_map/pallas_call | solution.py:296
  (2 shorter events, 0.0 us)
Async XLA Ops:
  0.0 11.5 %copy-start.2 = (bf16[128,768]{1,0:T(8,128)(2,1)S(1)}, bf16[128,768]{1,0:T(8,128)(2,1)}, u32[]{:S(2)}) copy-start(bf16[128,768]{1,0:T(8,128)(2,1)} %refs_3_.1) | copy-start | bytes 589828
  0.0 11.5 %copy-start.1 = (bf16[128,768]{1,0:T(8,128)(2,1)S(1)}, bf16[128,768]{1,0:T(8,128)(2,1)}, u32[]{:S(2)}) copy-start(bf16[128,768]{1,0:T(8,128)(2,1)} %refs_2_.1) | copy-start | bytes 589828
  0.0 11.5 %copy-start = (bf16[128,768]{1,0:T(8,128)(2,1)S(1)}, bf16[128,768]{1,0:T(8,128)(2,1)}, u32[]{:S(2)}) copy-start(bf16[128,768]{1,0:T(8,128)(2,1)} %refs_1_.1) | copy-start | bytes 589828
  2.4 10.5 %collective-permute-start.2 = (bf16[64,768]{1,0:T(8,128)(2,1)}, bf16[64,768]{1,0:T(8,128)(2,1)S(1)}, u32[]{:S(2)}, u32[]{:S(2)}) collective-permute-start(bf16[64,768]{1,0:T(8,128)(2,1)} %get-tuple-element.23.refs_0_), channel_id=1, source_target_pairs={{0,6},{1,7},{2,4},{3,5},{4,2},{5,3},{6,0},{7,1},{8,14},{9,15},{10,... | collective-permute-start | bytes 294920 | tf_op jit(solution)/shard_map/ppermute | solution.py:330
  6.4 6.5 %collective-permute-start.1 = (bf16[64,768]{1,0:T(8,128)(2,1)}, bf16[64,768]{1,0:T(8,128)(2,1)S(1)}, u32[]{:S(2)}, u32[]{:S(2)}) collective-permute-start(bf16[64,768]{1,0:T(8,128)(2,1)} %get-tuple-element.23.refs_0_), channel_id=1, source_target_pairs={{0,4},{4,0},{8,12},{12,8},{1,5},{5,1},{9,13},{13,9},{2,6},{6,2},{1... | collective-permute-start | bytes 294920 | tf_op jit(solution)/shard_map/ppermute | solution.py:316
  6.9 6.1 %collective-permute-start = (bf16[64,768]{1,0:T(8,128)(2,1)}, bf16[64,768]{1,0:T(8,128)(2,1)S(1)}, u32[]{:S(2)}, u32[]{:S(2)}) collective-permute-start(bf16[64,768]{1,0:T(8,128)(2,1)} %get-tuple-element.23.refs_0_), channel_id=1, source_target_pairs={{0,2},{1,3},{2,0},{3,1},{4,6},{5,7},{6,4},{7,5},{8,10},{9,11},{10,... | collective-permute-start | bytes 294920 | tf_op jit(solution)/shard_map/ppermute | solution.py:316
  7.1 4.4 %copy-start.3 = (s32[12]{0:T(128)S(1)}, s32[12]{0:T(128)}, u32[]{:S(2)}) copy-start(s32[12]{0:T(128)} %refs_0_.1) | copy-start | bytes 148
  7.1 6.5 %collective-permute-start.6 = (bf16[32,768]{1,0:T(8,128)(2,1)}, bf16[32,768]{1,0:T(8,128)(2,1)S(1)}, u32[]{:S(2)}, u32[]{:S(2)}) collective-permute-start(bf16[32,768]{1,0:T(8,128)(2,1)} %get-tuple-element.27), channel_id=1, source_target_pairs={{0,8},{4,12},{8,0},{12,4},{1,9},{5,13},{9,1},{13,5},{2,10},{6,14},... | collective-permute-start | bytes 147464 | tf_op jit(solution)/shard_map/ppermute | solution.py:316
  10.0 3.0 %copy-start.4 = (bf16[64,768]{1,0:T(8,128)(2,1)S(1)}, bf16[64,768]{1,0:T(8,128)(2,1)}, u32[]{:S(2)}) copy-start(bf16[64,768]{1,0:T(8,128)(2,1)} %get-tuple-element.23.refs_0_) | copy-start | bytes 294916
  10.0 8.0 %collective-permute-start.5 = (bf16[192,768]{1,0:T(8,128)(2,1)}, bf16[192,768]{1,0:T(8,128)(2,1)S(1)}, u32[]{:S(2)}, u32[]{:S(2)}) collective-permute-start(bf16[192,768]{1,0:T(8,128)(2,1)} %get-tuple-element.26), channel_id=1, source_target_pairs={{0,2},{1,3},{2,0},{3,1},{4,6},{5,7},{6,4},{7,5},{8,10},{9,11},{10,... | collective-permute-start | bytes 884744 | tf_op jit(solution)/shard_map/ppermute | solution.py:316
  13.0 1.8 %collective-permute-start.3 = (bf16[256,768]{1,0:T(8,128)(2,1)S(1)}, bf16[256,768]{1,0:T(8,128)(2,1)S(1)}, u32[]{:S(2)}, u32[]{:S(2)}) collective-permute-start(bf16[256,768]{1,0:T(8,128)(2,1)S(1)} %shard_map.48.lot_ref.refs_2_), channel_id=1, source_target_pairs={{0,1},{1,0},{2,3},{3,2},{4,5},{5,4},{6,7},{7,6},{8,9},{9,8},{10,11... | collective-permute-start | bytes 1179656 | tf_op jit(solution)/shard_map/ppermute | solution.py:316
  13.1 7.1 %collective-permute-start.4 = (bf16[192,768]{1,0:T(8,128)(2,1)S(1)}, bf16[192,768]{1,0:T(8,128)(2,1)S(1)}, u32[]{:S(2)}, u32[]{:S(2)}) collective-permute-start(bf16[192,768]{1,0:T(8,128)(2,1)S(1)} %get-tuple-element.25.refs_4_), channel_id=1, source_target_pairs={{0,1},{1,0},{2,3},{3,2},{4,5},{5,4},{6,7},{7,6},{8,9},{9,8},{10,11... | collective-permute-start | bytes 884744 | tf_op jit(solution)/shard_map/ppermute | solution.py:316
  15.4 6.4 %collective-permute-start.7 = (bf16[32,896]{1,0:T(8,128)(2,1)S(1)}, bf16[32,896]{1,0:T(8,128)(2,1)S(1)}, u32[]{:S(2)}, u32[]{:S(2)}) collective-permute-start(bf16[32,896]{1,0:T(8,128)(2,1)S(1)} %get-tuple-element.28), channel_id=1, source_target_pairs={{0,8},{4,12},{8,0},{12,4},{1,9},{5,13},{9,1},{13,5},{2,10},{6,14},... | collective-permute-start | bytes 172040 | tf_op jit(solution)/shard_map/ppermute | solution.py:316
